TPU v7x, 128 devices: a whole 4x4x4 slice. The times are simulated.
128 devices in a mesh: blk: 8 (over y, x_lo), rep: 16 (over z, x_hi, core).
Axes of the slice: x: 4 (x_hi: 2, x_lo: 2; x = x_hi * 2 + x_lo), y: 4, z: 4, core: 2. Of those that a mesh axis runs over, the one named last changes fastest.
Arguments:
- image_feats: bfloat16 [16, 4096, 1024], P('rep', 'blk'), may hold values from -6 to 6
- text_feats: bfloat16 [16, 4096, 768], P('rep', 'blk'), may hold values from -6 to 6
- image_head: bfloat16 [1024, 768], replicated, may hold values from -0.1875 to 0.1875
- text_head: bfloat16 [768, 768], replicated, may hold values from -0.21875 to 0.21875
- image_lse: float32 [16, 4096], P('rep', 'blk'), as said below
- text_lse: float32 [16, 4096], P('rep', 'blk'), as said below
Outputs:
- image_feat_grad: float32 [16, 4096, 1024], P('rep', 'blk')
- text_feat_grad: float32 [16, 4096, 768], P('rep', 'blk')
- image_head_grad: float32 [1024, 768], replicated
- text_head_grad: float32 [768, 768], replicated
Inputs may be any that keep to these rules, and one draw needn't show every extreme that they name: `image_lse`: each entry lies between ln(4096) + 1 and ln(4096) + 2.5. `text_lse`: each entry lies between ln(4096) + 1 and ln(4096) + 2.5.
All inputs are finite; a program needn't handle non-finite values.
Results may differ from a plain program's by a relative error of at most 0.028.
Values may be sent and summed in bfloat16 or wider, within the bound.
No kernel may reach another device: no remote copies, remote signals or barrier semaphores. Data moves between devices by JAX's collectives and lax.ppermute only.
A program may use at most 128 MiB of HBM per device.

v0:
```python
import jax
import jax.numpy as jnp
from jax import lax
from jax.sharding import Mesh
from jax.sharding import PartitionSpec as P

BLK = ("blk_0", "blk_1")
BLK_REP = ("blk_0", "blk_1", "rep")


logit_scale = 50.0
epsilon = 1e-06


def whole_of(value, axes, dim):
    for axis in reversed(axes):
        value = lax.all_gather(value, axis, axis=dim, tiled=True)
    return value


def project_head(feats, weight):
    raw = jnp.dot(feats, weight, preferred_element_type=jnp.float32)
    factor = lax.rsqrt(jnp.sum(raw * raw, axis=1, keepdims=True) + epsilon)
    return (raw * factor, factor)


def pre_gradient(embed, factor, grad):
    inner = jnp.sum(embed * grad, axis=1, keepdims=True)
    return (factor * (grad - embed * inner)).astype(jnp.bfloat16)


def weight_tile(left, left_lse, right, right_lse):
    scores = logit_scale * lax.dot_general(
        left, right, (((1,), (1,)), ((), ())), preferred_element_type=jnp.float32
    )
    return (
        0.5 * (jnp.exp(scores - left_lse[:, None]) + jnp.exp(scores - right_lse[None, :]))
    ).astype(jnp.bfloat16)


def shards(image_feats, text_feats, image_head, text_head, image_lse, text_lse):
    image_rows = image_feats[0]
    text_rows = text_feats[0]
    lse_img = image_lse[0]
    lse_txt = text_lse[0]
    image_embed, image_scale = project_head(image_rows, image_head)
    text_embed, text_scale = project_head(text_rows, text_head)
    image_round = image_embed.astype(jnp.bfloat16)
    text_round = text_embed.astype(jnp.bfloat16)
    image_piece = whole_of(image_round, BLK, 0)
    image_piece_lse = whole_of(lse_img.astype(jnp.bfloat16), BLK, 0).astype(jnp.float32)
    text_piece = whole_of(text_round, BLK, 0)
    text_piece_lse = whole_of(lse_txt.astype(jnp.bfloat16), BLK, 0).astype(jnp.float32)
    image_weights = weight_tile(image_round, lse_img, text_piece, text_piece_lse)
    image_total_part = jnp.dot(image_weights, text_piece, preferred_element_type=jnp.float32)
    text_weights = weight_tile(image_piece, image_piece_lse, text_round, lse_txt)
    text_total_part = lax.dot_general(
        text_weights, image_piece, (((0,), (0,)), ((), ())), preferred_element_type=jnp.float32
    )
    image_grad = logit_scale * image_total_part - logit_scale * text_round.astype(jnp.float32)
    text_grad = logit_scale * text_total_part - logit_scale * image_round.astype(jnp.float32)
    image_pre = pre_gradient(image_embed, image_scale, image_grad)
    text_pre = pre_gradient(text_embed, text_scale, text_grad)
    image_back = lax.dot_general(
        image_pre, image_head, (((1,), (1,)), ((), ())), preferred_element_type=jnp.float32
    )
    text_back = lax.dot_general(
        text_pre, text_head, (((1,), (1,)), ((), ())), preferred_element_type=jnp.float32
    )
    image_wgrad = lax.dot_general(
        image_rows, image_pre, (((0,), (0,)), ((), ())), preferred_element_type=jnp.float32
    )
    text_wgrad = lax.dot_general(
        text_rows, text_pre, (((0,), (0,)), ((), ())), preferred_element_type=jnp.float32
    )
    image_total, text_total = lax.psum((image_wgrad, text_wgrad), BLK_REP)
    return (image_back[None], text_back[None], image_total, text_total)


def solution(mesh):
    finer = Mesh(mesh.devices.reshape(4, 2, mesh.shape["rep"]), ("blk_0", "blk_1", "rep"))
    return jax.shard_map(
        shards,
        mesh=finer,
        in_specs=(P("rep", BLK, None), P("rep", BLK, None), P(), P(), P("rep", BLK), P("rep", BLK)),
        out_specs=(P("rep", BLK, None), P("rep", BLK, None), P(), P()),
        check_vma=False,
    )
```

profile of v0, /device:TPU:1, one launch (start us, length us, event | category | flops | bytes accessed | tf_op | source)
XLA Modules:
  0.0 403.6 jit_solution(7091597317224575274)
XLA Ops:
  7.2 1.4 copy-done
  8.6 2.3 multiply_reduce_fusion.3
  12.0 2.4 multiply_reduce_fusion.2
  14.4 1.1 copy-done.1
  16.7 28.4 %all-gather.11.cloned.1.call-done = bf16[1024,768]{1,0:T(8,128)(2,1)} async-done(((bf16[512,768]{1,0:T(8,128)(2,1)}), bf16[1024,768]{1,0:T(8,128)(2,1)}) %all-gather.11.cloned.1.call-update) | async-done | bytes 1572880 | tf_op jit(solution)/shard_map/all_gather | solution.py:17
  45.1 32.9 %all-gather.7.cloned.1.call-done = bf16[1024,768]{1,0:T(8,128)(2,1)} async-done(((bf16[512,768]{1,0:T(8,128)(2,1)}), bf16[1024,768]{1,0:T(8,128)(2,1)}) %all-gather.7.cloned.1.call-update) | async-done | bytes 1572880 | tf_op jit(solution)/shard_map/all_gather | solution.py:17
  78.1 3.2 all-gather.1
  81.4 8.4 %all_gather.31 = bf16[4096]{0:T(1024)(128)(2,1)S(1)} all-gather(bf16[1024]{0:T(1024)(128)(2,1)S(1)} %bitcast.42), channel_id=1, replica_groups=mesh['blk_0'=4,'blk_1'=2,'rep'=16] {'blk_0'}, dimensions={0}, use_global_device_ids=true | all-gather | bytes 10240 | tf_op jit(solution)/shard_map/all_gather | solution.py:17
  89.8 3.2 all-gather
  93.0 9.3 %all_gather.27 = bf16[4096]{0:T(1024)(128)(2,1)S(1)} all-gather(bf16[1024]{0:T(1024)(128)(2,1)S(1)} %bitcast.43), channel_id=1, replica_groups=mesh['blk_0'=4,'blk_1'=2,'rep'=16] {'blk_0'}, dimensions={0}, use_global_device_ids=true | all-gather | bytes 10240 | tf_op jit(solution)/shard_map/all_gather | solution.py:17
  102.3 44.2 %all-gather.13.cloned.1.call-done = bf16[4096,768]{1,0:T(8,128)(2,1)} async-done(((bf16[1024,768]{1,0:T(8,128)(2,1)}), bf16[4096,768]{1,0:T(8,128)(2,1)}) %all-gather.13.cloned.1.call-update) | async-done | bytes 6291472 | tf_op jit(solution)/shard_map/all_gather | solution.py:17
  146.5 15.9 %multiply_reduce_fusion = (f32[512]{0:T(512)S(1)}, f32[512,768]{1,0:T(8,128)}) fusion(f32[512,768]{1,0:T(8,128)} %copy-done.1, f32[512]{0:T(512)S(1)} %add_rsqrt_fusion, bf16[512,768]{1,0:T(8,128)(2,1)} %multiply_convert_fusion.5, bf16[4096,768]{1,0:T(8,128)(2,1)} %all-gather.13.cloned.1.call-done, bf16[512,768]{1,0:T(8,128)(2,1)} %multiply_convert_fusion.4, ...), kind=kOutput, calls=%fused_computation.6 | convolution fusion | flops 6457785856 | bytes 11032576 | tf_op jit(solution)/shard_map/dot_general | solution.py:57
  162.4 2.3 multiply_convert_fusion.2
  165.6 2.2 convolution_bitcast_fusion.1
  167.9 46.4 %all-gather.9.cloned.1.call-done = bf16[4096,768]{1,0:T(8,128)(2,1)} async-done(((bf16[1024,768]{1,0:T(8,128)(2,1)}), bf16[4096,768]{1,0:T(8,128)(2,1)}) %all-gather.9.cloned.1.call-update) | async-done | bytes 6291472 | tf_op jit(solution)/shard_map/all_gather | solution.py:17
  214.3 13.5 %multiply_reduce_fusion.1 = (f32[512]{0:T(512)S(1)}, f32[512,768]{1,0:T(8,128)}) fusion(f32[512,768]{1,0:T(8,128)S(1)} %get-tuple-element.21, f32[512]{0:T(512)S(1)} %add_rsqrt_fusion.1, bf16[512,768]{1,0:T(8,128)(2,1)} %multiply_convert_fusion.4, bf16[4096,768]{1,0:T(8,128)(2,1)} %all-gather.9.cloned.1.call-done, ...), kind=kOutput, calls=%fused_computation.9 | convolution fusion | flops 6457785856 | bytes 11032576 | tf_op jit(solution)/shard_map/dot_general | solution.py:55
  227.8 1.8 multiply_convert_fusion.3
  230.5 2.7 convolution_bitcast_fusion
  233.2 1.1 copy-done.3
  234.3 3.3 convolution_bitcast_fusion.3
  237.6 2.3 convolution_bitcast_fusion.2
  239.9 150.6 %all-reduce.3.cloned.1.call-done = (f32[1024,768]{0,1:T(8,128)}, f32[768,768]{0,1:T(8,128)}) async-done(((f32[1024,768]{0,1:T(8,128)}, f32[768,768]{0,1:T(8,128)}), (f32[1024,768]{0,1:T(8,128)}, f32[768,768]{0,1:T(8,128)})) %all-reduce.3.cloned.1.call-update) | async-done | bytes 5505040 | tf_op jit(solution)/shard_map/psum | solution.py:76
  390.5 3.5 copy.14
  394.0 3.0 copy.15
  (41 shorter events, 4.3 us)
Async XLA Ops:
  7.2 1.4 copy-start
  7.2 37.9 %all-gather.11.cloned.1.call-start = ((), (), s32[]{:S(2)}) async-start(), calls=%async_computation.2 | async-start | bytes 2359296 | tf_op jit(solution)/shard_map/all_gather | solution.py:17
  12.0 66.0 %all-gather.7.cloned.1.call-start = ((), (), s32[]{:S(2)}) async-start(), calls=%async_computation | async-start | bytes 2359296 | tf_op jit(solution)/shard_map/all_gather | solution.py:17
  14.4 1.1 copy-start.1
  16.6 129.9 %all-gather.13.cloned.1.call-start = ((), (), s32[]{:S(2)}) async-start(), calls=%async_computation.3 | async-start | bytes 7864320 | tf_op jit(solution)/shard_map/all_gather | solution.py:17
  45.1 33.0 %copy-start.9 = (f32[1,512]{1,0:T(1,128)S(1)}, f32[1,512]{1,0:T(1,128)}, u32[]{:S(2)}) copy-start(f32[1,512]{1,0:T(1,128)} %param.10) | copy-start | bytes 6148
  45.1 44.7 %copy-start.8 = (f32[1,512]{1,0:T(1,128)S(1)}, f32[1,512]{1,0:T(1,128)}, u32[]{:S(2)}) copy-start(f32[1,512]{1,0:T(1,128)} %param.11) | copy-start | bytes 6148
  45.1 169.2 %all-gather.9.cloned.1.call-start = ((), (), s32[]{:S(2)}) async-start(), calls=%async_computation.1 | async-start | bytes 7864320 | tf_op jit(solution)/shard_map/all_gather | solution.py:17
  78.0 312.4 %all-reduce.3.cloned.1.call-start = ((), (), s32[]{:S(2)}) async-start(), calls=%async_computation.4 | async-start | bytes 11010048 | tf_op jit(solution)/shard_map/psum | solution.py:76
  162.4 3.2 copy-start.7
  164.7 0.9 copy-start.2
  227.8 2.7 copy-start.6
  229.6 0.9 copy-start.4
  233.1 1.1 copy-start.3
  234.3 3.3 copy-start.5
Sparse Core Ops, SparseCore 0:
  12.1 32.9 all-gather.10
  47.3 30.6 all-gather.6
  79.7 66.7 all-gather.12
  148.0 66.2 all-gather.8
  233.3 157.1 all-reduce.2
where the time goes:
time: 404 us
  waiting for transfers between devices  303 us (75%)
  matrix products  44.6 us (11%)
  blocking collectives  24.1 us (6%)
  between operations  13.9 us (3%)
  local copies, waits for them, and re-layouts  12 us (3%)
  other arithmetic  6.31 us (2%)
    all_gather x4, waiting for transfers between devices, whole_of(): value = lax.all_gather(value, axis, axis=dim, tiled=True)  152 us
    psum x1, waiting for transfers between devices, shards(): image_total, text_total = lax.psum((image_wgrad, text_wgrad), BLK_REP)  151 us
    all_gather x4, blocking collectives, whole_of(): value = lax.all_gather(value, axis, axis=dim, tiled=True)  24.1 us
    dot_general x1, matrix products, shards(): lax.dot_general(text_weights, image_piece, (((0,), (0,)), ((), ())), pref...  15.9 us
    dot_general x1, matrix products, shards(): jnp.dot(image_weights, text_piece, preferred_element_type=jnp.float32)  13.5 us
    unnamed x26, local copies, waits for them, and re-layouts  12 us
  transfers between devices with their start and end apart: 5, of which 5 were waited for; matrix products, arithmetic and copies ran while one was open for 7% of the time, Pallas kernels for 0%

commit v1 on v0

v1 whole, which is shorter than its diff:
```python
import functools
import math

import jax
import jax.numpy as jnp
from jax import lax
from jax.experimental import pallas as pl
from jax.experimental.pallas import tpu as pltpu
from jax.sharding import Mesh
from jax.sharding import PartitionSpec as P

BLK = ("y", "xl")
REP = ("z", "xh", "core")
PLANE = ("xl", "z", "xh")

bf16 = jnp.bfloat16
f32 = jnp.float32

logit_scale = 50.0
epsilon = 1e-06
exp2_scale = logit_scale * math.log2(math.e)

ROWS = 512
PAD = 16
EMB = 768
VIS = 1024
TXT = 768
HV = VIS // 2
HT = TXT // 2
HALF = HV + HT


def permute(value, axis, size, shift):
    return lax.ppermute(value, axis, [(i, (i + shift) % size) for i in range(size)])


def nt(a, b):
    return lax.dot_general(a, b, (((1,), (1,)), ((), ())), preferred_element_type=f32)


def tn(a, b):
    return lax.dot_general(a, b, (((0,), (0,)), ((), ())), preferred_element_type=f32)


def nn(a, b):
    return jnp.dot(a, b, preferred_element_type=f32)


def scale_of(raw):
    return lax.rsqrt(jnp.sum(raw * raw, axis=1, keepdims=True) + epsilon)


def pre_gradient(raw, grad):
    factor = scale_of(raw)
    embed = raw * factor
    inner = jnp.sum(embed * grad, axis=1, keepdims=True)
    return (factor * (grad - embed * inner)).astype(bf16)


CH = 256


def tile_kernel(core, i0, i1, t0, t1, t2, t3, hi, ht,
                p1, p2, p3, tbase, ipart, ibase, send, keep,
                zi, ri, ea, zt, rt, eb, w, pre, prei):
    imgs = (i0, i1)
    txts = (t0, t1, t2, t3)
    for b, ref in enumerate(imgs):
        @pl.loop(0, ROWS // CH)
        def _(k, b=b, ref=ref):
            src = pl.ds(pl.multiple_of(k * CH, CH), CH)
            dst = pl.ds(pl.multiple_of(b * ROWS + k * CH, CH), CH)
            raw = nn(ref[src, :], hi[...])
            zi[dst, :] = raw
            ri[dst, :] = (raw * scale_of(raw)).astype(bf16)

        tail = ref[ROWS : ROWS + PAD, :].astype(f32)
        lse = tail[0:1, 0:ROWS] + tail[0:1, ROWS : 2 * ROWS]
        row = 0.5 * jnp.exp(-lse)
        ea[b * ROWS : (b + 1) * ROWS, :] = jnp.broadcast_to(row, (128, ROWS)).T

    for b, ref in enumerate(txts):
        @pl.loop(0, ROWS // CH)
        def _(k, b=b, ref=ref):
            src = pl.ds(pl.multiple_of(k * CH, CH), CH)
            dst = pl.ds(pl.multiple_of(b * ROWS + k * CH, CH), CH)
            raw = nn(ref[src, :], ht[...])
            zt[src, :] = raw
            rt[dst, :] = (raw * scale_of(raw)).astype(bf16)

        tail = ref[ROWS : ROWS + PAD, :].astype(f32)
        lse = tail[0:1, 0:ROWS] + tail[1:2, 0:ROWS]
        eb[...] = jnp.broadcast_to(0.5 * jnp.exp(-lse), (8, ROWS))

        @pl.loop(0, 2 * ROWS // CH)
        def _(k, b=b):
            rows = pl.ds(pl.multiple_of(k * CH, CH), CH)
            s = nt(ri[rows, :], rt[b * ROWS : (b + 1) * ROWS, :])
            col = ea[rows, :]
            both = jnp.concatenate([col] * (ROWS // 128), axis=1) + eb[0:1, :]
            w[rows, b * ROWS : (b + 1) * ROWS] = (jnp.exp2(s * exp2_scale) * both).astype(bf16)

        @pl.loop(0, ROWS // CH)
        def _(k, b=b):
            src = pl.ds(pl.multiple_of(k * CH, CH), CH)
            dst = pl.ds(pl.multiple_of(b * ROWS + k * CH, CH), CH)
            g = tn(w[:, pl.ds(pl.multiple_of(b * ROWS + k * CH, CH), CH)], ri[...])
            if b == 0:
                g = g - ri[src, :].astype(f32)
                tbase[src, :] = g
            else:
                (p1, p2, p3)[b - 1][src, :] = g.astype(bf16)
            pre[dst, :] = pre_gradient(zt[src, :], logit_scale * g)

    for b in range(2):
        @pl.loop(0, ROWS // CH)
        def _(k, b=b):
            src = pl.ds(pl.multiple_of(k * CH, CH), CH)
            dst = pl.ds(pl.multiple_of(b * ROWS + k * CH, CH), CH)
            g = nn(w[dst, :], rt[...])
            if b == 0:
                g = g - rt[src, :].astype(f32)
                ibase[src, :] = g
            else:
                ipart[src, :] = g.astype(bf16)
            prei[dst, :] = pre_gradient(zi[dst, :], logit_scale * g)

    mine = core[0]

    def head_half(which, store):
        ci = pl.ds(pl.multiple_of(which * HV, 128), HV)
        ct = pl.ds(pl.multiple_of(which * HT, 128), HT)
        total = None
        for b, ref in enumerate(imgs):
            part = tn(ref[0:ROWS, ci], prei[b * ROWS : (b + 1) * ROWS, :])
            total = part if total is None else total + part
        store(0, HV, total)
        total = None
        for b, ref in enumerate(txts):
            part = tn(ref[0:ROWS, ct], pre[b * ROWS : (b + 1) * ROWS, :])
            total = part if total is None else total + part
        store(HV, HT, total)

    def store_send(at, n, value):
        send[at : at + n, :] = value.astype(bf16)

    def store_keep(at, n, value):
        keep[at : at + n, :] = value

    head_half(1 - mine, store_send)
    head_half(mine, store_keep)


VMEM = pl.BlockSpec(memory_space=pltpu.VMEM)
SMEM = pl.BlockSpec(memory_space=pltpu.SMEM)


def tile_call(core, i0, i1, texts, image_head, text_head):
    block = jax.ShapeDtypeStruct((ROWS, EMB), bf16)
    wide = jax.ShapeDtypeStruct((ROWS, EMB), f32)
    return pl.pallas_call(
        tile_kernel,
        out_shape=(block, block, block, wide, block, wide,
                   jax.ShapeDtypeStruct((HALF, EMB), bf16), jax.ShapeDtypeStruct((HALF, EMB), f32)),
        in_specs=[SMEM] + [VMEM] * 8,
        out_specs=(VMEM,) * 8,
        scratch_shapes=[
            pltpu.VMEM((2 * ROWS, EMB), f32),
            pltpu.VMEM((2 * ROWS, EMB), bf16),
            pltpu.VMEM((2 * ROWS, 128), f32),
            pltpu.VMEM((ROWS, EMB), f32),
            pltpu.VMEM((4 * ROWS, EMB), bf16),
            pltpu.VMEM((8, ROWS), f32),
            pltpu.VMEM((2 * ROWS, 4 * ROWS), bf16),
            pltpu.VMEM((4 * ROWS, EMB), bf16),
            pltpu.VMEM((2 * ROWS, EMB), bf16),
        ],
        compiler_params=pltpu.CompilerParams(vmem_limit_bytes=56 * 1024 * 1024),
        cost_estimate=pl.CostEstimate(flops=20 * 10**9, bytes_accessed=20 * 10**6, transcendentals=2 * 10**6),
        name="tile",
    )(core, i0, i1, *texts, image_head, text_head)


def back_kernel(n, feats, head, base, *rest):
    parts, out = rest[:n], rest[n]

    @pl.loop(0, ROWS // CH)
    def _(k):
        rows = pl.ds(pl.multiple_of(k * CH, CH), CH)
        raw = nn(feats[rows, :], head[...])
        g = base[rows, :]
        for p in parts:
            g = g + p[rows, :].astype(f32)
        out[rows, :] = nt(pre_gradient(raw, logit_scale * g), head[...])


def back_call(feats, head, base, parts):
    width = head.shape[0]
    return pl.pallas_call(
        functools.partial(back_kernel, len(parts)),
        out_shape=jax.ShapeDtypeStruct((ROWS, width), f32),
        in_specs=[VMEM] * (3 + len(parts)),
        out_specs=VMEM,
        compiler_params=pltpu.CompilerParams(vmem_limit_bytes=40 * 1024 * 1024),
        cost_estimate=pl.CostEstimate(flops=4 * ROWS * EMB * width, bytes_accessed=10 * 10**6, transcendentals=0),
        name="back",
    )(feats, head, base, *parts)


def final_kernel(core, own, other, image, text):
    mine = core[0]
    for ref, which in ((own, mine), (other, 1 - mine)):
        image[pl.ds(pl.multiple_of(which * HV, 128), HV), :] = ref[0:HV, :].astype(f32)
        text[pl.ds(pl.multiple_of(which * HT, 128), HT), :] = ref[HV:HALF, :].astype(f32)


def final_call(core, own, other):
    return pl.pallas_call(
        final_kernel,
        out_shape=(jax.ShapeDtypeStruct((VIS, EMB), f32), jax.ShapeDtypeStruct((TXT, EMB), f32)),
        in_specs=[SMEM, VMEM, VMEM],
        out_specs=(VMEM, VMEM),
        compiler_params=pltpu.CompilerParams(vmem_limit_bytes=40 * 1024 * 1024),
        name="final",
    )(core, own, other)


def split_lse(lse):
    high = lse.astype(bf16)
    low = (lse - high.astype(f32)).astype(bf16)
    return high, low


def reduce_heads(send, keep):
    part = keep + permute(send, "core", 2, 1).astype(f32)
    part = part.astype(bf16).reshape(16, HALF // 16, EMB)
    part = lax.all_to_all(part, PLANE, 0, 0, tiled=True)
    part = jnp.sum(part.astype(f32), axis=0).astype(bf16)
    others = [permute(part, "y", 4, d).astype(f32) for d in (1, 3, 2)]
    part = ((part.astype(f32) + others[2]) + (others[0] + others[1])).astype(bf16)
    whole = jnp.broadcast_to(part[None], (16, HALF // 16, EMB))
    whole = lax.all_to_all(whole, PLANE, 0, 0, tiled=True).reshape(HALF, EMB)
    return whole, permute(whole, "core", 2, 1)


def shards(image_feats, text_feats, image_head, text_head, image_lse, text_lse):
    image_rows = image_feats[0]
    text_rows = text_feats[0]
    core = lax.axis_index("core").astype(jnp.int32).reshape(1)

    high, low = split_lse(text_lse)
    text_msg = jnp.concatenate(
        [text_rows, jnp.pad(jnp.concatenate([high, low], axis=0), ((0, PAD - 2), (0, TXT - ROWS)))], axis=0
    )
    high, low = split_lse(image_lse)
    image_msg = jnp.concatenate(
        [image_rows, jnp.pad(jnp.concatenate([high, low], axis=1), ((0, PAD - 1), (0, 0)))], axis=0
    )
    texts = [text_msg] + [permute(text_msg, "y", 4, d) for d in (1, 3, 2)]
    partner = permute(image_msg, "xl", 2, 1)

    p1, p2, p3, tbase, ipart, ibase, send, keep = tile_call(core, image_msg, partner, texts, image_head, text_head)

    own, other = reduce_heads(send, keep)
    text_parts = [permute(p, "y", 4, -d) for p, d in ((p1, 1), (p2, 3), (p3, 2))]
    image_part = permute(ipart, "xl", 2, 1)
    text_back = back_call(text_rows, text_head, tbase, text_parts)
    image_back = back_call(image_rows, image_head, ibase, [image_part])
    image_total, text_total = final_call(core, own, other)
    return (image_back[None], text_back[None], image_total, text_total)


def solution(mesh):
    finer = Mesh(mesh.devices.reshape(4, 2, 4, 2, 2), BLK + REP)
    return jax.shard_map(
        shards,
        mesh=finer,
        in_specs=(P(REP, BLK, None), P(REP, BLK, None), P(), P(), P(REP, BLK), P(REP, BLK)),
        out_specs=(P(REP, BLK, None), P(REP, BLK, None), P(), P()),
        check_vma=False,
    )
```

time: 404 us -> 195 us (0.48)
  waiting for transfers between devices: 303 us -> 76.8 us
  Pallas kernels: 0 us -> 45.9 us
  matrix products: 44.6 us -> 0 us
  blocking collectives: 24.1 us -> 46.2 us
  starting transfers between devices: 0.2 us -> 20.2 us
  between operations: 13.9 us -> 0.8 us
  local copies, waits for them, and re-layouts: 12 us -> 0.15 us
    all_gather x4 -> x0, waiting for transfers between devices: 152 us -> none  [whole_of(): value = lax.all_gather(value, axis, axis=dim, tiled=True)]
    psum x1 -> x0, waiting for transfers between devices: 151 us -> none  [shards(): image_total, text_total = lax.psum((image_wgrad, text_wgrad), BLK_REP)]
    ppermute x0 -> x13, waiting for transfers between devices: none -> 76.8 us  [permute(): lax.ppermute(value, axis, [(i, (i + shift) % size) for i in range(size)])]
    all_to_all x0 -> x2, blocking collectives: none -> 46.2 us  [the longest x1 26.3 us: reduce_heads(): part = lax.all_to_all(part, PLANE, 0, 0, tiled=True)]
    pallas_call x0 -> x4, Pallas kernels: none -> 45.9 us  [the longest x1 34.5 us: tile_call(): pl.pallas_call(tile_kernel, out_shape=(block, block, block, wide, block,...]
    dot_general x8 -> x0, matrix products: 44.6 us -> none  [the longest x1 15.9 us: shards(): lax.dot_general(text_weights, image_piece, (((0,), (0,)), ((), ())), pref...]
    all_gather x4 -> x0, blocking collectives: 24.1 us -> none  [whole_of(): value = lax.all_gather(value, axis, axis=dim, tiled=True)]
    ppermute x0 -> x13, starting transfers between devices: none -> 20.2 us  [permute(): lax.ppermute(value, axis, [(i, (i + shift) % size) for i in range(size)])]
  transfers between devices with their start and end apart: 5 -> 13, of which waited for: 5 -> 7; matrix products, arithmetic and copies ran while one was open for 7% -> 0% of each run, Pallas kernels for 0% -> 4%
where the time goes in v1:
time: 195 us
  waiting for transfers between devices  76.8 us (39%)
  blocking collectives  46.2 us (24%)
  Pallas kernels  45.9 us (24%)
  starting transfers between devices  20.2 us (10%)
  other arithmetic  4.52 us (2%)
    ppermute x13, waiting for transfers between devices, permute(): lax.ppermute(value, axis, [(i, (i + shift) % size) for i in range(size)])  76.8 us
    pallas_call x1, Pallas kernels, tile_call(): pl.pallas_call(tile_kernel, out_shape=(block, block, block, wide, block,...  34.5 us
    all_to_all x1, blocking collectives, reduce_heads(): part = lax.all_to_all(part, PLANE, 0, 0, tiled=True)  26.3 us
    ppermute x13, starting transfers between devices, permute(): lax.ppermute(value, axis, [(i, (i + shift) % size) for i in range(size)])  20.2 us
    all_to_all x1, blocking collectives, reduce_heads(): whole = lax.all_to_all(whole, PLANE, 0, 0, tiled=True).reshape(HALF, EMB)  20 us
    pallas_call x2, Pallas kernels, back_call(): pl.pallas_call(functools.partial(back_kernel, len(parts)), out_shape=jax....  8.73 us
  transfers between devices with their start and end apart: 13, of which 7 were waited for; matrix products, arithmetic and copies ran while one was open for 0% of the time, Pallas kernels for 4%

profile of v1, /device:TPU:1, one launch (start us, length us, event | category | flops | bytes accessed | tf_op | source)
XLA Modules:
  0.0 194.6 jit_solution(9221169005607308597)
XLA Ops:
  0.7 0.8 fusion.10
  1.4 1.3 pad_maximum_fusion.i0
  2.8 2.1 %collective-permute-start = (bf16[528,1024]{1,0:T(8,128)(2,1)S(1)}, bf16[528,1024]{1,0:T(8,128)(2,1)}, u32[]{:S(2)}, u32[]{:S(2)}) collective-permute-start(bf16[528,1024]{1,0:T(8,128)(2,1)S(1)} %pad_maximum_fusion.i0), channel_id=1, source_target_pairs={{0,16},{16,0},{1,17},{17,1},{2,18},{18,2},{3,19},{19,3},{4,20},{20... | collective-permute-start | bytes 3244040 | tf_op jit(solution)/shard_map/ppermute | solution.py:34
  5.0 3.0 %collective-permute-start.3 = (bf16[528,768]{1,0:T(8,128)(2,1)S(1)}, bf16[528,768]{1,0:T(8,128)(2,1)S(1)}, u32[]{:S(2)}, u32[]{:S(2)}) collective-permute-start(bf16[528,768]{1,0:T(8,128)(2,1)S(1)} %pad_maximum_fusion.1.t0), channel_id=1, source_target_pairs={{0,64},{32,96},{64,0},{96,32},{1,65},{33,97},{65,1},{97,33},{2,66}... | collective-permute-start | bytes 2433032 | tf_op jit(solution)/shard_map/ppermute | solution.py:34
  9.4 15.8 %collective-permute-done.3.t3 = bf16[528,768]{1,0:T(8,128)(2,1)S(1)} collective-permute-done((bf16[528,768]{1,0:T(8,128)(2,1)S(1)}, bf16[528,768]{1,0:T(8,128)(2,1)S(1)}, u32[]{:S(2)}, u32[]{:S(2)}) %collective-permute-start.3) | collective-permute-done | bytes 811040 | tf_op jit(solution)/shard_map/ppermute | solution.py:34
  25.2 18.0 %collective-permute-done.2.t2 = bf16[528,768]{1,0:T(8,128)(2,1)} collective-permute-done((bf16[528,768]{1,0:T(8,128)(2,1)S(1)}, bf16[528,768]{1,0:T(8,128)(2,1)}, u32[]{:S(2)}, u32[]{:S(2)}) %collective-permute-start.2) | collective-permute-done | bytes 811040 | tf_op jit(solution)/shard_map/ppermute | solution.py:34
  43.3 0.8 collective-permute-done.1.t1
  44.1 34.5 %tile.1 = (bf16[512,768]{1,0:T(8,128)(2,1)}, bf16[512,768]{1,0:T(8,128)(2,1)}, bf16[512,768]{1,0:T(8,128)(2,1)}, f32[512,768]{1,0:T(8,128)}, bf16[512,768]{1,0:T...) custom-call(s32[1]{0:T(128)} %bitcast.1.core, bf16[528,1024]{1,0:T(8,128)(2,1)} %copy-done.6, ...), custom_call_target="tpu_custom_call" | custom-call | flops 20000000000 | bytes 20000000 | tf_op jit(solution)/shard_map/tile/pallas_call | solution.py:161
  78.5 0.9 collective-permute-start.8
  79.4 3.0 %collective-permute-done.8 = bf16[896,768]{1,0:T(8,128)(2,1)S(1)} collective-permute-done((bf16[896,768]{1,0:T(8,128)(2,1)}, bf16[896,768]{1,0:T(8,128)(2,1)S(1)}, u32[]{:S(2)}, u32[]{:S(2)}) %collective-permute-start.8) | collective-permute-done | bytes 1376288 | tf_op jit(solution)/shard_map/ppermute | solution.py:34
  82.4 2.1 %add_convert_fusion = bf16[896,768]{1,0:T(8,128)(2,1)S(1)} fusion(f32[896,768]{1,0:T(8,128)} %get-tuple-element.20, bf16[896,768]{1,0:T(8,128)(2,1)S(1)} %collective-permute-done.8), kind=kLoop, calls=%fused_computation | loop fusion | flops 2064384 | bytes 5505024 | tf_op jit(solution)/shard_map/convert_element_type | solution.py:236
  84.5 26.3 %all_to_all.10 = bf16[16,56,768]{2,1,0:T(8,128)(2,1)S(1)} all-to-all(bf16[16,56,768]{2,1,0:T(8,128)(2,1)S(1)} %bitcast.13), channel_id=1, replica_groups=mesh['y'=4,'xl'=2,'z'=4,'xh'=2,'core'=2] {'xl','z','xh'}, dimensions={0} | all-to-all | bytes 2752512 | tf_op jit(solution)/shard_map/all_to_all | solution.py:237
  111.0 2.4 %collective-permute-start.11 = (bf16[56,768]{1,0:T(8,128)(2,1)S(1)}, bf16[56,768]{1,0:T(8,128)(2,1)S(1)}, u32[]{:S(2)}, u32[]{:S(2)}) collective-permute-start(bf16[56,768]{1,0:T(8,128)(2,1)S(1)} %reduce_sum.12), channel_id=1, source_target_pairs={{0,96},{32,0},{64,32},{96,64},{1,97},{33,1},{65,33},{97,65},{2,98}... | collective-permute-start | bytes 258056 | tf_op jit(solution)/shard_map/ppermute | solution.py:34
  113.4 1.6 collective-permute-start.9
  115.1 3.8 %collective-permute-done.10 = bf16[56,768]{1,0:T(8,128)(2,1)S(1)} collective-permute-done((bf16[56,768]{1,0:T(8,128)(2,1)S(1)}, bf16[56,768]{1,0:T(8,128)(2,1)S(1)}, u32[]{:S(2)}, u32[]{:S(2)}) %collective-permute-start.10) | collective-permute-done | bytes 86048 | tf_op jit(solution)/shard_map/ppermute | solution.py:34
  119.1 20.0 %all_to_all.11 = bf16[16,56,768]{2,1,0:T(8,128)(2,1)S(1)} all-to-all(bf16[16,56,768]{2,1,0:T(8,128)(2,1)S(1)} %broadcast_in_dim.14), channel_id=1, replica_groups=mesh['y'=4,'xl'=2,'z'=4,'xh'=2,'core'=2] {'xl','z','xh'}, dimensions={0} | all-to-all | bytes 2752512 | tf_op jit(solution)/shard_map/all_to_all | solution.py:242
  139.0 5.0 %collective-permute-start.12 = (bf16[896,768]{1,0:T(8,128)(2,1)S(1)}, bf16[896,768]{1,0:T(8,128)(2,1)S(1)}, u32[]{:S(2)}, u32[]{:S(2)}) collective-permute-start(bf16[896,768]{1,0:T(8,128)(2,1)S(1)} %bitcast.7), channel_id=1, source_target_pairs={{0,1},{1,0},{2,3},{3,2},{4,5},{5,4},{6,7},{7,6},{8,9},{9,8},{10,11... | collective-permute-start | bytes 4128776 | tf_op jit(solution)/shard_map/ppermute | solution.py:34
  144.0 2.2 %collective-permute-start.5 = (bf16[512,768]{1,0:T(8,128)(2,1)}, bf16[512,768]{1,0:T(8,128)(2,1)S(1)}, u32[]{:S(2)}, u32[]{:S(2)}) collective-permute-start(bf16[512,768]{1,0:T(8,128)(2,1)} %get-tuple-element.17), channel_id=1, source_target_pairs={{0,96},{32,0},{64,32},{96,64},{1,97},{33,1},{65,33},{97,65},{2,98}... | collective-permute-start | bytes 2359304 | tf_op jit(solution)/shard_map/ppermute | solution.py:34
  146.2 1.2 collective-permute-start.7
  147.7 32.5 %collective-permute-done.5.rest_0_ = bf16[512,768]{1,0:T(8,128)(2,1)S(1)} collective-permute-done((bf16[512,768]{1,0:T(8,128)(2,1)}, bf16[512,768]{1,0:T(8,128)(2,1)S(1)}, u32[]{:S(2)}, u32[]{:S(2)}) %collective-permute-start.5) | collective-permute-done | bytes 786464 | tf_op jit(solution)/shard_map/ppermute | solution.py:34
  180.2 2.9 %collective-permute-done.6.rest_1_ = bf16[512,768]{1,0:T(8,128)(2,1)S(1)} collective-permute-done((bf16[512,768]{1,0:T(8,128)(2,1)S(1)}, bf16[512,768]{1,0:T(8,128)(2,1)S(1)}, u32[]{:S(2)}, u32[]{:S(2)}) %collective-permute-start.6) | collective-permute-done | bytes 786464 | tf_op jit(solution)/shard_map/ppermute | solution.py:34
  183.2 3.9 %back.3 = f32[512,768]{1,0:T(8,128)} custom-call(bf16[512,768]{1,0:T(8,128)(2,1)S(1)} %bitcast.12, bf16[768,768]{1,0:T(8,128)(2,1)S(1)} %copy-done.5, f32[512,768]{1,0:T(8,128)S(1)} %copy-done.4, bf16[512,768]{1,0:T(8,128)(2,1)S(1)} %collective-permute-done.5.rest_0_, bf16[512,768]{1,0:T(8,128)(2,1)S(1)} %collective-permute-done.6.rest_1_, ...), custom_call_target="tpu_custom_call" | custom-call | flops 1207959552 | bytes 10000000 | tf_op jit(solution)/shard_map/back/pallas_call | solution.py:199
  187.1 4.8 %back.2 = f32[512,1024]{1,0:T(8,128)} custom-call(bf16[512,1024]{1,0:T(8,128)(2,1)S(1)} %bitcast.10, bf16[1024,768]{1,0:T(8,128)(2,1)S(1)} %copy-done.2, f32[512,768]{1,0:T(8,128)S(1)} %copy-done.3, bf16[512,768]{1,0:T(8,128)(2,1)S(1)} %collective-permute-done.4.rest_0_), custom_call_target="tpu_custom_call" | custom-call | flops 1610612736 | bytes 10000000 | tf_op jit(solution)/shard_map/back/pallas_call | solution.py:199
  191.9 2.7 %final.1 = (f32[1024,768]{1,0:T(8,128)}, f32[768,768]{1,0:T(8,128)}) custom-call(s32[1]{0:T(128)} %bitcast.1.core, bf16[896,768]{1,0:T(8,128)(2,1)S(1)} %bitcast.8, bf16[896,768]{1,0:T(8,128)(2,1)S(1)} %collective-permute-done.12.other), custom_call_target="tpu_custom_call" | custom-call | tf_op jit(solution)/shard_map/final/pallas_call | solution.py:218
  (44 shorter events, 2.2 us)
Async XLA Ops:
  0.6 4.2 %copy-start.8 = (f32[1,512]{1,0:T(1,128)S(1)}, f32[1,512]{1,0:T(1,128)}, u32[]{:S(2)}) copy-start(f32[1,512]{1,0:T(1,128)} %param.11) | copy-start | bytes 6148
  0.6 4.3 %copy-start.1 = (bf16[1,512,768]{2,1,0:T(8,128)(2,1)S(1)}, bf16[1,512,768]{2,1,0:T(8,128)(2,1)}, u32[]{:S(2)}) copy-start(bf16[1,512,768]{2,1,0:T(8,128)(2,1)} %param.7) | copy-start | bytes 2359300
  2.7 41.3 %copy-start.6 = (bf16[528,1024]{1,0:T(8,128)(2,1)}, bf16[528,1024]{1,0:T(8,128)(2,1)S(1)}, u32[]{:S(2)}) copy-start(bf16[528,1024]{1,0:T(8,128)(2,1)S(1)} %pad_maximum_fusion.i0) | copy-start | bytes 3244036
  2.8 41.3 %collective-permute-start = (bf16[528,1024]{1,0:T(8,128)(2,1)S(1)}, bf16[528,1024]{1,0:T(8,128)(2,1)}, u32[]{:S(2)}, u32[]{:S(2)}) collective-permute-start(bf16[528,1024]{1,0:T(8,128)(2,1)S(1)} %pad_maximum_fusion.i0), channel_id=1, source_target_pairs={{0,16},{16,0},{1,17},{17,1},{2,18},{18,2},{3,19},{19,3},{4,20},{20... | collective-permute-start | bytes 3244040 | tf_op jit(solution)/shard_map/ppermute | solution.py:34
  5.0 39.1 %copy-start.7 = (bf16[528,768]{1,0:T(8,128)(2,1)}, bf16[528,768]{1,0:T(8,128)(2,1)S(1)}, u32[]{:S(2)}) copy-start(bf16[528,768]{1,0:T(8,128)(2,1)S(1)} %pad_maximum_fusion.1.t0) | copy-start | bytes 2433028
  5.0 20.2 %collective-permute-start.3 = (bf16[528,768]{1,0:T(8,128)(2,1)S(1)}, bf16[528,768]{1,0:T(8,128)(2,1)S(1)}, u32[]{:S(2)}, u32[]{:S(2)}) collective-permute-start(bf16[528,768]{1,0:T(8,128)(2,1)S(1)} %pad_maximum_fusion.1.t0), channel_id=1, source_target_pairs={{0,64},{32,96},{64,0},{96,32},{1,65},{33,97},{65,1},{97,33},{2,66}... | collective-permute-start | bytes 2433032 | tf_op jit(solution)/shard_map/ppermute | solution.py:34
  8.0 35.3 %collective-permute-start.2 = (bf16[528,768]{1,0:T(8,128)(2,1)S(1)}, bf16[528,768]{1,0:T(8,128)(2,1)}, u32[]{:S(2)}, u32[]{:S(2)}) collective-permute-start(bf16[528,768]{1,0:T(8,128)(2,1)S(1)} %pad_maximum_fusion.1.t0), channel_id=1, source_target_pairs={{0,96},{32,0},{64,32},{96,64},{1,97},{33,1},{65,33},{97,65},{2,98}... | collective-permute-start | bytes 2433032 | tf_op jit(solution)/shard_map/ppermute | solution.py:34
  8.8 35.3 %collective-permute-start.1 = (bf16[528,768]{1,0:T(8,128)(2,1)S(1)}, bf16[528,768]{1,0:T(8,128)(2,1)}, u32[]{:S(2)}, u32[]{:S(2)}) collective-permute-start(bf16[528,768]{1,0:T(8,128)(2,1)S(1)} %pad_maximum_fusion.1.t0), channel_id=1, source_target_pairs={{0,32},{32,64},{64,96},{96,0},{1,33},{33,65},{65,97},{97,1},{2,34}... | collective-permute-start | bytes 2433032 | tf_op jit(solution)/shard_map/ppermute | solution.py:34
  25.2 18.8 %copy-start.9 = (bf16[528,768]{1,0:T(8,128)(2,1)}, bf16[528,768]{1,0:T(8,128)(2,1)S(1)}, u32[]{:S(2)}) copy-start(bf16[528,768]{1,0:T(8,128)(2,1)S(1)} %collective-permute-done.3.t3) | copy-start | bytes 2433028
  78.5 3.9 %collective-permute-start.8 = (bf16[896,768]{1,0:T(8,128)(2,1)}, bf16[896,768]{1,0:T(8,128)(2,1)S(1)}, u32[]{:S(2)}, u32[]{:S(2)}) collective-permute-start(bf16[896,768]{1,0:T(8,128)(2,1)} %get-tuple-element.21), channel_id=1, source_target_pairs={{0,1},{1,0},{2,3},{3,2},{4,5},{5,4},{6,7},{7,6},{8,9},{9,8},{10,11... | collective-permute-start | bytes 4128776 | tf_op jit(solution)/shard_map/ppermute | solution.py:34
  110.8 35.4 %copy-start.12 = (bf16[512,768]{1,0:T(8,128)(2,1)S(1)}, bf16[512,768]{1,0:T(8,128)(2,1)}, u32[]{:S(2)}) copy-start(bf16[512,768]{1,0:T(8,128)(2,1)} %get-tuple-element.18) | copy-start | bytes 2359300
  111.0 4.1 %collective-permute-start.11 = (bf16[56,768]{1,0:T(8,128)(2,1)S(1)}, bf16[56,768]{1,0:T(8,128)(2,1)S(1)}, u32[]{:S(2)}, u32[]{:S(2)}) collective-permute-start(bf16[56,768]{1,0:T(8,128)(2,1)S(1)} %reduce_sum.12), channel_id=1, source_target_pairs={{0,96},{32,0},{64,32},{96,64},{1,97},{33,1},{65,33},{97,65},{2,98}... | collective-permute-start | bytes 258056 | tf_op jit(solution)/shard_map/ppermute | solution.py:34
  113.4 5.5 %collective-permute-start.10 = (bf16[56,768]{1,0:T(8,128)(2,1)S(1)}, bf16[56,768]{1,0:T(8,128)(2,1)S(1)}, u32[]{:S(2)}, u32[]{:S(2)}) collective-permute-start(bf16[56,768]{1,0:T(8,128)(2,1)S(1)} %reduce_sum.12), channel_id=1, source_target_pairs={{0,32},{32,64},{64,96},{96,0},{1,33},{33,65},{65,97},{97,1},{2,34}... | collective-permute-start | bytes 258056 | tf_op jit(solution)/shard_map/ppermute | solution.py:34
  113.4 5.5 %collective-permute-start.9 = (bf16[56,768]{1,0:T(8,128)(2,1)S(1)}, bf16[56,768]{1,0:T(8,128)(2,1)S(1)}, u32[]{:S(2)}, u32[]{:S(2)}) collective-permute-start(bf16[56,768]{1,0:T(8,128)(2,1)S(1)} %reduce_sum.12), channel_id=1, source_target_pairs={{0,64},{32,96},{64,0},{96,32},{1,65},{33,97},{65,1},{97,33},{2,66}... | collective-permute-start | bytes 258056 | tf_op jit(solution)/shard_map/ppermute | solution.py:34
  118.9 27.3 %copy-start.11 = (bf16[512,768]{1,0:T(8,128)(2,1)S(1)}, bf16[512,768]{1,0:T(8,128)(2,1)}, u32[]{:S(2)}) copy-start(bf16[512,768]{1,0:T(8,128)(2,1)} %get-tuple-element.19) | copy-start | bytes 2359300
  118.9 28.4 %copy-start.10 = (bf16[512,768]{1,0:T(8,128)(2,1)S(1)}, bf16[512,768]{1,0:T(8,128)(2,1)}, u32[]{:S(2)}) copy-start(bf16[512,768]{1,0:T(8,128)(2,1)} %get-tuple-element.15) | copy-start | bytes 2359300
  119.1 64.1 %copy-start.4 = (f32[512,768]{1,0:T(8,128)S(1)}, f32[512,768]{1,0:T(8,128)}, u32[]{:S(2)}) copy-start(f32[512,768]{1,0:T(8,128)} %get-tuple-element.16.base) | copy-start | bytes 4718596
  119.1 64.1 %copy-start.5 = (bf16[768,768]{1,0:T(8,128)(2,1)S(1)}, bf16[768,768]{1,0:T(8,128)(2,1)}, u32[]{:S(2)}) copy-start(bf16[768,768]{1,0:T(8,128)(2,1)} %head.3) | copy-start | bytes 3538948
  139.0 52.9 %collective-permute-start.12 = (bf16[896,768]{1,0:T(8,128)(2,1)S(1)}, bf16[896,768]{1,0:T(8,128)(2,1)S(1)}, u32[]{:S(2)}, u32[]{:S(2)}) collective-permute-start(bf16[896,768]{1,0:T(8,128)(2,1)S(1)} %bitcast.7), channel_id=1, source_target_pairs={{0,1},{1,0},{2,3},{3,2},{4,5},{5,4},{6,7},{7,6},{8,9},{9,8},{10,11... | collective-permute-start | bytes 4128776 | tf_op jit(solution)/shard_map/ppermute | solution.py:34
  144.0 36.2 %collective-permute-start.5 = (bf16[512,768]{1,0:T(8,128)(2,1)}, bf16[512,768]{1,0:T(8,128)(2,1)S(1)}, u32[]{:S(2)}, u32[]{:S(2)}) collective-permute-start(bf16[512,768]{1,0:T(8,128)(2,1)} %get-tuple-element.17), channel_id=1, source_target_pairs={{0,96},{32,0},{64,32},{96,64},{1,97},{33,1},{65,33},{97,65},{2,98}... | collective-permute-start | bytes 2359304 | tf_op jit(solution)/shard_map/ppermute | solution.py:34
  146.2 36.9 %collective-permute-start.6 = (bf16[512,768]{1,0:T(8,128)(2,1)S(1)}, bf16[512,768]{1,0:T(8,128)(2,1)S(1)}, u32[]{:S(2)}, u32[]{:S(2)}) collective-permute-start(bf16[512,768]{1,0:T(8,128)(2,1)S(1)} %copy-done.12), channel_id=1, source_target_pairs={{0,32},{32,64},{64,96},{96,0},{1,33},{33,65},{65,97},{97,1},{2,34}... | collective-permute-start | bytes 2359304 | tf_op jit(solution)/shard_map/ppermute | solution.py:34
  146.2 36.9 %collective-permute-start.7 = (bf16[512,768]{1,0:T(8,128)(2,1)S(1)}, bf16[512,768]{1,0:T(8,128)(2,1)S(1)}, u32[]{:S(2)}, u32[]{:S(2)}) collective-permute-start(bf16[512,768]{1,0:T(8,128)(2,1)S(1)} %copy-done.11), channel_id=1, source_target_pairs={{0,64},{32,96},{64,0},{96,32},{1,65},{33,97},{65,1},{97,33},{2,66}... | collective-permute-start | bytes 2359304 | tf_op jit(solution)/shard_map/ppermute | solution.py:34
  147.4 39.7 %collective-permute-start.4 = (bf16[512,768]{1,0:T(8,128)(2,1)S(1)}, bf16[512,768]{1,0:T(8,128)(2,1)S(1)}, u32[]{:S(2)}, u32[]{:S(2)}) collective-permute-start(bf16[512,768]{1,0:T(8,128)(2,1)S(1)} %copy-done.10), channel_id=1, source_target_pairs={{0,16},{16,0},{1,17},{17,1},{2,18},{18,2},{3,19},{19,3},{4,20},{20... | collective-permute-start | bytes 2359304 | tf_op jit(solution)/shard_map/ppermute | solution.py:34
  183.1 4.0 %copy-start = (bf16[1,512,1024]{2,1,0:T(8,128)(2,1)S(1)}, bf16[1,512,1024]{2,1,0:T(8,128)(2,1)}, u32[]{:S(2)}) copy-start(bf16[1,512,1024]{2,1,0:T(8,128)(2,1)} %param.6) | copy-start | bytes 3145732
  (2 other events, 7.9 us)

commit v2 on v0

v2 whole, which is shorter than its diff:
```python
import functools
import math

import jax
import jax.numpy as jnp
from jax import lax
from jax.experimental import pallas as pl
from jax.experimental.pallas import tpu as pltpu
from jax.sharding import Mesh
from jax.sharding import PartitionSpec as P

BLK = ("y", "xl")
REP = ("z", "xh", "core")
PLANE = ("xl", "z", "xh")

bf16 = jnp.bfloat16
f32 = jnp.float32

logit_scale = 50.0
epsilon = 1e-06
exp2_scale = logit_scale * math.log2(math.e)

ROWS = 512
PAD = 16
EMB = 768
VIS = 1024
TXT = 768
HV = VIS // 2
HT = TXT // 2
HALF = HV + HT


def permute(value, axis, size, shift):
    return lax.ppermute(value, axis, [(i, (i + shift) % size) for i in range(size)])


def nt(a, b):
    return lax.dot_general(a, b, (((1,), (1,)), ((), ())), preferred_element_type=f32)


def tn(a, b):
    return lax.dot_general(a, b, (((0,), (0,)), ((), ())), preferred_element_type=f32)


def nn(a, b):
    return jnp.dot(a, b, preferred_element_type=f32)


def scale_of(raw):
    return lax.rsqrt(jnp.sum(raw * raw, axis=1, keepdims=True) + epsilon)


def pre_gradient(raw, grad):
    factor = scale_of(raw)
    embed = raw * factor
    inner = jnp.sum(embed * grad, axis=1, keepdims=True)
    return (factor * (grad - embed * inner)).astype(bf16)


CH = 256
MID = ROWS // 2
CHUNKS = range(0, ROWS, CH)
ANY = pl.BlockSpec(memory_space=pl.ANY)
VMEM = pl.BlockSpec(memory_space=pltpu.VMEM)
SMEM = pl.BlockSpec(memory_space=pltpu.SMEM)
LIMIT = pltpu.CompilerParams(vmem_limit_bytes=48 * 1024 * 1024)


def wide(rows, columns=EMB):
    return jax.ShapeDtypeStruct((rows, columns), f32)


def narrow(rows, columns=EMB):
    return jax.ShapeDtypeStruct((rows, columns), bf16)


class Copies:
    def __init__(self, sems):
        self.sems = sems
        self.count = 0

    def start(self, src, dst):
        copy = pltpu.make_async_copy(src, dst, self.sems.at[self.count])
        self.count += 1
        copy.start()
        return copy


def own_kernel(image, text, hi, ht, zi, ri, zt, rt):
    for feats, head, raw_ref, round_ref in ((image, hi, zi, ri), (text, ht, zt, rt)):
        for c in CHUNKS:
            raw = nn(feats[c : c + CH, :], head[...])
            raw_ref[c : c + CH, :] = raw
            round_ref[c : c + CH, :] = (raw * scale_of(raw)).astype(bf16)


def own_call(image, text, hi, ht):
    return pl.pallas_call(
        own_kernel,
        out_shape=(wide(ROWS), narrow(ROWS), wide(ROWS), narrow(ROWS)),
        in_specs=[VMEM] * 4,
        out_specs=(VMEM,) * 4,
        compiler_params=LIMIT,
        cost_estimate=pl.CostEstimate(flops=14 * 10**8, bytes_accessed=10**7, transcendentals=0),
        name="own",
    )(image, text, hi, ht)


def column_weights(lse_row):
    row = 0.5 * jnp.exp(-lse_row)
    return jnp.broadcast_to(row, (128, ROWS)).T


def image_tail(tail):
    tail = tail[...].astype(f32)
    return tail[0:1, 0:ROWS] + tail[0:1, ROWS : 2 * ROWS]


def text_tail(tail):
    tail = tail[...].astype(f32)
    return tail[0:1, 0:ROWS] + tail[1:2, 0:ROWS]


def fill_weights(ri, rt_block, ea, lse_row, w, column):
    eb = 0.5 * jnp.exp(-lse_row)
    for r in range(0, 2 * ROWS, CH):
        s = nt(ri[r : r + CH, :], rt_block)
        both = jnp.concatenate([ea[r : r + CH, :]] * (ROWS // 128), axis=1) + eb
        w[r : r + CH, column : column + ROWS] = (jnp.exp2(s * exp2_scale) * both).astype(bf16)


def first_kernel(i1, t0, t1, t2, ri0, rt0, zt0, lse_i, lse_t, hi, ht,
                 tbase, p1, p2, ri1, zi1, ig, wt,
                 ri, ea, t, rt, zt, w, pre, image, head_i, head_t, itail, ttail, zout, bout, pout, iout, wout, sems):
    io = Copies(sems)
    n = ROWS
    c_image = io.start(i1.at[pl.ds(0, n)], image)
    c_hi = io.start(hi, head_i)
    c_itail = io.start(i1.at[pl.ds(n, PAD)], itail)
    c_rt0 = io.start(rt0, rt.at[pl.ds(0, n)])
    c_ri0 = io.start(ri0, ri.at[pl.ds(0, n)])
    c_zt0 = io.start(zt0, zt.at[pl.ds(0, n)])
    c_t = [io.start(t0, t.at[pl.ds(0, n)])]
    c_ht = io.start(ht, head_t)
    c_tail = []
    for b, ref in ((1, t1), (2, t2)):
        c_t.append(io.start(ref.at[pl.ds(0, n)], t.at[pl.ds(b * n, n)]))
        c_tail.append(io.start(ref.at[pl.ds(n, PAD)], ttail.at[b - 1]))
    outs = []

    c_image.wait()
    c_hi.wait()
    for c in CHUNKS:
        raw = nn(image[c : c + CH, :], head_i[...])
        zout[c : c + CH, :] = raw
        ri[n + c : n + c + CH, :] = (raw * scale_of(raw)).astype(bf16)
    outs.append(io.start(zout, zi1))
    outs.append(io.start(ri.at[pl.ds(n, n)], ri1))
    c_itail.wait()
    ea[0:n, :] = column_weights(lse_i[...])
    ea[n : 2 * n, :] = column_weights(image_tail(itail))
    c_rt0.wait()
    c_ri0.wait()
    for b in range(3):
        at = b * n
        c_t[b].wait()
        if b == 0:
            c_zt0.wait()
            lse_row = lse_t[...]
        else:
            c_tail[b - 1].wait()
            if b == 1:
                c_ht.wait()
            for c in CHUNKS:
                raw = nn(t[at + c : at + c + CH, :], head_t[...])
                zt[at + c : at + c + CH, :] = raw
                rt[at + c : at + c + CH, :] = (raw * scale_of(raw)).astype(bf16)
            lse_row = text_tail(ttail.at[b - 1])
        fill_weights(ri, rt[at : at + n, :], ea, lse_row, w, at)
        for c in CHUNKS:
            g = tn(w[:, at + c : at + c + CH], ri[...])
            if b == 0:
                g = g - ri[c : c + CH, :].astype(f32)
                bout[c : c + CH, :] = g
            else:
                pout[b - 1, c : c + CH, :] = g.astype(bf16)
            pre[at + c : at + c + CH, :] = pre_gradient(zt[at + c : at + c + CH, :], logit_scale * g)
        outs.append(io.start(bout, tbase) if b == 0 else io.start(pout.at[b - 1], (p1, p2)[b - 1]))
    for r in range(0, 2 * n, CH):
        g = nn(w[r : r + CH, :], rt[...])
        if r < n:
            g = g - rt[r : r + CH, :].astype(f32)
        iout[r : r + CH, :] = g
    outs.append(io.start(iout, ig))
    for r in range(0, TXT, CH):
        wout[r : r + CH, :] = tn(t[:, r : r + CH], pre[...])
    outs.append(io.start(wout, wt))
    for copy in outs:
        copy.wait()


def first_call(i1, t0, t1, t2, ri0, rt0, zt0, lse_i, lse_t, hi, ht):
    n = ROWS
    return pl.pallas_call(
        first_kernel,
        out_shape=(wide(n), narrow(n), narrow(n), narrow(n), wide(n), wide(2 * n), wide(TXT)),
        in_specs=[ANY] * 7 + [VMEM] * 2 + [ANY] * 2,
        out_specs=(ANY,) * 7,
        scratch_shapes=[
            pltpu.VMEM((2 * n, EMB), bf16),
            pltpu.VMEM((2 * n, 128), f32),
            pltpu.VMEM((3 * n, TXT), bf16),
            pltpu.VMEM((3 * n, EMB), bf16),
            pltpu.VMEM((3 * n, EMB), f32),
            pltpu.VMEM((2 * n, 3 * n), bf16),
            pltpu.VMEM((3 * n, EMB), bf16),
            pltpu.VMEM((n, VIS), bf16),
            pltpu.VMEM((VIS, EMB), bf16),
            pltpu.VMEM((TXT, EMB), bf16),
            pltpu.VMEM((PAD, VIS), bf16),
            pltpu.VMEM((2, PAD, TXT), bf16),
            pltpu.VMEM((n, EMB), f32),
            pltpu.VMEM((n, EMB), f32),
            pltpu.VMEM((2, n, EMB), bf16),
            pltpu.VMEM((2 * n, EMB), f32),
            pltpu.VMEM((TXT, EMB), f32),
            pltpu.SemaphoreType.DMA((24,)),
        ],
        compiler_params=LIMIT,
        cost_estimate=pl.CostEstimate(flops=12 * 10**9, bytes_accessed=20 * 10**6, transcendentals=2 * 10**6),
        name="first",
    )(i1, t0, t1, t2, ri0, rt0, zt0, lse_i, lse_t, hi, ht)


def second_kernel(core, i0, i1, t3a, t3b, p1, p2, ri0, ri1, zi0, zi1, ig, wt, lse_i, ht,
                  up, down, ipart, ibase, send, keep,
                  ri, ea, t, rt, zt, w, pre, prei, image, head_t, itail, ttail, zi, gi, wsum,
                  pout, qout, bout, sout, kout, sems):
    io = Copies(sems)
    n = ROWS
    c_t = [io.start(t3a, t.at[pl.ds(0, MID)]), io.start(t3b.at[pl.ds(0, n - MID)], t.at[pl.ds(MID, n - MID)])]
    c_ht = io.start(ht, head_t)
    c_ttail = io.start(t3b.at[pl.ds(n - MID, PAD)], ttail)
    c_itail = io.start(i1.at[pl.ds(n, PAD)], itail)
    c_ri = [io.start(ri0, ri.at[pl.ds(0, n)]), io.start(ri1, ri.at[pl.ds(n, n)])]
    c_ig = io.start(ig, gi)
    c_zi = [io.start(zi0, zi.at[pl.ds(0, n)]), io.start(zi1, zi.at[pl.ds(n, n)])]
    c_image = [io.start(i0, image.at[pl.ds(0, n)]), io.start(i1.at[pl.ds(0, n)], image.at[pl.ds(n, n)])]
    c_wt = io.start(wt, wsum)
    outs = [io.start(p2, up.at[pl.ds(0, n)]), io.start(p1, down.at[pl.ds(0, n)])]

    c_itail.wait()
    ea[0:n, :] = column_weights(lse_i[...])
    ea[n : 2 * n, :] = column_weights(image_tail(itail))
    for copy in c_t:
        copy.wait()
    c_ht.wait()
    for c in CHUNKS:
        raw = nn(t[c : c + CH, :], head_t[...])
        zt[c : c + CH, :] = raw
        rt[c : c + CH, :] = (raw * scale_of(raw)).astype(bf16)
    c_ttail.wait()
    for copy in c_ri:
        copy.wait()
    fill_weights(ri, rt[...], ea, text_tail(ttail), w, 0)
    for c in CHUNKS:
        g = tn(w[:, c : c + CH], ri[...])
        pout[c : c + CH, :] = g.astype(bf16)
        pre[c : c + CH, :] = pre_gradient(zt[c : c + CH, :], logit_scale * g)
    outs.append(io.start(pout.at[pl.ds(0, MID)], up.at[pl.ds(n, MID)]))
    outs.append(io.start(pout.at[pl.ds(MID, n - MID)], down.at[pl.ds(n, n - MID)]))
    c_ig.wait()
    for copy in c_zi:
        copy.wait()
    for r in range(0, 2 * n, CH):
        g = gi[r : r + CH, :] + nn(w[r : r + CH, :], rt[...])
        if r < n:
            bout[r : r + CH, :] = g
        else:
            qout[r - n : r - n + CH, :] = g.astype(bf16)
        prei[r : r + CH, :] = pre_gradient(zi[r : r + CH, :], logit_scale * g)
    outs.append(io.start(bout, ibase))
    outs.append(io.start(qout, ipart))
    for copy in c_image:
        copy.wait()
    c_wt.wait()
    mine = core[0]
    for which, ref, out in ((1 - mine, sout, send), (mine, kout, keep)):
        for c in range(0, HV, CH):
            cols = pl.ds(pl.multiple_of(which * HV + c, 128), CH)
            ref[c : c + CH, :] = tn(image[:, cols], prei[...]).astype(ref.dtype)
        for c in range(0, HT, 128):
            cols = pl.ds(pl.multiple_of(which * HT + c, 128), 128)
            ref[HV + c : HV + c + 128, :] = (wsum[cols, :] + tn(t[:, cols], pre[...])).astype(ref.dtype)
        outs.append(io.start(ref, out))
    for copy in outs:
        copy.wait()


def second_call(core, i0, i1, t3a, t3b, p1, p2, ri0, ri1, zi0, zi1, ig, wt, lse_i, ht):
    n = ROWS
    return pl.pallas_call(
        second_kernel,
        out_shape=(narrow(n + MID), narrow(n + MID), narrow(n), wide(n), narrow(HALF), wide(HALF)),
        in_specs=[SMEM] + [ANY] * 12 + [VMEM] + [ANY],
        out_specs=(ANY,) * 6,
        scratch_shapes=[
            pltpu.VMEM((2 * n, EMB), bf16),
            pltpu.VMEM((2 * n, 128), f32),
            pltpu.VMEM((n, TXT), bf16),
            pltpu.VMEM((n, EMB), bf16),
            pltpu.VMEM((n, EMB), f32),
            pltpu.VMEM((2 * n, n), bf16),
            pltpu.VMEM((n, EMB), bf16),
            pltpu.VMEM((2 * n, EMB), bf16),
            pltpu.VMEM((2 * n, VIS), bf16),
            pltpu.VMEM((TXT, EMB), bf16),
            pltpu.VMEM((PAD, VIS), bf16),
            pltpu.VMEM((PAD, TXT), bf16),
            pltpu.VMEM((2 * n, EMB), f32),
            pltpu.VMEM((2 * n, EMB), f32),
            pltpu.VMEM((TXT, EMB), f32),
            pltpu.VMEM((n, EMB), bf16),
            pltpu.VMEM((n, EMB), bf16),
            pltpu.VMEM((n, EMB), f32),
            pltpu.VMEM((HALF, EMB), bf16),
            pltpu.VMEM((HALF, EMB), f32),
            pltpu.SemaphoreType.DMA((24,)),
        ],
        compiler_params=LIMIT,
        cost_estimate=pl.CostEstimate(flops=8 * 10**9, bytes_accessed=20 * 10**6, transcendentals=10**6),
        name="second",
    )(core, i0, i1, t3a, t3b, p1, p2, ri0, ri1, zi0, zi1, ig, wt, lse_i, ht)


def back_kernel(whole, split, raw, head, base, *rest):
    out = rest[-1]
    for i, c in enumerate(CHUNKS):
        g = base[c : c + CH, :]
        for p in rest[:whole]:
            g = g + p[c : c + CH, :].astype(f32)
        if split:
            g = g + rest[whole + i][...].astype(f32)
        out[c : c + CH, :] = nt(pre_gradient(raw[c : c + CH, :], logit_scale * g), head[...])


def back_call(raw, head, base, parts, halves=()):
    width = head.shape[0]
    return pl.pallas_call(
        functools.partial(back_kernel, len(parts), len(halves) > 0),
        out_shape=wide(ROWS, width),
        in_specs=[VMEM] * (3 + len(parts) + len(halves)),
        out_specs=VMEM,
        compiler_params=pltpu.CompilerParams(vmem_limit_bytes=40 * 1024 * 1024),
        cost_estimate=pl.CostEstimate(flops=2 * ROWS * EMB * width, bytes_accessed=10 * 10**6, transcendentals=0),
        name="back",
    )(raw, head, base, *parts, *halves)


def final_kernel(core, own, other, image, text):
    mine = core[0]
    for ref, which in ((own, mine), (other, 1 - mine)):
        image[pl.ds(pl.multiple_of(which * HV, 128), HV), :] = ref[0:HV, :].astype(f32)
        text[pl.ds(pl.multiple_of(which * HT, 128), HT), :] = ref[HV:HALF, :].astype(f32)


def final_call(core, own, other):
    return pl.pallas_call(
        final_kernel,
        out_shape=(jax.ShapeDtypeStruct((VIS, EMB), f32), jax.ShapeDtypeStruct((TXT, EMB), f32)),
        in_specs=[SMEM, VMEM, VMEM],
        out_specs=(VMEM, VMEM),
        compiler_params=pltpu.CompilerParams(vmem_limit_bytes=40 * 1024 * 1024),
        name="final",
    )(core, own, other)


def split_lse(lse):
    high = lse.astype(bf16)
    low = (lse - high.astype(f32)).astype(bf16)
    return high, low


def reduce_heads(send, keep):
    part = keep + permute(send, "core", 2, 1).astype(f32)
    part = part.astype(bf16).reshape(16, HALF // 16, EMB)
    part = lax.all_to_all(part, PLANE, 0, 0, tiled=True)
    return jnp.sum(part.astype(f32), axis=0).astype(bf16)


def spread_heads(part):
    others = [permute(part, "y", 4, d).astype(f32) for d in (1, 3, 2)]
    part = ((part.astype(f32) + others[2]) + (others[0] + others[1])).astype(bf16)
    whole = jnp.broadcast_to(part[None], (16, HALF // 16, EMB))
    return lax.all_to_all(whole, PLANE, 0, 0, tiled=True).reshape(HALF, EMB)


def shards(image_feats, text_feats, image_head, text_head, image_lse, text_lse):
    image_rows = image_feats[0]
    text_rows = text_feats[0]
    core = lax.axis_index("core").astype(jnp.int32).reshape(1)

    high, low = split_lse(text_lse)
    text_msg = jnp.concatenate(
        [text_rows, jnp.pad(jnp.concatenate([high, low], axis=0), ((0, PAD - 2), (0, TXT - ROWS)))], axis=0
    )
    high, low = split_lse(image_lse)
    image_msg = jnp.concatenate(
        [image_rows, jnp.pad(jnp.concatenate([high, low], axis=1), ((0, PAD - 1), (0, 0)))], axis=0
    )
    t1 = permute(text_msg, "y", 4, 1)
    t2 = permute(text_msg, "y", 4, 3)
    i1 = permute(image_msg, "xl", 2, 1)
    zi0, ri0, zt0, rt0 = own_call(image_rows, text_rows, image_head, text_head)
    t3a = permute(t1[:MID], "y", 4, 1)
    t3b = permute(t2[MID:], "y", 4, 3)

    tbase, p1, p2, ri1, zi1, ig, wt = first_call(
        i1, text_rows, t1, t2, ri0, rt0, zt0, image_lse, text_lse, image_head, text_head
    )
    up, down, ipart, ibase, send, keep = second_call(
        core, image_rows, i1, t3a, t3b, p1, p2, ri0, ri1, zi0, zi1, ig, wt, image_lse, text_head
    )
    part = reduce_heads(send, keep)
    up, down, ipart = permute(up, "y", 4, 1), permute(down, "y", 4, 3), permute(ipart, "xl", 2, 1)
    part, up, down, ipart = lax.optimization_barrier((part, up, down, ipart))
    whole = spread_heads(part)
    top, bottom = permute(up[ROWS:], "y", 4, 1), permute(down[ROWS:], "y", 4, 3)
    text_back = back_call(zt0, text_head, tbase, [up, down], [top, bottom])
    image_back = back_call(zi0, image_head, ibase, [ipart])
    whole, text_back, image_back = lax.optimization_barrier((whole, text_back, image_back))
    image_total, text_total = final_call(core, whole, permute(whole, "core", 2, 1))
    return (image_back[None], text_back[None], image_total, text_total)


def solution(mesh):
    finer = Mesh(mesh.devices.reshape(4, 2, 4, 2, 2), BLK + REP)
    return jax.shard_map(
        shards,
        mesh=finer,
        in_specs=(P(REP, BLK, None), P(REP, BLK, None), P(), P(), P(REP, BLK), P(REP, BLK)),
        out_specs=(P(REP, BLK, None), P(REP, BLK, None), P(), P()),
        check_vma=False,
    )
```

time: 404 us -> 155 us (0.38)
  waiting for transfers between devices: 303 us -> 55.1 us
  matrix products: 44.6 us -> 0 us
  starting transfers between devices: 0.2 us -> 40.8 us
  Pallas kernels: 0 us -> 40.1 us
  blocking collectives: 24.1 us -> 0 us
  between operations: 13.9 us -> 0.84 us
    all_gather x4 -> x0, waiting for transfers between devices: 152 us -> none  [whole_of(): value = lax.all_gather(value, axis, axis=dim, tiled=True)]
    psum x1 -> x0, waiting for transfers between devices: 151 us -> none  [shards(): image_total, text_total = lax.psum((image_wgrad, text_wgrad), BLK_REP)]
    dot_general x8 -> x0, matrix products: 44.6 us -> none  [the longest x1 15.9 us: shards(): lax.dot_general(text_weights, image_piece, (((0,), (0,)), ((), ())), pref...]
    pallas_call x0 -> x6, Pallas kernels: none -> 40.1 us  [the longest x1 17.4 us: first_call(): pl.pallas_call(first_kernel, out_shape=(wide(n), narrow(n), narrow(n), na...]
    ppermute x0 -> x15, waiting for transfers between devices: none -> 35.9 us  [permute(): lax.ppermute(value, axis, [(i, (i + shift) % size) for i in range(size)])]
    ppermute x0 -> x15, starting transfers between devices: none -> 25 us  [permute(): lax.ppermute(value, axis, [(i, (i + shift) % size) for i in range(size)])]
    all_gather x4 -> x0, blocking collectives: 24.1 us -> none  [whole_of(): value = lax.all_gather(value, axis, axis=dim, tiled=True)]
    all_to_all x0 -> x2, waiting for transfers between devices: none -> 19.2 us  [the longest x1 15.8 us: reduce_heads(): part = lax.all_to_all(part, PLANE, 0, 0, tiled=True)]
  transfers between devices with their start and end apart: 5 -> 17, of which waited for: 5 -> 9; matrix products, arithmetic and copies ran while one was open for 7% -> 4% of each run, Pallas kernels for 0% -> 17%
where the time goes in v2:
time: 155 us; the launch traced here: 154 us
  waiting for transfers between devices  55.1 us (36%)
  starting transfers between devices  40.8 us (26%)
  Pallas kernels  40.1 us (26%)
  other arithmetic  8.95 us (6%)
  local copies, waits for them, and re-layouts  8.39 us (5%)
    ppermute x15, waiting for transfers between devices, permute(): lax.ppermute(value, axis, [(i, (i + shift) % size) for i in range(size)])  35.9 us
    ppermute x15, starting transfers between devices, permute(): lax.ppermute(value, axis, [(i, (i + shift) % size) for i in range(size)])  25 us
    pallas_call x1, Pallas kernels, first_call(): pl.pallas_call(first_kernel, out_shape=(wide(n), narrow(n), narrow(n), na...  17.4 us
    all_to_all x1, waiting for transfers between devices, reduce_heads(): part = lax.all_to_all(part, PLANE, 0, 0, tiled=True)  15.8 us
    pallas_call x1, Pallas kernels, second_call(): pl.pallas_call(second_kernel, out_shape=(narrow(n + MID), narrow(n + MID)...  10.7 us
    all_to_all x1, starting transfers between devices, spread_heads(): return lax.all_to_all(whole, PLANE, 0, 0, tiled=True).reshape(HALF, EMB)  8.43 us
    all_to_all x1, starting transfers between devices, reduce_heads(): part = lax.all_to_all(part, PLANE, 0, 0, tiled=True)  7.35 us
    pallas_call x2, Pallas kernels, back_call(): pl.pallas_call(functools.partial(back_kernel, len(parts), len(halves) > 0...  5.12 us
  transfers between devices with their start and end apart: 17, of which 9 were waited for; matrix products, arithmetic and copies ran while one was open for 4% of the time, Pallas kernels for 17%

profile of v2, /device:TPU:1, one launch (start us, length us, event | category | flops | bytes accessed | tf_op | source)
XLA Modules:
  0.0 154.2 jit_solution(740645917689909719)
XLA Ops:
  1.5 2.4 %pad_maximum_fusion = bf16[528,1024]{1,0:T(8,128)(2,1)} fusion(bf16[16,1024]{1,0:T(8,128)(2,1)S(1)} %fusion.7, bf16[512,1024]{1,0:T(8,128)(2,1)} %bitcast.9), kind=kLoop, calls=%fused_computation.1 | loop fusion | flops 2162688 | bytes 2162688 | tf_op jit(solution)/shard_map/concatenate | solution.py:408
  6.9 2.7 %collective-permute-start.3 = (bf16[528,768]{1,0:T(8,128)(2,1)}, bf16[528,768]{1,0:T(8,128)(2,1)}, u32[]{:S(2)}, u32[]{:S(2)}) collective-permute-start(bf16[528,768]{1,0:T(8,128)(2,1)} %pad_maximum_fusion.1), channel_id=1, source_target_pairs={{0,96},{32,0},{64,32},{96,64},{1,97},{33,1},{65,33},{97,65},{2,98}... | collective-permute-start | bytes 2433032 | tf_op jit(solution)/shard_map/ppermute | solution.py:34
  9.7 4.2 %own.1 = (f32[512,768]{1,0:T(8,128)S(1)}, bf16[512,768]{1,0:T(8,128)(2,1)S(1)}, f32[512,768]{1,0:T(8,128)}, bf16[512,768]{1,0:T(8,128)(2,1)S(1)}) custom-call(bf16[512,1024]{1,0:T(8,128)(2,1)S(1)} %bitcast.10, bf16[512,768]{1,0:T(8,128)(2,1)S(1)} %bitcast.13, bf16[1024,768]{1,0:T(8,128)(2,1)} %head.3, bf16[768,768]{1,0:T(8,128)(2,1)S(1)} %copy-done.8), custom_call_target="tpu_custom_call" | custom-call | flops 1400000000 | bytes 10000000 | tf_op jit(solution)/shard_map/own/pallas_call | solution.py:98
  15.0 11.4 %collective-permute-done.3.t2 = bf16[528,768]{1,0:T(8,128)(2,1)} collective-permute-done((bf16[528,768]{1,0:T(8,128)(2,1)}, bf16[528,768]{1,0:T(8,128)(2,1)}, u32[]{:S(2)}, u32[]{:S(2)}) %collective-permute-start.3) | collective-permute-done | bytes 811040 | tf_op jit(solution)/shard_map/ppermute | solution.py:34
  27.4 3.5 %collective-permute-start.4 = (bf16[272,768]{1,0:T(8,128)(2,1)S(1)}, bf16[272,768]{1,0:T(8,128)(2,1)S(1)}, u32[]{:S(2)}, u32[]{:S(2)}) collective-permute-start(bf16[272,768]{1,0:T(8,128)(2,1)S(1)} %slice.17), channel_id=1, source_target_pairs={{0,96},{32,0},{64,32},{96,64},{1,97},{33,1},{65,33},{97,65},{2,98}... | collective-permute-start | bytes 1253384 | tf_op jit(solution)/shard_map/ppermute | solution.py:34
  32.2 17.4 %first.1 = (f32[512,768]{1,0:T(8,128)}, bf16[512,768]{1,0:T(8,128)(2,1)S(1)}, bf16[512,768]{1,0:T(8,128)(2,1)S(1)}, bf16[512,768]{1,0:T(8,128)(2,1)S(1)}, f32[51...) custom-call(bf16[528,1024]{1,0:T(8,128)(2,1)} %collective-permute-done.i1, bf16[512,768]{1,0:T(8,128)(2,1)S(1)} %bitcast.14, ...), custom_call_target="tpu_custom_call" | custom-call | flops 12000000000 | bytes 20000000 | tf_op jit(solution)/shard_map/first/pallas_call | solution.py:204
  49.6 10.7 %second.1 = (bf16[768,768]{1,0:T(8,128)(2,1)}, bf16[768,768]{1,0:T(8,128)(2,1)}, bf16[512,768]{1,0:T(8,128)(2,1)S(1)}, f32[512,768]{1,0:T(8,128)}, bf16[896,768]{1,0:T(8,128)(2,1)}, /*index=5*/f32[896,768]{1,0:T(8,128)}) custom-call(s32[1]{0:T(128)} %bitcast.core, bf16[512,1024]{1,0:T(8,128)(2,1)S(1)} %bitcast.11, ...), custom_call_target="tpu_custom_call" | custom-call | flops 8000000000 | bytes 20000000 | tf_op jit(solution)/shard_map/second/pallas_call | solution.py:302
  60.3 2.2 %collective-permute-start.5 = (bf16[896,768]{1,0:T(8,128)(2,1)}, bf16[896,768]{1,0:T(8,128)(2,1)S(1)}, u32[]{:S(2)}, u32[]{:S(2)}) collective-permute-start(bf16[896,768]{1,0:T(8,128)(2,1)} %get-tuple-element.41), channel_id=1, source_target_pairs={{0,1},{1,0},{2,3},{3,2},{4,5},{5,4},{6,7},{7,6},{8,9},{9,8},{10,11... | collective-permute-start | bytes 4128776 | tf_op jit(solution)/shard_map/ppermute | solution.py:34
  62.5 3.0 %collective-permute-done.5 = bf16[896,768]{1,0:T(8,128)(2,1)S(1)} collective-permute-done((bf16[896,768]{1,0:T(8,128)(2,1)}, bf16[896,768]{1,0:T(8,128)(2,1)S(1)}, u32[]{:S(2)}, u32[]{:S(2)}) %collective-permute-start.5) | collective-permute-done | bytes 1376288 | tf_op jit(solution)/shard_map/ppermute | solution.py:34
  65.5 3.2 %add_convert_fusion = bf16[896,768]{1,0:T(8,128)(2,1)} fusion(f32[896,768]{1,0:T(8,128)} %get-tuple-element.40, bf16[896,768]{1,0:T(8,128)(2,1)S(1)} %collective-permute-done.5), kind=kLoop, calls=%fused_computation | loop fusion | flops 2064384 | bytes 5505024 | tf_op jit(solution)/shard_map/convert_element_type | solution.py:386
  68.7 7.3 %all-to-all-start = ((bf16[16,56,768]{2,1,0:T(8,128)(2,1)}), bf16[16,56,768]{2,1,0:T(8,128)(2,1)}, u32[]{:S(2)}, u32[]{:S(2)}) async-start(bf16[16,56,768]{2,1,0:T(8,128)(2,1)} %bitcast.3), calls=%async_computation | async-start | bytes 2752512 | tf_op jit(solution)/shard_map/all_to_all | solution.py:387
  76.1 3.0 %collective-permute-start.7 = (bf16[768,768]{1,0:T(8,128)(2,1)}, bf16[768,768]{1,0:T(8,128)(2,1)S(1)}, u32[]{:S(2)}, u32[]{:S(2)}) collective-permute-start(bf16[768,768]{1,0:T(8,128)(2,1)} %get-tuple-element.43), channel_id=1, source_target_pairs={{0,96},{32,0},{64,32},{96,64},{1,97},{33,1},{65,33},{97,65},{2,98}... | collective-permute-start | bytes 3538952 | tf_op jit(solution)/shard_map/ppermute | solution.py:34
  80.4 15.8 %all-to-all-done = bf16[16,56,768]{2,1,0:T(8,128)(2,1)} async-done(((bf16[16,56,768]{2,1,0:T(8,128)(2,1)}), bf16[16,56,768]{2,1,0:T(8,128)(2,1)}, u32[]{:S(2)}, u32[]{:S(2)}) %all-to-all-start) | async-done | bytes 1376288 | tf_op jit(solution)/shard_map/all_to_all | solution.py:387
  97.8 11.9 %collective-permute-done.8.rest_0_ = bf16[512,768]{1,0:T(8,128)(2,1)S(1)} collective-permute-done((bf16[512,768]{1,0:T(8,128)(2,1)}, bf16[512,768]{1,0:T(8,128)(2,1)S(1)}, u32[]{:S(2)}, u32[]{:S(2)}) %collective-permute-start.8) | collective-permute-done | bytes 786464 | tf_op jit(solution)/shard_map/ppermute | solution.py:34
  109.7 3.0 %collective-permute-start.11 = (bf16[56,768]{1,0:T(8,128)(2,1)S(1)}, bf16[56,768]{1,0:T(8,128)(2,1)S(1)}, u32[]{:S(2)}, u32[]{:S(2)}) collective-permute-start(bf16[56,768]{1,0:T(8,128)(2,1)S(1)} %reduce_sum.12), channel_id=1, source_target_pairs={{0,96},{32,0},{64,32},{96,64},{1,97},{33,1},{65,33},{97,65},{2,98}... | collective-permute-start | bytes 258056 | tf_op jit(solution)/shard_map/ppermute | solution.py:34
  114.2 3.9 %collective-permute-done.10 = bf16[56,768]{1,0:T(8,128)(2,1)S(1)} collective-permute-done((bf16[56,768]{1,0:T(8,128)(2,1)S(1)}, bf16[56,768]{1,0:T(8,128)(2,1)S(1)}, u32[]{:S(2)}, u32[]{:S(2)}) %collective-permute-start.10) | collective-permute-done | bytes 86048 | tf_op jit(solution)/shard_map/ppermute | solution.py:34
  119.4 8.4 %all-to-all-start.1 = ((bf16[16,56,768]{2,1,0:T(8,128)(2,1)}), bf16[16,56,768]{2,1,0:T(8,128)(2,1)S(1)}, u32[]{:S(2)}, u32[]{:S(2)}) async-start(bf16[16,56,768]{2,1,0:T(8,128)(2,1)} %broadcast_in_dim.12), calls=%async_computation.1 | async-start | bytes 2752512 | tf_op jit(solution)/shard_map/all_to_all | solution.py:395
  133.9 2.6 %back.3 = f32[512,1024]{1,0:T(8,128)} custom-call(f32[512,768]{1,0:T(8,128)S(1)} %copy-done.5, bf16[1024,768]{1,0:T(8,128)(2,1)S(1)} %copy-done.2, f32[512,768]{1,0:T(8,128)S(1)} %copy-done.7, bf16[512,768]{1,0:T(8,128)(2,1)S(1)} %collective-permute-done.8.rest_0_), custom_call_target="tpu_custom_call" | custom-call | flops 805306368 | bytes 10000000 | tf_op jit(solution)/shard_map/back/pallas_call | solution.py:349
  136.5 2.6 %collective-permute-done.12.rest_2_ = bf16[256,768]{1,0:T(8,128)(2,1)S(1)} collective-permute-done((bf16[256,768]{1,0:T(8,128)(2,1)S(1)}, bf16[256,768]{1,0:T(8,128)(2,1)S(1)}, u32[]{:S(2)}, u32[]{:S(2)}) %collective-permute-start.12) | collective-permute-done | bytes 393248 | tf_op jit(solution)/shard_map/ppermute | solution.py:34
  139.2 2.5 %back.2 = f32[512,768]{1,0:T(8,128)} custom-call(f32[512,768]{1,0:T(8,128)S(1)} %copy-done.3, bf16[768,768]{1,0:T(8,128)(2,1)S(1)} %copy-done.9, f32[512,768]{1,0:T(8,128)S(1)} %copy-done.6, bf16[768,768]{1,0:T(8,128)(2,1)S(1)} %collective-permute-done.6.rest_0_, bf16[768,768]{1,0:T(8,128)(2,1)S(1)} %copy-done.1, ...), custom_call_target="tpu_custom_call" | custom-call | flops 603979776 | bytes 10000000 | tf_op jit(solution)/shard_map/back/pallas_call | solution.py:349
  141.7 3.3 %all-to-all-done.1 = bf16[16,56,768]{2,1,0:T(8,128)(2,1)S(1)} async-done(((bf16[16,56,768]{2,1,0:T(8,128)(2,1)}), bf16[16,56,768]{2,1,0:T(8,128)(2,1)S(1)}, u32[]{:S(2)}, u32[]{:S(2)}) %all-to-all-start.1) | async-done | bytes 1376288 | tf_op jit(solution)/shard_map/all_to_all | solution.py:395
  145.0 3.7 %collective-permute-start.14 = (bf16[896,768]{1,0:T(8,128)(2,1)S(1)}, bf16[896,768]{1,0:T(8,128)(2,1)S(1)}, u32[]{:S(2)}, u32[]{:S(2)}) collective-permute-start(bf16[896,768]{1,0:T(8,128)(2,1)S(1)} %bitcast.7), channel_id=1, source_target_pairs={{0,1},{1,0},{2,3},{3,2},{4,5},{5,4},{6,7},{7,6},{8,9},{9,8},{10,11... | collective-permute-start | bytes 4128776 | tf_op jit(solution)/shard_map/ppermute | solution.py:34
  148.8 2.8 %collective-permute-done.14.other = bf16[896,768]{1,0:T(8,128)(2,1)S(1)} collective-permute-done((bf16[896,768]{1,0:T(8,128)(2,1)S(1)}, bf16[896,768]{1,0:T(8,128)(2,1)S(1)}, u32[]{:S(2)}, u32[]{:S(2)}) %collective-permute-start.14) | collective-permute-done | bytes 1376288 | tf_op jit(solution)/shard_map/ppermute | solution.py:34
  151.5 2.7 %final.1 = (f32[1024,768]{1,0:T(8,128)}, f32[768,768]{1,0:T(8,128)}) custom-call(s32[1]{0:T(128)} %bitcast.core, bf16[896,768]{1,0:T(8,128)(2,1)S(1)} %bitcast.8, bf16[896,768]{1,0:T(8,128)(2,1)S(1)} %collective-permute-done.14.other), custom_call_target="tpu_custom_call" | custom-call | tf_op jit(solution)/shard_map/final/pallas_call | solution.py:368
  (60 shorter events, 19.0 us)
Async XLA Ops:
  0.6 5.3 %copy-start.11 = (bf16[1,512,768]{2,1,0:T(8,128)(2,1)S(1)}, bf16[1,512,768]{2,1,0:T(8,128)(2,1)}, u32[]{:S(2)}) copy-start(bf16[1,512,768]{2,1,0:T(8,128)(2,1)} %param.7) | copy-start | bytes 2359300
  1.4 8.2 %copy-start.8 = (bf16[768,768]{1,0:T(8,128)(2,1)S(1)}, bf16[768,768]{1,0:T(8,128)(2,1)}, u32[]{:S(2)}) copy-start(bf16[768,768]{1,0:T(8,128)(2,1)} %head.2) | copy-start | bytes 3538948
  1.5 8.2 %copy-start.10 = (bf16[1,512,1024]{2,1,0:T(8,128)(2,1)S(1)}, bf16[1,512,1024]{2,1,0:T(8,128)(2,1)}, u32[]{:S(2)}) copy-start(bf16[1,512,1024]{2,1,0:T(8,128)(2,1)} %param.6) | copy-start | bytes 3145732
  3.9 28.3 %collective-permute-start = (bf16[528,1024]{1,0:T(8,128)(2,1)}, bf16[528,1024]{1,0:T(8,128)(2,1)}, u32[]{:S(2)}, u32[]{:S(2)}) collective-permute-start(bf16[528,1024]{1,0:T(8,128)(2,1)} %pad_maximum_fusion), channel_id=1, source_target_pairs={{0,16},{16,0},{1,17},{17,1},{2,18},{18,2},{3,19},{19,3},{4,20},{20... | collective-permute-start | bytes 3244040 | tf_op jit(solution)/shard_map/ppermute | solution.py:34
  6.9 19.5 %collective-permute-start.3 = (bf16[528,768]{1,0:T(8,128)(2,1)}, bf16[528,768]{1,0:T(8,128)(2,1)}, u32[]{:S(2)}, u32[]{:S(2)}) collective-permute-start(bf16[528,768]{1,0:T(8,128)(2,1)} %pad_maximum_fusion.1), channel_id=1, source_target_pairs={{0,96},{32,0},{64,32},{96,64},{1,97},{33,1},{65,33},{97,65},{2,98}... | collective-permute-start | bytes 2433032 | tf_op jit(solution)/shard_map/ppermute | solution.py:34
  9.6 21.3 %collective-permute-start.1 = (bf16[528,768]{1,0:T(8,128)(2,1)}, bf16[528,768]{1,0:T(8,128)(2,1)}, u32[]{:S(2)}, u32[]{:S(2)}) collective-permute-start(bf16[528,768]{1,0:T(8,128)(2,1)} %pad_maximum_fusion.1), channel_id=1, source_target_pairs={{0,32},{32,64},{64,96},{96,0},{1,33},{33,65},{65,97},{97,1},{2,34}... | collective-permute-start | bytes 2433032 | tf_op jit(solution)/shard_map/ppermute | solution.py:34
  15.0 17.2 %copy-start.13 = (f32[1,512]{1,0:T(1,128)S(1)}, f32[1,512]{1,0:T(1,128)}, u32[]{:S(2)}) copy-start(f32[1,512]{1,0:T(1,128)} %lse_i.3) | copy-start | bytes 6148
  27.4 22.2 %collective-permute-start.4 = (bf16[272,768]{1,0:T(8,128)(2,1)S(1)}, bf16[272,768]{1,0:T(8,128)(2,1)S(1)}, u32[]{:S(2)}, u32[]{:S(2)}) collective-permute-start(bf16[272,768]{1,0:T(8,128)(2,1)S(1)} %slice.17), channel_id=1, source_target_pairs={{0,96},{32,0},{64,32},{96,64},{1,97},{33,1},{65,33},{97,65},{2,98}... | collective-permute-start | bytes 1253384 | tf_op jit(solution)/shard_map/ppermute | solution.py:34
  31.9 17.7 %collective-permute-start.2 = (bf16[256,768]{1,0:T(8,128)(2,1)S(1)}, bf16[256,768]{1,0:T(8,128)(2,1)S(1)}, u32[]{:S(2)}, u32[]{:S(2)}) collective-permute-start(bf16[256,768]{1,0:T(8,128)(2,1)S(1)} %slice.16), channel_id=1, source_target_pairs={{0,32},{32,64},{64,96},{96,0},{1,33},{33,65},{65,97},{97,1},{2,34}... | collective-permute-start | bytes 1179656 | tf_op jit(solution)/shard_map/ppermute | solution.py:34
  60.3 8.4 %copy-start.14 = (bf16[512,768]{1,0:T(8,128)(2,1)}, bf16[512,768]{1,0:T(8,128)(2,1)S(1)}, u32[]{:S(2)}) copy-start(bf16[512,768]{1,0:T(8,128)(2,1)S(1)} %get-tuple-element.44) | copy-start | bytes 2359300
  60.3 5.2 %collective-permute-start.5 = (bf16[896,768]{1,0:T(8,128)(2,1)}, bf16[896,768]{1,0:T(8,128)(2,1)S(1)}, u32[]{:S(2)}, u32[]{:S(2)}) collective-permute-start(bf16[896,768]{1,0:T(8,128)(2,1)} %get-tuple-element.41), channel_id=1, source_target_pairs={{0,1},{1,0},{2,3},{3,2},{4,5},{5,4},{6,7},{7,6},{8,9},{9,8},{10,11... | collective-permute-start | bytes 4128776 | tf_op jit(solution)/shard_map/ppermute | solution.py:34
  68.7 27.5 %all-to-all-start = ((bf16[16,56,768]{2,1,0:T(8,128)(2,1)}), bf16[16,56,768]{2,1,0:T(8,128)(2,1)}, u32[]{:S(2)}, u32[]{:S(2)}) async-start(bf16[16,56,768]{2,1,0:T(8,128)(2,1)} %bitcast.3), calls=%async_computation | async-start | bytes 2752512 | tf_op jit(solution)/shard_map/all_to_all | solution.py:387
  76.1 33.6 %collective-permute-start.6 = (bf16[768,768]{1,0:T(8,128)(2,1)}, bf16[768,768]{1,0:T(8,128)(2,1)S(1)}, u32[]{:S(2)}, u32[]{:S(2)}) collective-permute-start(bf16[768,768]{1,0:T(8,128)(2,1)} %get-tuple-element.42), channel_id=1, source_target_pairs={{0,32},{32,64},{64,96},{96,0},{1,33},{33,65},{65,97},{97,1},{2,34}... | collective-permute-start | bytes 3538952 | tf_op jit(solution)/shard_map/ppermute | solution.py:34
  76.1 33.5 %collective-permute-start.7 = (bf16[768,768]{1,0:T(8,128)(2,1)}, bf16[768,768]{1,0:T(8,128)(2,1)S(1)}, u32[]{:S(2)}, u32[]{:S(2)}) collective-permute-start(bf16[768,768]{1,0:T(8,128)(2,1)} %get-tuple-element.43), channel_id=1, source_target_pairs={{0,96},{32,0},{64,32},{96,64},{1,97},{33,1},{65,33},{97,65},{2,98}... | collective-permute-start | bytes 3538952 | tf_op jit(solution)/shard_map/ppermute | solution.py:34
  79.1 30.6 %collective-permute-start.8 = (bf16[512,768]{1,0:T(8,128)(2,1)}, bf16[512,768]{1,0:T(8,128)(2,1)S(1)}, u32[]{:S(2)}, u32[]{:S(2)}) collective-permute-start(bf16[512,768]{1,0:T(8,128)(2,1)} %copy-done.14), channel_id=1, source_target_pairs={{0,16},{16,0},{1,17},{17,1},{2,18},{18,2},{3,19},{19,3},{4,20},{20... | collective-permute-start | bytes 2359304 | tf_op jit(solution)/shard_map/ppermute | solution.py:34
  109.7 9.7 %copy-start = (bf16[768,768]{1,0:T(8,128)(2,1)}, bf16[768,768]{1,0:T(8,128)(2,1)S(1)}, u32[]{:S(2)}) copy-start(bf16[768,768]{1,0:T(8,128)(2,1)S(1)} %collective-permute-done.7.rest_1_) | copy-start | bytes 3538948
  109.7 4.5 %collective-permute-start.11 = (bf16[56,768]{1,0:T(8,128)(2,1)S(1)}, bf16[56,768]{1,0:T(8,128)(2,1)S(1)}, u32[]{:S(2)}, u32[]{:S(2)}) collective-permute-start(bf16[56,768]{1,0:T(8,128)(2,1)S(1)} %reduce_sum.12), channel_id=1, source_target_pairs={{0,96},{32,0},{64,32},{96,64},{1,97},{33,1},{65,33},{97,65},{2,98}... | collective-permute-start | bytes 258056 | tf_op jit(solution)/shard_map/ppermute | solution.py:34
  112.7 5.4 %collective-permute-start.10 = (bf16[56,768]{1,0:T(8,128)(2,1)S(1)}, bf16[56,768]{1,0:T(8,128)(2,1)S(1)}, u32[]{:S(2)}, u32[]{:S(2)}) collective-permute-start(bf16[56,768]{1,0:T(8,128)(2,1)S(1)} %reduce_sum.12), channel_id=1, source_target_pairs={{0,32},{32,64},{64,96},{96,0},{1,33},{33,65},{65,97},{97,1},{2,34}... | collective-permute-start | bytes 258056 | tf_op jit(solution)/shard_map/ppermute | solution.py:34
  112.7 5.5 %collective-permute-start.9 = (bf16[56,768]{1,0:T(8,128)(2,1)S(1)}, bf16[56,768]{1,0:T(8,128)(2,1)S(1)}, u32[]{:S(2)}, u32[]{:S(2)}) collective-permute-start(bf16[56,768]{1,0:T(8,128)(2,1)S(1)} %reduce_sum.12), channel_id=1, source_target_pairs={{0,64},{32,96},{64,0},{96,32},{1,65},{33,97},{65,1},{97,33},{2,66}... | collective-permute-start | bytes 258056 | tf_op jit(solution)/shard_map/ppermute | solution.py:34
  119.4 25.7 %all-to-all-start.1 = ((bf16[16,56,768]{2,1,0:T(8,128)(2,1)}), bf16[16,56,768]{2,1,0:T(8,128)(2,1)S(1)}, u32[]{:S(2)}, u32[]{:S(2)}) async-start(bf16[16,56,768]{2,1,0:T(8,128)(2,1)} %broadcast_in_dim.12), calls=%async_computation.1 | async-start | bytes 2752512 | tf_op jit(solution)/shard_map/all_to_all | solution.py:395
  129.0 7.6 %collective-permute-start.13 = (bf16[256,768]{1,0:T(8,128)(2,1)S(1)}, bf16[256,768]{1,0:T(8,128)(2,1)S(1)}, u32[]{:S(2)}, u32[]{:S(2)}) collective-permute-start(bf16[256,768]{1,0:T(8,128)(2,1)S(1)} %slice.15), channel_id=1, source_target_pairs={{0,96},{32,0},{64,32},{96,64},{1,97},{33,1},{65,33},{97,65},{2,98}... | collective-permute-start | bytes 1179656 | tf_op jit(solution)/shard_map/ppermute | solution.py:34
  131.0 8.1 %collective-permute-start.12 = (bf16[256,768]{1,0:T(8,128)(2,1)S(1)}, bf16[256,768]{1,0:T(8,128)(2,1)S(1)}, u32[]{:S(2)}, u32[]{:S(2)}) collective-permute-start(bf16[256,768]{1,0:T(8,128)(2,1)S(1)} %slice.14), channel_id=1, source_target_pairs={{0,32},{32,64},{64,96},{96,0},{1,33},{33,65},{65,97},{97,1},{2,34}... | collective-permute-start | bytes 1179656 | tf_op jit(solution)/shard_map/ppermute | solution.py:34
  133.9 5.3 %copy-start.9 = (bf16[768,768]{1,0:T(8,128)(2,1)S(1)}, bf16[768,768]{1,0:T(8,128)(2,1)}, u32[]{:S(2)}) copy-start(bf16[768,768]{1,0:T(8,128)(2,1)} %head.2) | copy-start | bytes 3538948
  145.0 6.5 %collective-permute-start.14 = (bf16[896,768]{1,0:T(8,128)(2,1)S(1)}, bf16[896,768]{1,0:T(8,128)(2,1)S(1)}, u32[]{:S(2)}, u32[]{:S(2)}) collective-permute-start(bf16[896,768]{1,0:T(8,128)(2,1)S(1)} %bitcast.7), channel_id=1, source_target_pairs={{0,1},{1,0},{2,3},{3,2},{4,5},{5,4},{6,7},{7,6},{8,9},{9,8},{10,11... | collective-permute-start | bytes 4128776 | tf_op jit(solution)/shard_map/ppermute | solution.py:34
  (8 other events, 28.4 us)

commit v3 on v2

--- a/solution.py
+++ b/solution.py
@@ -64,6 +64,7 @@
 VMEM = pl.BlockSpec(memory_space=pltpu.VMEM)
 SMEM = pl.BlockSpec(memory_space=pltpu.SMEM)
 LIMIT = pltpu.CompilerParams(vmem_limit_bytes=48 * 1024 * 1024)
+MOST = pltpu.CompilerParams(vmem_limit_bytes=60 * 1024 * 1024)
 
 
 def wide(rows, columns=EMB):
@@ -84,6 +85,32 @@
         self.count += 1
         copy.start()
         return copy
+
+
+def pack_kernel(text, image, lse_t, lse_i, text_a, text_b, image_msg):
+    n = ROWS
+    text_a[...] = text[0:MID, :]
+    text_b[0 : n - MID, :] = text[MID:n, :]
+    row = lax.broadcasted_iota(jnp.int32, (PAD, n), 0)
+    high = lse_t[...].astype(bf16).astype(f32)
+    text_b[n - MID :, 0:n] = jnp.where(row == 0, high, lse_t[...] - high).astype(bf16)
+    text_b[n - MID :, n:TXT] = jnp.zeros((PAD, TXT - n), bf16)
+    image_msg[0:n, :] = image[...]
+    high = lse_i[...].astype(bf16).astype(f32)
+    image_msg[n:, 0:n] = jnp.broadcast_to(high, (PAD, n)).astype(bf16)
+    image_msg[n:, n : 2 * n] = jnp.broadcast_to(lse_i[...] - high, (PAD, n)).astype(bf16)
+
+
+def pack_call(text, image, lse_t, lse_i):
+    return pl.pallas_call(
+        pack_kernel,
+        out_shape=(narrow(MID, TXT), narrow(ROWS - MID + PAD, TXT), narrow(ROWS + PAD, VIS)),
+        in_specs=[VMEM] * 4,
+        out_specs=(VMEM,) * 3,
+        compiler_params=MOST,
+        cost_estimate=pl.CostEstimate(flops=10**5, bytes_accessed=4 * 10**6, transcendentals=0),
+        name="pack",
+    )(text, image, lse_t, lse_i)
 
 
 def own_kernel(image, text, hi, ht, zi, ri, zt, rt):
@@ -100,7 +127,7 @@
         out_shape=(wide(ROWS), narrow(ROWS), wide(ROWS), narrow(ROWS)),
         in_specs=[VMEM] * 4,
         out_specs=(VMEM,) * 4,
-        compiler_params=LIMIT,
+        compiler_params=MOST,
         cost_estimate=pl.CostEstimate(flops=14 * 10**8, bytes_accessed=10**7, transcendentals=0),
         name="own",
     )(image, text, hi, ht)
@@ -129,7 +156,7 @@
         w[r : r + CH, column : column + ROWS] = (jnp.exp2(s * exp2_scale) * both).astype(bf16)
 
 
-def first_kernel(i1, t0, t1, t2, ri0, rt0, zt0, lse_i, lse_t, hi, ht,
+def first_kernel(i1, t0, t1a, t1b, t2a, t2b, ri0, rt0, zt0, lse_i, lse_t, hi, ht,
                  tbase, p1, p2, ri1, zi1, ig, wt,
                  ri, ea, t, rt, zt, w, pre, image, head_i, head_t, itail, ttail, zout, bout, pout, iout, wout, sems):
     io = Copies(sems)
@@ -140,12 +167,15 @@
     c_rt0 = io.start(rt0, rt.at[pl.ds(0, n)])
     c_ri0 = io.start(ri0, ri.at[pl.ds(0, n)])
     c_zt0 = io.start(zt0, zt.at[pl.ds(0, n)])
-    c_t = [io.start(t0, t.at[pl.ds(0, n)])]
+    c_t = [[io.start(t0, t.at[pl.ds(0, n)])]]
     c_ht = io.start(ht, head_t)
     c_tail = []
-    for b, ref in ((1, t1), (2, t2)):
-        c_t.append(io.start(ref.at[pl.ds(0, n)], t.at[pl.ds(b * n, n)]))
-        c_tail.append(io.start(ref.at[pl.ds(n, PAD)], ttail.at[b - 1]))
+    for b, top, low in ((1, t1a, t1b), (2, t2a, t2b)):
+        c_t.append([
+            io.start(top, t.at[pl.ds(b * n, MID)]),
+            io.start(low.at[pl.ds(0, n - MID)], t.at[pl.ds(b * n + MID, n - MID)]),
+        ])
+        c_tail.append(io.start(low.at[pl.ds(n - MID, PAD)], ttail.at[b - 1]))
     outs = []
 
     c_image.wait()
@@ -163,7 +193,8 @@
     c_ri0.wait()
     for b in range(3):
         at = b * n
-        c_t[b].wait()
+        for copy in c_t[b]:
+            copy.wait()
         if b == 0:
             c_zt0.wait()
             lse_row = lse_t[...]
@@ -199,12 +230,12 @@
         copy.wait()
 
 
-def first_call(i1, t0, t1, t2, ri0, rt0, zt0, lse_i, lse_t, hi, ht):
+def first_call(i1, t0, t1a, t1b, t2a, t2b, ri0, rt0, zt0, lse_i, lse_t, hi, ht):
     n = ROWS
     return pl.pallas_call(
         first_kernel,
         out_shape=(wide(n), narrow(n), narrow(n), narrow(n), wide(n), wide(2 * n), wide(TXT)),
-        in_specs=[ANY] * 7 + [VMEM] * 2 + [ANY] * 2,
+        in_specs=[ANY] * 9 + [VMEM] * 2 + [ANY] * 2,
         out_specs=(ANY,) * 7,
         scratch_shapes=[
             pltpu.VMEM((2 * n, EMB), bf16),
@@ -226,28 +257,29 @@
             pltpu.VMEM((TXT, EMB), f32),
             pltpu.SemaphoreType.DMA((24,)),
         ],
-        compiler_params=LIMIT,
+        compiler_params=pltpu.CompilerParams(vmem_limit_bytes=48 * 1024 * 1024),
         cost_estimate=pl.CostEstimate(flops=12 * 10**9, bytes_accessed=20 * 10**6, transcendentals=2 * 10**6),
         name="first",
-    )(i1, t0, t1, t2, ri0, rt0, zt0, lse_i, lse_t, hi, ht)
+    )(i1, t0, t1a, t1b, t2a, t2b, ri0, rt0, zt0, lse_i, lse_t, hi, ht)
 
 
 def second_kernel(core, i0, i1, t3a, t3b, p1, p2, ri0, ri1, zi0, zi1, ig, wt, lse_i, ht,
                   up, down, ipart, ibase, send, keep,
                   ri, ea, t, rt, zt, w, pre, prei, image, head_t, itail, ttail, zi, gi, wsum,
-                  pout, qout, bout, sout, kout, sems):
+                  ubuf, dbuf, qout, bout, sout, kout, sems):
     io = Copies(sems)
     n = ROWS
     c_t = [io.start(t3a, t.at[pl.ds(0, MID)]), io.start(t3b.at[pl.ds(0, n - MID)], t.at[pl.ds(MID, n - MID)])]
     c_ht = io.start(ht, head_t)
+    c_itail = io.start(i1.at[pl.ds(n, PAD)], itail)
     c_ttail = io.start(t3b.at[pl.ds(n - MID, PAD)], ttail)
-    c_itail = io.start(i1.at[pl.ds(n, PAD)], itail)
     c_ri = [io.start(ri0, ri.at[pl.ds(0, n)]), io.start(ri1, ri.at[pl.ds(n, n)])]
     c_ig = io.start(ig, gi)
     c_zi = [io.start(zi0, zi.at[pl.ds(0, n)]), io.start(zi1, zi.at[pl.ds(n, n)])]
     c_image = [io.start(i0, image.at[pl.ds(0, n)]), io.start(i1.at[pl.ds(0, n)], image.at[pl.ds(n, n)])]
     c_wt = io.start(wt, wsum)
-    outs = [io.start(p2, up.at[pl.ds(0, n)]), io.start(p1, down.at[pl.ds(0, n)])]
+    c_p = [io.start(p2, ubuf.at[pl.ds(0, n)]), io.start(p1, dbuf.at[pl.ds(0, n)])]
+    outs = []
 
     c_itail.wait()
     ea[0:n, :] = column_weights(lse_i[...])
@@ -265,10 +297,12 @@
     fill_weights(ri, rt[...], ea, text_tail(ttail), w, 0)
     for c in CHUNKS:
         g = tn(w[:, c : c + CH], ri[...])
-        pout[c : c + CH, :] = g.astype(bf16)
+        (ubuf, dbuf)[c // MID][n : n + MID, :] = g.astype(bf16)
         pre[c : c + CH, :] = pre_gradient(zt[c : c + CH, :], logit_scale * g)
-    outs.append(io.start(pout.at[pl.ds(0, MID)], up.at[pl.ds(n, MID)]))
-    outs.append(io.start(pout.at[pl.ds(MID, n - MID)], down.at[pl.ds(n, n - MID)]))
+    for copy in c_p:
+        copy.wait()
+    outs.append(io.start(ubuf, up))
+    outs.append(io.start(dbuf, down))
     c_ig.wait()
     for copy in c_zi:
         copy.wait()
@@ -301,7 +335,7 @@
     n = ROWS
     return pl.pallas_call(
         second_kernel,
-        out_shape=(narrow(n + MID), narrow(n + MID), narrow(n), wide(n), narrow(HALF), wide(HALF)),
+        out_shape=(narrow(n + MID), narrow(n + MID), narrow(n), wide(n), narrow(HALF), narrow(HALF)),
         in_specs=[SMEM] + [ANY] * 12 + [VMEM] + [ANY],
         out_specs=(ANY,) * 6,
         scratch_shapes=[
@@ -320,14 +354,15 @@
             pltpu.VMEM((2 * n, EMB), f32),
             pltpu.VMEM((2 * n, EMB), f32),
             pltpu.VMEM((TXT, EMB), f32),
-            pltpu.VMEM((n, EMB), bf16),
+            pltpu.VMEM((n + MID, EMB), bf16),
+            pltpu.VMEM((n + MID, EMB), bf16),
             pltpu.VMEM((n, EMB), bf16),
             pltpu.VMEM((n, EMB), f32),
             pltpu.VMEM((HALF, EMB), bf16),
-            pltpu.VMEM((HALF, EMB), f32),
+            pltpu.VMEM((HALF, EMB), bf16),
             pltpu.SemaphoreType.DMA((24,)),
         ],
-        compiler_params=LIMIT,
+        compiler_params=pltpu.CompilerParams(vmem_limit_bytes=48 * 1024 * 1024),
         cost_estimate=pl.CostEstimate(flops=8 * 10**9, bytes_accessed=20 * 10**6, transcendentals=10**6),
         name="second",
     )(core, i0, i1, t3a, t3b, p1, p2, ri0, ri1, zi0, zi1, ig, wt, lse_i, ht)
@@ -357,42 +392,79 @@
     )(raw, head, base, *parts, *halves)
 
 
-def final_kernel(core, own, other, image, text):
-    mine = core[0]
-    for ref, which in ((own, mine), (other, 1 - mine)):
-        image[pl.ds(pl.multiple_of(which * HV, 128), HV), :] = ref[0:HV, :].astype(f32)
-        text[pl.ds(pl.multiple_of(which * HT, 128), HT), :] = ref[HV:HALF, :].astype(f32)
-
-
-def final_call(core, own, other):
-    return pl.pallas_call(
-        final_kernel,
-        out_shape=(jax.ShapeDtypeStruct((VIS, EMB), f32), jax.ShapeDtypeStruct((TXT, EMB), f32)),
-        in_specs=[SMEM, VMEM, VMEM],
-        out_specs=(VMEM, VMEM),
-        compiler_params=pltpu.CompilerParams(vmem_limit_bytes=40 * 1024 * 1024),
+def final_kernel(first, core, half, *rest):
+    image, text, buf, sems = rest[-4:]
+    io = Copies(sems)
+    which = core[0] if first else 1 - core[0]
+    buf[...] = half[...].astype(f32)
+    copies = [
+        io.start(buf.at[pl.ds(0, HV)], image.at[pl.ds(pl.multiple_of(which * HV, 128), HV)]),
+        io.start(buf.at[pl.ds(HV, HT)], text.at[pl.ds(pl.multiple_of(which * HT, 128), HT)]),
+    ]
+    for copy in copies:
+        copy.wait()
+
+
+def final_call(core, half, *written):
+    return pl.pallas_call(
+        functools.partial(final_kernel, len(written) == 0),
+        out_shape=(wide(VIS), wide(TXT)),
+        in_specs=[SMEM, VMEM] + [ANY] * len(written),
+        out_specs=(ANY, ANY),
+        scratch_shapes=[pltpu.VMEM((HALF, EMB), f32), pltpu.SemaphoreType.DMA((2,))],
+        input_output_aliases={2: 0, 3: 1} if written else {},
+        compiler_params=pltpu.CompilerParams(vmem_limit_bytes=32 * 1024 * 1024),
+        cost_estimate=pl.CostEstimate(flops=10**6, bytes_accessed=4 * 10**6, transcendentals=0),
         name="final",
-    )(core, own, other)
-
-
-def split_lse(lse):
-    high = lse.astype(bf16)
-    low = (lse - high.astype(f32)).astype(bf16)
-    return high, low
+    )(core, half, *written)
+
+
+def merge_kernel(a, b, out):
+    for r in range(0, HALF, 128):
+        out[r : r + 128, :] = (a[r : r + 128, :].astype(f32) + b[r : r + 128, :].astype(f32)).astype(bf16)
+
+
+def merge_call(a, b):
+    return pl.pallas_call(
+        merge_kernel,
+        out_shape=narrow(HALF),
+        in_specs=[VMEM] * 2,
+        out_specs=VMEM,
+        compiler_params=pltpu.CompilerParams(vmem_limit_bytes=32 * 1024 * 1024),
+        cost_estimate=pl.CostEstimate(flops=10**6, bytes_accessed=4 * 10**6, transcendentals=0),
+        name="merge",
+    )(a, b)
+
+
+def total_kernel(own, plus, minus, across, out):
+    total = (own[...].astype(f32) + across[...].astype(f32)) + (plus[...].astype(f32) + minus[...].astype(f32))
+    total = total.astype(bf16)
+    for k in range(16):
+        out[k] = total
+
+
+def total_call(*parts):
+    return pl.pallas_call(
+        total_kernel,
+        out_shape=jax.ShapeDtypeStruct((16, HALF // 16, EMB), bf16),
+        in_specs=[VMEM] * 4,
+        out_specs=VMEM,
+        compiler_params=pltpu.CompilerParams(vmem_limit_bytes=16 * 1024 * 1024),
+        cost_estimate=pl.CostEstimate(flops=10**6, bytes_accessed=2 * 10**6, transcendentals=0),
+        name="total",
+    )(*parts)
 
 
 def reduce_heads(send, keep):
-    part = keep + permute(send, "core", 2, 1).astype(f32)
-    part = part.astype(bf16).reshape(16, HALF // 16, EMB)
+    part = merge_call(keep, permute(send, "core", 2, 1)).reshape(16, HALF // 16, EMB)
     part = lax.all_to_all(part, PLANE, 0, 0, tiled=True)
     return jnp.sum(part.astype(f32), axis=0).astype(bf16)
 
 
-def spread_heads(part):
-    others = [permute(part, "y", 4, d).astype(f32) for d in (1, 3, 2)]
-    part = ((part.astype(f32) + others[2]) + (others[0] + others[1])).astype(bf16)
-    whole = jnp.broadcast_to(part[None], (16, HALF // 16, EMB))
-    return lax.all_to_all(whole, PLANE, 0, 0, tiled=True).reshape(HALF, EMB)
+def spread_heads(part, *beside):
+    whole = total_call(part, *[permute(part, "y", 4, d) for d in (1, 3, 2)])
+    whole, *beside = lax.optimization_barrier((whole, *beside))
+    return lax.all_to_all(whole, PLANE, 0, 0, tiled=True).reshape(HALF, EMB), *beside
 
 
 def shards(image_feats, text_feats, image_head, text_head, image_lse, text_lse):
@@ -400,36 +472,32 @@
     text_rows = text_feats[0]
     core = lax.axis_index("core").astype(jnp.int32).reshape(1)
 
-    high, low = split_lse(text_lse)
-    text_msg = jnp.concatenate(
-        [text_rows, jnp.pad(jnp.concatenate([high, low], axis=0), ((0, PAD - 2), (0, TXT - ROWS)))], axis=0
-    )
-    high, low = split_lse(image_lse)
-    image_msg = jnp.concatenate(
-        [image_rows, jnp.pad(jnp.concatenate([high, low], axis=1), ((0, PAD - 1), (0, 0)))], axis=0
-    )
-    t1 = permute(text_msg, "y", 4, 1)
-    t2 = permute(text_msg, "y", 4, 3)
+    text_a, text_b, image_msg = pack_call(text_rows, image_rows, text_lse, image_lse)
+    t1a = permute(text_a, "y", 4, 1)
+    t2b = permute(text_b, "y", 4, 3)
+    t1b = permute(text_b, "y", 4, 1)
+    t2a = permute(text_a, "y", 4, 3)
     i1 = permute(image_msg, "xl", 2, 1)
     zi0, ri0, zt0, rt0 = own_call(image_rows, text_rows, image_head, text_head)
-    t3a = permute(t1[:MID], "y", 4, 1)
-    t3b = permute(t2[MID:], "y", 4, 3)
+    t1a, t2b, zi0, ri0, zt0, rt0 = lax.optimization_barrier((t1a, t2b, zi0, ri0, zt0, rt0))
+    t3a = permute(t1a, "y", 4, 1)
+    t3b = permute(t2b, "y", 4, 3)
 
     tbase, p1, p2, ri1, zi1, ig, wt = first_call(
-        i1, text_rows, t1, t2, ri0, rt0, zt0, image_lse, text_lse, image_head, text_head
+        i1, text_rows, t1a, t1b, t2a, t2b, ri0, rt0, zt0, image_lse, text_lse, image_head, text_head
     )
     up, down, ipart, ibase, send, keep = second_call(
         core, image_rows, i1, t3a, t3b, p1, p2, ri0, ri1, zi0, zi1, ig, wt, image_lse, text_head
     )
     part = reduce_heads(send, keep)
     up, down, ipart = permute(up, "y", 4, 1), permute(down, "y", 4, 3), permute(ipart, "xl", 2, 1)
-    part, up, down, ipart = lax.optimization_barrier((part, up, down, ipart))
-    whole = spread_heads(part)
+    whole, up, down, ipart = spread_heads(part, up, down, ipart)
     top, bottom = permute(up[ROWS:], "y", 4, 1), permute(down[ROWS:], "y", 4, 3)
     text_back = back_call(zt0, text_head, tbase, [up, down], [top, bottom])
     image_back = back_call(zi0, image_head, ibase, [ipart])
     whole, text_back, image_back = lax.optimization_barrier((whole, text_back, image_back))
-    image_total, text_total = final_call(core, whole, permute(whole, "core", 2, 1))
+    other = permute(whole, "core", 2, 1)
+    image_total, text_total = final_call(core, other, *final_call(core, whole))
     return (image_back[None], text_back[None], image_total, text_total)
 
 

time: 155 us -> 146 us (0.942)
  waiting for transfers between devices: 55.1 us -> 46.7 us
  other arithmetic: 8.95 us -> 1.53 us
  Pallas kernels: 40.1 us -> 47.1 us
    ppermute x15 -> x17, waiting for transfers between devices: 35.9 us -> 25.7 us  [permute(): lax.ppermute(value, axis, [(i, (i + shift) % size) for i in range(size)])]
    pallas_call x1 -> x5, Pallas kernels: 2.72 us -> 8.76 us  [the longest x2 3.45 us: final_call(): pl.pallas_call(functools.partial(final_kernel, len(written) == 0), out_sh...]
    convert_element_type x4 -> x0, other arithmetic: 4.03 us -> none  [the longest x1 3.2 us: reduce_heads(): part = part.astype(bf16).reshape(16, HALF // 16, EMB)]
    concatenate x4 -> x0, other arithmetic: 3.39 us -> none  [the longest x1 2.43 us: shards(): jnp.concatenate([image_rows, jnp.pad(jnp.concatenate([high, low], axis=1)...]
    unnamed x30 -> x32, local copies, waits for them, and re-layouts: 4.01 us -> 7.31 us
    slice x2 -> x0, local copies, waits for them, and re-layouts: 2.05 us -> none  [the longest x1 1.03 us: shards(): t3b = permute(t2[MID:], 'y', 4, 3)]
    ppermute x15 -> x17, starting transfers between devices: 25 us -> 25.4 us  [permute(): lax.ppermute(value, axis, [(i, (i + shift) % size) for i in range(size)])]
  transfers between devices with their start and end apart: 17 -> 19, of which waited for: 9 -> 10; matrix products, arithmetic and copies ran while one was open for 4% -> 2% of each run, Pallas kernels for 17% -> 21%
where the time goes in v3:
time: 146 us; the launch traced here: 145 us
  Pallas kernels  47.1 us (32%)
  waiting for transfers between devices  46.7 us (32%)
  starting transfers between devices  40.2 us (28%)
  local copies, waits for them, and re-layouts  8.47 us (6%)
  other arithmetic  1.53 us (1%)
    ppermute x17, waiting for transfers between devices, permute(): lax.ppermute(value, axis, [(i, (i + shift) % size) for i in range(size)])  25.7 us
    ppermute x17, starting transfers between devices, permute(): lax.ppermute(value, axis, [(i, (i + shift) % size) for i in range(size)])  25.4 us
    pallas_call x1, Pallas kernels, first_call(): pl.pallas_call(first_kernel, out_shape=(wide(n), narrow(n), narrow(n), na...  17.4 us
    all_to_all x1, waiting for transfers between devices, reduce_heads(): part = lax.all_to_all(part, PLANE, 0, 0, tiled=True)  16.2 us
    pallas_call x1, Pallas kernels, second_call(): pl.pallas_call(second_kernel, out_shape=(narrow(n + MID), narrow(n + MID)...  10.3 us
    all_to_all x1, starting transfers between devices, spread_heads(): lax.all_to_all(whole, PLANE, 0, 0, tiled=True).reshape(HALF, EMB)  7.45 us
    all_to_all x1, starting transfers between devices, reduce_heads(): part = lax.all_to_all(part, PLANE, 0, 0, tiled=True)  7.35 us
    unnamed x32, local copies, waits for them, and re-layouts  7.31 us
  transfers between devices with their start and end apart: 19, of which 10 were waited for; matrix products, arithmetic and copies ran while one was open for 2% of the time, Pallas kernels for 21%

profile of v3, /device:TPU:1, one launch (start us, length us, event | category | flops | bytes accessed | tf_op | source)
XLA Modules:
  0.0 145.1 jit_solution(6210610306686825720)
XLA Ops:
  0.6 2.7 %pack.1 = (bf16[256,768]{1,0:T(8,128)(2,1)}, bf16[272,768]{1,0:T(8,128)(2,1)}, bf16[528,1024]{1,0:T(8,128)(2,1)}) custom-call(bf16[512,768]{1,0:T(8,128)(2,1)} %bitcast.12, bf16[512,1024]{1,0:T(8,128)(2,1)} %bitcast.9, f32[1,512]{1,0:T(1,128)} %lse_t.3, f32[1,512]{1,0:T(1,128)} %lse_i.5), custom_call_target="tpu_custom_call" | custom-call | flops 100000 | bytes 4000000 | tf_op jit(solution)/shard_map/pack/pallas_call | solution.py:105
  3.4 2.0 %collective-permute-start = (bf16[528,1024]{1,0:T(8,128)(2,1)}, bf16[528,1024]{1,0:T(8,128)(2,1)S(1)}, u32[]{:S(2)}, u32[]{:S(2)}) collective-permute-start(bf16[528,1024]{1,0:T(8,128)(2,1)} %get-tuple-element.41), channel_id=1, source_target_pairs={{0,16},{16,0},{1,17},{17,1},{2,18},{18,2},{3,19},{19,3},{4,20},{20... | collective-permute-start | bytes 3244040 | tf_op jit(solution)/shard_map/ppermute | solution.py:34
  5.4 2.7 %collective-permute-start.2 = (bf16[272,768]{1,0:T(8,128)(2,1)}, bf16[272,768]{1,0:T(8,128)(2,1)S(1)}, u32[]{:S(2)}, u32[]{:S(2)}) collective-permute-start(bf16[272,768]{1,0:T(8,128)(2,1)} %get-tuple-element.43), channel_id=1, source_target_pairs={{0,96},{32,0},{64,32},{96,64},{1,97},{33,1},{65,33},{97,65},{2,98}... | collective-permute-start | bytes 1253384 | tf_op jit(solution)/shard_map/ppermute | solution.py:34
  8.2 2.7 %collective-permute-start.6 = (bf16[256,768]{1,0:T(8,128)(2,1)}, bf16[256,768]{1,0:T(8,128)(2,1)S(1)}, u32[]{:S(2)}, u32[]{:S(2)}) collective-permute-start(bf16[256,768]{1,0:T(8,128)(2,1)} %get-tuple-element.42), channel_id=1, source_target_pairs={{0,96},{32,0},{64,32},{96,64},{1,97},{33,1},{65,33},{97,65},{2,98}... | collective-permute-start | bytes 1179656 | tf_op jit(solution)/shard_map/ppermute | solution.py:34
  10.9 5.5 %own.1 = (f32[512,768]{1,0:T(8,128)}, bf16[512,768]{1,0:T(8,128)(2,1)}, f32[512,768]{1,0:T(8,128)}, bf16[512,768]{1,0:T(8,128)(2,1)}) custom-call(bf16[512,1024]{1,0:T(8,128)(2,1)} %bitcast.10, bf16[512,768]{1,0:T(8,128)(2,1)} %bitcast.13, bf16[1024,768]{1,0:T(8,128)(2,1)} %head.3, bf16[768,768]{1,0:T(8,128)(2,1)} %head.2), custom_call_target="tpu_custom_call" | custom-call | flops 1400000000 | bytes 10000000 | tf_op jit(solution)/shard_map/own/pallas_call | solution.py:125
  16.4 11.5 %collective-permute-done.1.t1a = bf16[256,768]{1,0:T(8,128)(2,1)S(1)} collective-permute-done((bf16[256,768]{1,0:T(8,128)(2,1)}, bf16[256,768]{1,0:T(8,128)(2,1)S(1)}, u32[]{:S(2)}, u32[]{:S(2)}) %collective-permute-start.1) | collective-permute-done | bytes 393248 | tf_op jit(solution)/shard_map/ppermute | solution.py:34
  27.9 2.7 %collective-permute-start.4 = (bf16[272,768]{1,0:T(8,128)(2,1)S(1)}, bf16[272,768]{1,0:T(8,128)(2,1)S(1)}, u32[]{:S(2)}, u32[]{:S(2)}) collective-permute-start(bf16[272,768]{1,0:T(8,128)(2,1)S(1)} %collective-permute-done.2.t2b), channel_id=1, source_target_pairs={{0,96},{32,0},{64,32},{96,64},{1,97},{33,1},{65,33},{97,65},{2,98}... | collective-permute-start | bytes 1253384 | tf_op jit(solution)/shard_map/ppermute | solution.py:34
  32.7 17.4 %first.1 = (f32[512,768]{1,0:T(8,128)}, bf16[512,768]{1,0:T(8,128)(2,1)S(1)}, bf16[512,768]{1,0:T(8,128)(2,1)S(1)}, bf16[512,768]{1,0:T(8,128)(2,1)S(1)}, f32[51...) custom-call(bf16[528,1024]{1,0:T(8,128)(2,1)} %copy-done.15, bf16[512,768]{1,0:T(8,128)(2,1)S(1)} %bitcast.14, ...), custom_call_target="tpu_custom_call" | custom-call | flops 12000000000 | bytes 20000000 | tf_op jit(solution)/shard_map/first/pallas_call | solution.py:235
  50.1 10.3 %second.1 = (bf16[768,768]{1,0:T(8,128)(2,1)}, bf16[768,768]{1,0:T(8,128)(2,1)}, bf16[512,768]{1,0:T(8,128)(2,1)S(1)}, f32[512,768]{1,0:T(8,128)}, bf16[896,768]{1,0:T(8,128)(2,1)}, /*index=5*/bf16[896,768]{1,0:T(8,128)(2,1)}) custom-call(s32[1]{0:T(128)} %bitcast.core, bf16[512,1024]{1,0:T(8,128)(2,1)S(1)} %bitcast.11, bf16[528,1024]{1,0:T(8,128)(2,1)} %copy-done.15, ...), custom_call_target="tpu_custom_call" | custom-call | flops 8000000000 | bytes 20000000 | tf_op jit(solution)/shard_map/second/pallas_call | solution.py:336
  60.5 2.8 %collective-permute-start.7 = (bf16[896,768]{1,0:T(8,128)(2,1)}, bf16[896,768]{1,0:T(8,128)(2,1)S(1)}, u32[]{:S(2)}, u32[]{:S(2)}) collective-permute-start(bf16[896,768]{1,0:T(8,128)(2,1)} %get-tuple-element.61), channel_id=1, source_target_pairs={{0,1},{1,0},{2,3},{3,2},{4,5},{5,4},{6,7},{7,6},{8,9},{9,8},{10,11... | collective-permute-start | bytes 4128776 | tf_op jit(solution)/shard_map/ppermute | solution.py:34
  63.3 3.0 %collective-permute-done.7.b = bf16[896,768]{1,0:T(8,128)(2,1)S(1)} collective-permute-done((bf16[896,768]{1,0:T(8,128)(2,1)}, bf16[896,768]{1,0:T(8,128)(2,1)S(1)}, u32[]{:S(2)}, u32[]{:S(2)}) %collective-permute-start.7) | collective-permute-done | bytes 1376288 | tf_op jit(solution)/shard_map/ppermute | solution.py:34
  69.0 7.3 %all-to-all-start = ((bf16[16,56,768]{2,1,0:T(8,128)(2,1)}), bf16[16,56,768]{2,1,0:T(8,128)(2,1)}, u32[]{:S(2)}, u32[]{:S(2)}) async-start(bf16[16,56,768]{2,1,0:T(8,128)(2,1)} %bitcast.3), calls=%async_computation | async-start | bytes 2752512 | tf_op jit(solution)/shard_map/all_to_all | solution.py:460
  76.4 2.7 %collective-permute-start.12 = (bf16[768,768]{1,0:T(8,128)(2,1)}, bf16[768,768]{1,0:T(8,128)(2,1)S(1)}, u32[]{:S(2)}, u32[]{:S(2)}) collective-permute-start(bf16[768,768]{1,0:T(8,128)(2,1)} %get-tuple-element.63), channel_id=1, source_target_pairs={{0,96},{32,0},{64,32},{96,64},{1,97},{33,1},{65,33},{97,65},{2,98}... | collective-permute-start | bytes 3538952 | tf_op jit(solution)/shard_map/ppermute | solution.py:34
  80.3 16.2 %all-to-all-done = bf16[16,56,768]{2,1,0:T(8,128)(2,1)} async-done(((bf16[16,56,768]{2,1,0:T(8,128)(2,1)}), bf16[16,56,768]{2,1,0:T(8,128)(2,1)}, u32[]{:S(2)}, u32[]{:S(2)}) %all-to-all-start) | async-done | bytes 1376288 | tf_op jit(solution)/shard_map/all_to_all | solution.py:460
  99.4 5.7 %collective-permute-done.10.across = bf16[56,768]{1,0:T(8,128)(2,1)S(1)} collective-permute-done((bf16[56,768]{1,0:T(8,128)(2,1)S(1)}, bf16[56,768]{1,0:T(8,128)(2,1)S(1)}, u32[]{:S(2)}, u32[]{:S(2)}) %collective-permute-start.10) | collective-permute-done | bytes 86048 | tf_op jit(solution)/shard_map/ppermute | solution.py:34
  105.1 1.7 %collective-permute-start.8 = (bf16[56,768]{1,0:T(8,128)(2,1)S(1)}, bf16[56,768]{1,0:T(8,128)(2,1)S(1)}, u32[]{:S(2)}, u32[]{:S(2)}) collective-permute-start(bf16[56,768]{1,0:T(8,128)(2,1)S(1)} %reduce_sum.12.own), channel_id=1, source_target_pairs={{0,32},{32,64},{64,96},{96,0},{1,33},{33,65},{65,97},{97,1},{2,34}... | collective-permute-start | bytes 258056 | tf_op jit(solution)/shard_map/ppermute | solution.py:34
  107.2 2.5 %collective-permute-done.8.plus = bf16[56,768]{1,0:T(8,128)(2,1)S(1)} collective-permute-done((bf16[56,768]{1,0:T(8,128)(2,1)S(1)}, bf16[56,768]{1,0:T(8,128)(2,1)S(1)}, u32[]{:S(2)}, u32[]{:S(2)}) %collective-permute-start.8) | collective-permute-done | bytes 86048 | tf_op jit(solution)/shard_map/ppermute | solution.py:34
  111.9 7.5 %all-to-all-start.1 = ((bf16[16,56,768]{2,1,0:T(8,128)(2,1)}), bf16[16,56,768]{2,1,0:T(8,128)(2,1)S(1)}, u32[]{:S(2)}, u32[]{:S(2)}) async-start(bf16[16,56,768]{2,1,0:T(8,128)(2,1)} %total.1), calls=%async_computation.1 | async-start | bytes 2752512 | tf_op jit(solution)/shard_map/all_to_all | solution.py:467
  124.9 2.6 %back.3 = f32[512,1024]{1,0:T(8,128)} custom-call(f32[512,768]{1,0:T(8,128)S(1)} %copy-done.4, bf16[1024,768]{1,0:T(8,128)(2,1)S(1)} %copy-done.2, f32[512,768]{1,0:T(8,128)S(1)} %copy-done.6, bf16[512,768]{1,0:T(8,128)(2,1)S(1)} %collective-permute-done.13.rest_0_), custom_call_target="tpu_custom_call" | custom-call | flops 805306368 | bytes 10000000 | tf_op jit(solution)/shard_map/back/pallas_call | solution.py:384
  129.2 2.5 %back.2 = f32[512,768]{1,0:T(8,128)} custom-call(f32[512,768]{1,0:T(8,128)S(1)} %copy-done.3, bf16[768,768]{1,0:T(8,128)(2,1)S(1)} %copy-done.8, f32[512,768]{1,0:T(8,128)S(1)} %copy-done.5, bf16[768,768]{1,0:T(8,128)(2,1)S(1)} %collective-permute-done.11.rest_0_, bf16[768,768]{1,0:T(8,128)(2,1)S(1)} %copy-done.1, ...), custom_call_target="tpu_custom_call" | custom-call | flops 603979776 | bytes 10000000 | tf_op jit(solution)/shard_map/back/pallas_call | solution.py:384
  131.7 4.8 %all-to-all-done.1 = bf16[16,56,768]{2,1,0:T(8,128)(2,1)S(1)} async-done(((bf16[16,56,768]{2,1,0:T(8,128)(2,1)}), bf16[16,56,768]{2,1,0:T(8,128)(2,1)S(1)}, u32[]{:S(2)}, u32[]{:S(2)}) %all-to-all-start.1) | async-done | bytes 1376288 | tf_op jit(solution)/shard_map/all_to_all | solution.py:467
  136.5 3.9 %collective-permute-start.16 = (bf16[896,768]{1,0:T(8,128)(2,1)S(1)}, bf16[896,768]{1,0:T(8,128)(2,1)S(1)}, u32[]{:S(2)}, u32[]{:S(2)}) collective-permute-start(bf16[896,768]{1,0:T(8,128)(2,1)S(1)} %bitcast.7), channel_id=1, source_target_pairs={{0,1},{1,0},{2,3},{3,2},{4,5},{5,4},{6,7},{7,6},{8,9},{9,8},{10,11... | collective-permute-start | bytes 4128776 | tf_op jit(solution)/shard_map/ppermute | solution.py:34
  140.4 1.7 %final.2 = (f32[1024,768]{1,0:T(8,128)}, f32[768,768]{1,0:T(8,128)}) custom-call(s32[1]{0:T(128)} %bitcast.core, bf16[896,768]{1,0:T(8,128)(2,1)S(1)} %bitcast.8), custom_call_target="tpu_custom_call" | custom-call | flops 1000000 | bytes 4000000 | tf_op jit(solution)/shard_map/final/pallas_call | solution.py:409
  143.1 1.7 %final.3 = (f32[1024,768]{1,0:T(8,128)}, f32[768,768]{1,0:T(8,128)}) custom-call(s32[1]{0:T(128)} %bitcast.core, bf16[896,768]{1,0:T(8,128)(2,1)S(1)} %collective-permute-done.16.half, f32[1024,768]{1,0:T(8,128)} %get-tuple-element.74.rest_0_, f32[768,768]{1,0:T(8,128)} %get-tuple-element.75.rest_1_), custom_call_target="tpu_custom_call", output_to_operand_aliasing={{0}: (2, {}), {1}: (3, {})} | custom-call | flops 1000000 | bytes 4000000 | tf_op jit(solution)/shard_map/final/pallas_call | solution.py:409
  (59 shorter events, 20.0 us)
Async XLA Ops:
  3.4 27.2 %collective-permute-start = (bf16[528,1024]{1,0:T(8,128)(2,1)}, bf16[528,1024]{1,0:T(8,128)(2,1)S(1)}, u32[]{:S(2)}, u32[]{:S(2)}) collective-permute-start(bf16[528,1024]{1,0:T(8,128)(2,1)} %get-tuple-element.41), channel_id=1, source_target_pairs={{0,16},{16,0},{1,17},{17,1},{2,18},{18,2},{3,19},{19,3},{4,20},{20... | collective-permute-start | bytes 3244040 | tf_op jit(solution)/shard_map/ppermute | solution.py:34
  5.4 22.5 %collective-permute-start.2 = (bf16[272,768]{1,0:T(8,128)(2,1)}, bf16[272,768]{1,0:T(8,128)(2,1)S(1)}, u32[]{:S(2)}, u32[]{:S(2)}) collective-permute-start(bf16[272,768]{1,0:T(8,128)(2,1)} %get-tuple-element.43), channel_id=1, source_target_pairs={{0,96},{32,0},{64,32},{96,64},{1,97},{33,1},{65,33},{97,65},{2,98}... | collective-permute-start | bytes 1253384 | tf_op jit(solution)/shard_map/ppermute | solution.py:34
  8.2 22.4 %collective-permute-start.5 = (bf16[272,768]{1,0:T(8,128)(2,1)}, bf16[272,768]{1,0:T(8,128)(2,1)S(1)}, u32[]{:S(2)}, u32[]{:S(2)}) collective-permute-start(bf16[272,768]{1,0:T(8,128)(2,1)} %get-tuple-element.43), channel_id=1, source_target_pairs={{0,32},{32,64},{64,96},{96,0},{1,33},{33,65},{65,97},{97,1},{2,34}... | collective-permute-start | bytes 1253384 | tf_op jit(solution)/shard_map/ppermute | solution.py:34
  8.2 19.7 %collective-permute-start.1 = (bf16[256,768]{1,0:T(8,128)(2,1)}, bf16[256,768]{1,0:T(8,128)(2,1)S(1)}, u32[]{:S(2)}, u32[]{:S(2)}) collective-permute-start(bf16[256,768]{1,0:T(8,128)(2,1)} %get-tuple-element.42), channel_id=1, source_target_pairs={{0,32},{32,64},{64,96},{96,0},{1,33},{33,65},{65,97},{97,1},{2,34}... | collective-permute-start | bytes 1179656 | tf_op jit(solution)/shard_map/ppermute | solution.py:34
  8.2 22.4 %collective-permute-start.6 = (bf16[256,768]{1,0:T(8,128)(2,1)}, bf16[256,768]{1,0:T(8,128)(2,1)S(1)}, u32[]{:S(2)}, u32[]{:S(2)}) collective-permute-start(bf16[256,768]{1,0:T(8,128)(2,1)} %get-tuple-element.42), channel_id=1, source_target_pairs={{0,96},{32,0},{64,32},{96,64},{1,97},{33,1},{65,33},{97,65},{2,98}... | collective-permute-start | bytes 1179656 | tf_op jit(solution)/shard_map/ppermute | solution.py:34
  10.9 20.7 %copy-start.10 = (bf16[1,512,768]{2,1,0:T(8,128)(2,1)S(1)}, bf16[1,512,768]{2,1,0:T(8,128)(2,1)}, u32[]{:S(2)}) copy-start(bf16[1,512,768]{2,1,0:T(8,128)(2,1)} %param.7) | copy-start | bytes 2359300
  10.9 20.7 %copy-start.11 = (f32[1,512]{1,0:T(1,128)S(1)}, f32[1,512]{1,0:T(1,128)}, u32[]{:S(2)}) copy-start(f32[1,512]{1,0:T(1,128)} %lse_t.3) | copy-start | bytes 6148
  10.9 20.7 %copy-start.12 = (f32[1,512]{1,0:T(1,128)S(1)}, f32[1,512]{1,0:T(1,128)}, u32[]{:S(2)}) copy-start(f32[1,512]{1,0:T(1,128)} %lse_i.5) | copy-start | bytes 6148
  27.9 22.2 %copy-start.9 = (bf16[1,512,1024]{2,1,0:T(8,128)(2,1)S(1)}, bf16[1,512,1024]{2,1,0:T(8,128)(2,1)}, u32[]{:S(2)}) copy-start(bf16[1,512,1024]{2,1,0:T(8,128)(2,1)} %param.6) | copy-start | bytes 3145732
  27.9 22.2 %collective-permute-start.3 = (bf16[256,768]{1,0:T(8,128)(2,1)S(1)}, bf16[256,768]{1,0:T(8,128)(2,1)S(1)}, u32[]{:S(2)}, u32[]{:S(2)}) collective-permute-start(bf16[256,768]{1,0:T(8,128)(2,1)S(1)} %collective-permute-done.1.t1a), channel_id=1, source_target_pairs={{0,32},{32,64},{64,96},{96,0},{1,33},{33,65},{65,97},{97,1},{2,34}... | collective-permute-start | bytes 1179656 | tf_op jit(solution)/shard_map/ppermute | solution.py:34
  27.9 22.2 %collective-permute-start.4 = (bf16[272,768]{1,0:T(8,128)(2,1)S(1)}, bf16[272,768]{1,0:T(8,128)(2,1)S(1)}, u32[]{:S(2)}, u32[]{:S(2)}) collective-permute-start(bf16[272,768]{1,0:T(8,128)(2,1)S(1)} %collective-permute-done.2.t2b), channel_id=1, source_target_pairs={{0,96},{32,0},{64,32},{96,64},{1,97},{33,1},{65,33},{97,65},{2,98}... | collective-permute-start | bytes 1253384 | tf_op jit(solution)/shard_map/ppermute | solution.py:34
  60.5 8.5 %copy-start.13 = (bf16[512,768]{1,0:T(8,128)(2,1)}, bf16[512,768]{1,0:T(8,128)(2,1)S(1)}, u32[]{:S(2)}) copy-start(bf16[512,768]{1,0:T(8,128)(2,1)S(1)} %get-tuple-element.64) | copy-start | bytes 2359300
  60.5 5.7 %collective-permute-start.7 = (bf16[896,768]{1,0:T(8,128)(2,1)}, bf16[896,768]{1,0:T(8,128)(2,1)S(1)}, u32[]{:S(2)}, u32[]{:S(2)}) collective-permute-start(bf16[896,768]{1,0:T(8,128)(2,1)} %get-tuple-element.61), channel_id=1, source_target_pairs={{0,1},{1,0},{2,3},{3,2},{4,5},{5,4},{6,7},{7,6},{8,9},{9,8},{10,11... | collective-permute-start | bytes 4128776 | tf_op jit(solution)/shard_map/ppermute | solution.py:34
  69.0 27.5 %all-to-all-start = ((bf16[16,56,768]{2,1,0:T(8,128)(2,1)}), bf16[16,56,768]{2,1,0:T(8,128)(2,1)}, u32[]{:S(2)}, u32[]{:S(2)}) async-start(bf16[16,56,768]{2,1,0:T(8,128)(2,1)} %bitcast.3), calls=%async_computation | async-start | bytes 2752512 | tf_op jit(solution)/shard_map/all_to_all | solution.py:460
  76.3 34.5 %collective-permute-start.11 = (bf16[768,768]{1,0:T(8,128)(2,1)}, bf16[768,768]{1,0:T(8,128)(2,1)S(1)}, u32[]{:S(2)}, u32[]{:S(2)}) collective-permute-start(bf16[768,768]{1,0:T(8,128)(2,1)} %get-tuple-element.62), channel_id=1, source_target_pairs={{0,32},{32,64},{64,96},{96,0},{1,33},{33,65},{65,97},{97,1},{2,34}... | collective-permute-start | bytes 3538952 | tf_op jit(solution)/shard_map/ppermute | solution.py:34
  76.4 34.5 %collective-permute-start.12 = (bf16[768,768]{1,0:T(8,128)(2,1)}, bf16[768,768]{1,0:T(8,128)(2,1)S(1)}, u32[]{:S(2)}, u32[]{:S(2)}) collective-permute-start(bf16[768,768]{1,0:T(8,128)(2,1)} %get-tuple-element.63), channel_id=1, source_target_pairs={{0,96},{32,0},{64,32},{96,64},{1,97},{33,1},{65,33},{97,65},{2,98}... | collective-permute-start | bytes 3538952 | tf_op jit(solution)/shard_map/ppermute | solution.py:34
  79.1 31.8 %collective-permute-start.13 = (bf16[512,768]{1,0:T(8,128)(2,1)}, bf16[512,768]{1,0:T(8,128)(2,1)S(1)}, u32[]{:S(2)}, u32[]{:S(2)}) collective-permute-start(bf16[512,768]{1,0:T(8,128)(2,1)} %copy-done.13), channel_id=1, source_target_pairs={{0,16},{16,0},{1,17},{17,1},{2,18},{18,2},{3,19},{19,3},{4,20},{20... | collective-permute-start | bytes 2359304 | tf_op jit(solution)/shard_map/ppermute | solution.py:34
  98.0 7.1 %collective-permute-start.10 = (bf16[56,768]{1,0:T(8,128)(2,1)S(1)}, bf16[56,768]{1,0:T(8,128)(2,1)S(1)}, u32[]{:S(2)}, u32[]{:S(2)}) collective-permute-start(bf16[56,768]{1,0:T(8,128)(2,1)S(1)} %reduce_sum.12.own), channel_id=1, source_target_pairs={{0,64},{32,96},{64,0},{96,32},{1,65},{33,97},{65,1},{97,33},{2,66}... | collective-permute-start | bytes 258056 | tf_op jit(solution)/shard_map/ppermute | solution.py:34
  98.7 8.5 %collective-permute-start.9 = (bf16[56,768]{1,0:T(8,128)(2,1)S(1)}, bf16[56,768]{1,0:T(8,128)(2,1)S(1)}, u32[]{:S(2)}, u32[]{:S(2)}) collective-permute-start(bf16[56,768]{1,0:T(8,128)(2,1)S(1)} %reduce_sum.12.own), channel_id=1, source_target_pairs={{0,96},{32,0},{64,32},{96,64},{1,97},{33,1},{65,33},{97,65},{2,98}... | collective-permute-start | bytes 258056 | tf_op jit(solution)/shard_map/ppermute | solution.py:34
  105.1 4.5 %collective-permute-start.8 = (bf16[56,768]{1,0:T(8,128)(2,1)S(1)}, bf16[56,768]{1,0:T(8,128)(2,1)S(1)}, u32[]{:S(2)}, u32[]{:S(2)}) collective-permute-start(bf16[56,768]{1,0:T(8,128)(2,1)S(1)} %reduce_sum.12.own), channel_id=1, source_target_pairs={{0,32},{32,64},{64,96},{96,0},{1,33},{33,65},{65,97},{97,1},{2,34}... | collective-permute-start | bytes 258056 | tf_op jit(solution)/shard_map/ppermute | solution.py:34
  111.9 24.6 %all-to-all-start.1 = ((bf16[16,56,768]{2,1,0:T(8,128)(2,1)}), bf16[16,56,768]{2,1,0:T(8,128)(2,1)S(1)}, u32[]{:S(2)}, u32[]{:S(2)}) async-start(bf16[16,56,768]{2,1,0:T(8,128)(2,1)} %total.1), calls=%async_computation.1 | async-start | bytes 2752512 | tf_op jit(solution)/shard_map/all_to_all | solution.py:467
  120.5 7.9 %collective-permute-start.15 = (bf16[256,768]{1,0:T(8,128)(2,1)S(1)}, bf16[256,768]{1,0:T(8,128)(2,1)S(1)}, u32[]{:S(2)}, u32[]{:S(2)}) collective-permute-start(bf16[256,768]{1,0:T(8,128)(2,1)S(1)} %slice.7), channel_id=1, source_target_pairs={{0,96},{32,0},{64,32},{96,64},{1,97},{33,1},{65,33},{97,65},{2,98}... | collective-permute-start | bytes 1179656 | tf_op jit(solution)/shard_map/ppermute | solution.py:34
  121.0 8.1 %collective-permute-start.14 = (bf16[256,768]{1,0:T(8,128)(2,1)S(1)}, bf16[256,768]{1,0:T(8,128)(2,1)S(1)}, u32[]{:S(2)}, u32[]{:S(2)}) collective-permute-start(bf16[256,768]{1,0:T(8,128)(2,1)S(1)} %slice.6), channel_id=1, source_target_pairs={{0,32},{32,64},{64,96},{96,0},{1,33},{33,65},{65,97},{97,1},{2,34}... | collective-permute-start | bytes 1179656 | tf_op jit(solution)/shard_map/ppermute | solution.py:34
  136.5 6.6 %collective-permute-start.16 = (bf16[896,768]{1,0:T(8,128)(2,1)S(1)}, bf16[896,768]{1,0:T(8,128)(2,1)S(1)}, u32[]{:S(2)}, u32[]{:S(2)}) collective-permute-start(bf16[896,768]{1,0:T(8,128)(2,1)S(1)} %bitcast.7), channel_id=1, source_target_pairs={{0,1},{1,0},{2,3},{3,2},{4,5},{5,4},{6,7},{7,6},{8,9},{9,8},{10,11... | collective-permute-start | bytes 4128776 | tf_op jit(solution)/shard_map/ppermute | solution.py:34
  (11 other events, 27.1 us)

commit v4 on v3

--- a/solution.py
+++ b/solution.py
@@ -127,7 +127,7 @@
         out_shape=(wide(ROWS), narrow(ROWS), wide(ROWS), narrow(ROWS)),
         in_specs=[VMEM] * 4,
         out_specs=(VMEM,) * 4,
-        compiler_params=MOST,
+        compiler_params=LIMIT,
         cost_estimate=pl.CostEstimate(flops=14 * 10**8, bytes_accessed=10**7, transcendentals=0),
         name="own",
     )(image, text, hi, ht)
@@ -184,24 +184,15 @@
         raw = nn(image[c : c + CH, :], head_i[...])
         zout[c : c + CH, :] = raw
         ri[n + c : n + c + CH, :] = (raw * scale_of(raw)).astype(bf16)
-    outs.append(io.start(zout, zi1))
-    outs.append(io.start(ri.at[pl.ds(n, n)], ri1))
-    c_itail.wait()
+    for copy in [c_itail, c_rt0, c_ri0, c_zt0, c_ht, *c_tail, *c_t[0], *c_t[1], *c_t[2]]:
+        copy.wait()
     ea[0:n, :] = column_weights(lse_i[...])
     ea[n : 2 * n, :] = column_weights(image_tail(itail))
-    c_rt0.wait()
-    c_ri0.wait()
     for b in range(3):
         at = b * n
-        for copy in c_t[b]:
-            copy.wait()
         if b == 0:
-            c_zt0.wait()
             lse_row = lse_t[...]
         else:
-            c_tail[b - 1].wait()
-            if b == 1:
-                c_ht.wait()
             for c in CHUNKS:
                 raw = nn(t[at + c : at + c + CH, :], head_t[...])
                 zt[at + c : at + c + CH, :] = raw
@@ -216,7 +207,11 @@
             else:
                 pout[b - 1, c : c + CH, :] = g.astype(bf16)
             pre[at + c : at + c + CH, :] = pre_gradient(zt[at + c : at + c + CH, :], logit_scale * g)
-        outs.append(io.start(bout, tbase) if b == 0 else io.start(pout.at[b - 1], (p1, p2)[b - 1]))
+    outs.append(io.start(zout, zi1))
+    outs.append(io.start(ri.at[pl.ds(n, n)], ri1))
+    outs.append(io.start(bout, tbase))
+    outs.append(io.start(pout.at[0], p1))
+    outs.append(io.start(pout.at[1], p2))
     for r in range(0, 2 * n, CH):
         g = nn(w[r : r + CH, :], rt[...])
         if r < n:
@@ -225,7 +220,9 @@
     outs.append(io.start(iout, ig))
     for r in range(0, TXT, CH):
         wout[r : r + CH, :] = tn(t[:, r : r + CH], pre[...])
-    outs.append(io.start(wout, wt))
+        if r + CH == TXT - CH:
+            outs.append(io.start(wout.at[pl.ds(0, TXT - CH)], wt.at[pl.ds(0, TXT - CH)]))
+    outs.append(io.start(wout.at[pl.ds(TXT - CH, CH)], wt.at[pl.ds(TXT - CH, CH)]))
     for copy in outs:
         copy.wait()
 

time: 146 us -> 143 us (0.979)
  waiting for transfers between devices: 46.7 us -> 43.7 us
  local copies, waits for them, and re-layouts: 8.47 us -> 10.7 us
  Pallas kernels: 47.1 us -> 45.3 us
    ppermute x17, waiting for transfers between devices: 25.7 us -> 22.8 us  [permute(): lax.ppermute(value, axis, [(i, (i + shift) % size) for i in range(size)])]
    unnamed x32 -> x38, local copies, waits for them, and re-layouts: 7.31 us -> 9.58 us
  transfers between devices with their start and end apart: 19 -> 19, of which waited for: 10 -> 10; matrix products, arithmetic and copies ran while one was open for 2% -> 2% of each run, Pallas kernels for 21% -> 20%
where the time goes in v4:
time: 143 us; the launch traced here: 142 us
  Pallas kernels  45.3 us (32%)
  waiting for transfers between devices  43.7 us (31%)
  starting transfers between devices  40.2 us (28%)
  local copies, waits for them, and re-layouts  10.7 us (7%)
  other arithmetic  1.53 us (1%)
    ppermute x17, starting transfers between devices, permute(): lax.ppermute(value, axis, [(i, (i + shift) % size) for i in range(size)])  25.4 us
    ppermute x17, waiting for transfers between devices, permute(): lax.ppermute(value, axis, [(i, (i + shift) % size) for i in range(size)])  22.8 us
    pallas_call x1, Pallas kernels, first_call(): pl.pallas_call(first_kernel, out_shape=(wide(n), narrow(n), narrow(n), na...  16.8 us
    all_to_all x1, waiting for transfers between devices, reduce_heads(): part = lax.all_to_all(part, PLANE, 0, 0, tiled=True)  16.2 us
    pallas_call x1, Pallas kernels, second_call(): pl.pallas_call(second_kernel, out_shape=(narrow(n + MID), narrow(n + MID)...  10.3 us
    unnamed x38, local copies, waits for them, and re-layouts  9.58 us
    all_to_all x1, starting transfers between devices, spread_heads(): lax.all_to_all(whole, PLANE, 0, 0, tiled=True).reshape(HALF, EMB)  7.38 us
    all_to_all x1, starting transfers between devices, reduce_heads(): part = lax.all_to_all(part, PLANE, 0, 0, tiled=True)  7.36 us
  transfers between devices with their start and end apart: 19, of which 10 were waited for; matrix products, arithmetic and copies ran while one was open for 2% of the time, Pallas kernels for 20%

profile of v4, /device:TPU:1, one launch (start us, length us, event | category | flops | bytes accessed | tf_op | source)
XLA Modules:
  0.0 142.5 jit_solution(6741487357083841622)
XLA Ops:
  0.6 2.8 %pack.1 = (bf16[256,768]{1,0:T(8,128)(2,1)}, bf16[272,768]{1,0:T(8,128)(2,1)}, bf16[528,1024]{1,0:T(8,128)(2,1)}) custom-call(bf16[512,768]{1,0:T(8,128)(2,1)} %bitcast.12, bf16[512,1024]{1,0:T(8,128)(2,1)} %bitcast.9, f32[1,512]{1,0:T(1,128)} %lse_t.3, f32[1,512]{1,0:T(1,128)} %lse_i.5), custom_call_target="tpu_custom_call" | custom-call | flops 100000 | bytes 4000000 | tf_op jit(solution)/shard_map/pack/pallas_call | solution.py:105
  3.5 2.0 %collective-permute-start = (bf16[528,1024]{1,0:T(8,128)(2,1)}, bf16[528,1024]{1,0:T(8,128)(2,1)}, u32[]{:S(2)}, u32[]{:S(2)}) collective-permute-start(bf16[528,1024]{1,0:T(8,128)(2,1)} %get-tuple-element.41), channel_id=1, source_target_pairs={{0,16},{16,0},{1,17},{17,1},{2,18},{18,2},{3,19},{19,3},{4,20},{20... | collective-permute-start | bytes 3244040 | tf_op jit(solution)/shard_map/ppermute | solution.py:34
  5.5 2.7 %collective-permute-start.2 = (bf16[272,768]{1,0:T(8,128)(2,1)}, bf16[272,768]{1,0:T(8,128)(2,1)S(1)}, u32[]{:S(2)}, u32[]{:S(2)}) collective-permute-start(bf16[272,768]{1,0:T(8,128)(2,1)} %get-tuple-element.43), channel_id=1, source_target_pairs={{0,96},{32,0},{64,32},{96,64},{1,97},{33,1},{65,33},{97,65},{2,98}... | collective-permute-start | bytes 1253384 | tf_op jit(solution)/shard_map/ppermute | solution.py:34
  8.3 2.7 %collective-permute-start.6 = (bf16[256,768]{1,0:T(8,128)(2,1)}, bf16[256,768]{1,0:T(8,128)(2,1)S(1)}, u32[]{:S(2)}, u32[]{:S(2)}) collective-permute-start(bf16[256,768]{1,0:T(8,128)(2,1)} %get-tuple-element.42), channel_id=1, source_target_pairs={{0,96},{32,0},{64,32},{96,64},{1,97},{33,1},{65,33},{97,65},{2,98}... | collective-permute-start | bytes 1179656 | tf_op jit(solution)/shard_map/ppermute | solution.py:34
  13.3 4.2 %own.1 = (f32[512,768]{1,0:T(8,128)S(1)}, bf16[512,768]{1,0:T(8,128)(2,1)S(1)}, f32[512,768]{1,0:T(8,128)}, bf16[512,768]{1,0:T(8,128)(2,1)S(1)}) custom-call(bf16[512,1024]{1,0:T(8,128)(2,1)S(1)} %bitcast.10, bf16[512,768]{1,0:T(8,128)(2,1)S(1)} %bitcast.13, bf16[1024,768]{1,0:T(8,128)(2,1)} %head.3, bf16[768,768]{1,0:T(8,128)(2,1)S(1)} %copy-done.9), custom_call_target="tpu_custom_call" | custom-call | flops 1400000000 | bytes 10000000 | tf_op jit(solution)/shard_map/own/pallas_call | solution.py:125
  19.6 8.4 %collective-permute-done.1.t1a = bf16[256,768]{1,0:T(8,128)(2,1)S(1)} collective-permute-done((bf16[256,768]{1,0:T(8,128)(2,1)}, bf16[256,768]{1,0:T(8,128)(2,1)S(1)}, u32[]{:S(2)}, u32[]{:S(2)}) %collective-permute-start.1) | collective-permute-done | bytes 393248 | tf_op jit(solution)/shard_map/ppermute | solution.py:34
  28.0 2.7 %collective-permute-start.4 = (bf16[272,768]{1,0:T(8,128)(2,1)S(1)}, bf16[272,768]{1,0:T(8,128)(2,1)S(1)}, u32[]{:S(2)}, u32[]{:S(2)}) collective-permute-start(bf16[272,768]{1,0:T(8,128)(2,1)S(1)} %collective-permute-done.2.t2b), channel_id=1, source_target_pairs={{0,96},{32,0},{64,32},{96,64},{1,97},{33,1},{65,33},{97,65},{2,98}... | collective-permute-start | bytes 1253384 | tf_op jit(solution)/shard_map/ppermute | solution.py:34
  30.7 16.8 %first.1 = (f32[512,768]{1,0:T(8,128)}, bf16[512,768]{1,0:T(8,128)(2,1)S(1)}, bf16[512,768]{1,0:T(8,128)(2,1)S(1)}, bf16[512,768]{1,0:T(8,128)(2,1)S(1)}, f32[51...) custom-call(bf16[528,1024]{1,0:T(8,128)(2,1)} %collective-permute-done.i1, bf16[512,768]{1,0:T(8,128)(2,1)S(1)} %bitcast.14, ...), custom_call_target="tpu_custom_call" | custom-call | flops 12000000000 | bytes 20000000 | tf_op jit(solution)/shard_map/first/pallas_call | solution.py:232
  47.5 10.3 %second.1 = (bf16[768,768]{1,0:T(8,128)(2,1)}, bf16[768,768]{1,0:T(8,128)(2,1)}, bf16[512,768]{1,0:T(8,128)(2,1)S(1)}, f32[512,768]{1,0:T(8,128)}, bf16[896,768]{1,0:T(8,128)(2,1)}, /*index=5*/bf16[896,768]{1,0:T(8,128)(2,1)}) custom-call(s32[1]{0:T(128)} %bitcast.core, bf16[512,1024]{1,0:T(8,128)(2,1)S(1)} %bitcast.11, ...), custom_call_target="tpu_custom_call" | custom-call | flops 8000000000 | bytes 20000000 | tf_op jit(solution)/shard_map/second/pallas_call | solution.py:333
  57.9 2.8 %collective-permute-start.7 = (bf16[896,768]{1,0:T(8,128)(2,1)}, bf16[896,768]{1,0:T(8,128)(2,1)S(1)}, u32[]{:S(2)}, u32[]{:S(2)}) collective-permute-start(bf16[896,768]{1,0:T(8,128)(2,1)} %get-tuple-element.61), channel_id=1, source_target_pairs={{0,1},{1,0},{2,3},{3,2},{4,5},{5,4},{6,7},{7,6},{8,9},{9,8},{10,11... | collective-permute-start | bytes 4128776 | tf_op jit(solution)/shard_map/ppermute | solution.py:34
  60.7 3.0 %collective-permute-done.7.b = bf16[896,768]{1,0:T(8,128)(2,1)S(1)} collective-permute-done((bf16[896,768]{1,0:T(8,128)(2,1)}, bf16[896,768]{1,0:T(8,128)(2,1)S(1)}, u32[]{:S(2)}, u32[]{:S(2)}) %collective-permute-start.7) | collective-permute-done | bytes 1376288 | tf_op jit(solution)/shard_map/ppermute | solution.py:34
  66.4 7.4 %all-to-all-start = ((bf16[16,56,768]{2,1,0:T(8,128)(2,1)}), bf16[16,56,768]{2,1,0:T(8,128)(2,1)}, u32[]{:S(2)}, u32[]{:S(2)}) async-start(bf16[16,56,768]{2,1,0:T(8,128)(2,1)} %bitcast.3), calls=%async_computation | async-start | bytes 2752512 | tf_op jit(solution)/shard_map/all_to_all | solution.py:457
  73.8 2.7 %collective-permute-start.12 = (bf16[768,768]{1,0:T(8,128)(2,1)}, bf16[768,768]{1,0:T(8,128)(2,1)S(1)}, u32[]{:S(2)}, u32[]{:S(2)}) collective-permute-start(bf16[768,768]{1,0:T(8,128)(2,1)} %get-tuple-element.63), channel_id=1, source_target_pairs={{0,96},{32,0},{64,32},{96,64},{1,97},{33,1},{65,33},{97,65},{2,98}... | collective-permute-start | bytes 3538952 | tf_op jit(solution)/shard_map/ppermute | solution.py:34
  77.7 16.2 %all-to-all-done = bf16[16,56,768]{2,1,0:T(8,128)(2,1)} async-done(((bf16[16,56,768]{2,1,0:T(8,128)(2,1)}), bf16[16,56,768]{2,1,0:T(8,128)(2,1)}, u32[]{:S(2)}, u32[]{:S(2)}) %all-to-all-start) | async-done | bytes 1376288 | tf_op jit(solution)/shard_map/all_to_all | solution.py:457
  96.9 5.7 %collective-permute-done.10.across = bf16[56,768]{1,0:T(8,128)(2,1)S(1)} collective-permute-done((bf16[56,768]{1,0:T(8,128)(2,1)S(1)}, bf16[56,768]{1,0:T(8,128)(2,1)S(1)}, u32[]{:S(2)}, u32[]{:S(2)}) %collective-permute-start.10) | collective-permute-done | bytes 86048 | tf_op jit(solution)/shard_map/ppermute | solution.py:34
  102.6 1.6 %collective-permute-start.8 = (bf16[56,768]{1,0:T(8,128)(2,1)S(1)}, bf16[56,768]{1,0:T(8,128)(2,1)S(1)}, u32[]{:S(2)}, u32[]{:S(2)}) collective-permute-start(bf16[56,768]{1,0:T(8,128)(2,1)S(1)} %reduce_sum.12.own), channel_id=1, source_target_pairs={{0,32},{32,64},{64,96},{96,0},{1,33},{33,65},{65,97},{97,1},{2,34}... | collective-permute-start | bytes 258056 | tf_op jit(solution)/shard_map/ppermute | solution.py:34
  104.6 2.5 %collective-permute-done.8.plus = bf16[56,768]{1,0:T(8,128)(2,1)S(1)} collective-permute-done((bf16[56,768]{1,0:T(8,128)(2,1)S(1)}, bf16[56,768]{1,0:T(8,128)(2,1)S(1)}, u32[]{:S(2)}, u32[]{:S(2)}) %collective-permute-start.8) | collective-permute-done | bytes 86048 | tf_op jit(solution)/shard_map/ppermute | solution.py:34
  109.4 7.4 %all-to-all-start.1 = ((bf16[16,56,768]{2,1,0:T(8,128)(2,1)}), bf16[16,56,768]{2,1,0:T(8,128)(2,1)S(1)}, u32[]{:S(2)}, u32[]{:S(2)}) async-start(bf16[16,56,768]{2,1,0:T(8,128)(2,1)} %total.1), calls=%async_computation.1 | async-start | bytes 2752512 | tf_op jit(solution)/shard_map/all_to_all | solution.py:464
  122.3 2.6 %back.3 = f32[512,1024]{1,0:T(8,128)} custom-call(f32[512,768]{1,0:T(8,128)S(1)} %copy-done.5, bf16[1024,768]{1,0:T(8,128)(2,1)S(1)} %copy-done.2, f32[512,768]{1,0:T(8,128)S(1)} %copy-done.7, bf16[512,768]{1,0:T(8,128)(2,1)S(1)} %collective-permute-done.13.rest_0_), custom_call_target="tpu_custom_call" | custom-call | flops 805306368 | bytes 10000000 | tf_op jit(solution)/shard_map/back/pallas_call | solution.py:381
  126.7 2.5 %back.2 = f32[512,768]{1,0:T(8,128)} custom-call(f32[512,768]{1,0:T(8,128)S(1)} %copy-done.3, bf16[768,768]{1,0:T(8,128)(2,1)S(1)} %copy-done.10, f32[512,768]{1,0:T(8,128)S(1)} %copy-done.6, bf16[768,768]{1,0:T(8,128)(2,1)S(1)} %collective-permute-done.11.rest_0_, bf16[768,768]{1,0:T(8,128)(2,1)S(1)} %copy-done.1, ...), custom_call_target="tpu_custom_call" | custom-call | flops 603979776 | bytes 10000000 | tf_op jit(solution)/shard_map/back/pallas_call | solution.py:381
  129.2 4.8 %all-to-all-done.1 = bf16[16,56,768]{2,1,0:T(8,128)(2,1)S(1)} async-done(((bf16[16,56,768]{2,1,0:T(8,128)(2,1)}), bf16[16,56,768]{2,1,0:T(8,128)(2,1)S(1)}, u32[]{:S(2)}, u32[]{:S(2)}) %all-to-all-start.1) | async-done | bytes 1376288 | tf_op jit(solution)/shard_map/all_to_all | solution.py:464
  133.9 3.9 %collective-permute-start.16 = (bf16[896,768]{1,0:T(8,128)(2,1)S(1)}, bf16[896,768]{1,0:T(8,128)(2,1)S(1)}, u32[]{:S(2)}, u32[]{:S(2)}) collective-permute-start(bf16[896,768]{1,0:T(8,128)(2,1)S(1)} %bitcast.7), channel_id=1, source_target_pairs={{0,1},{1,0},{2,3},{3,2},{4,5},{5,4},{6,7},{7,6},{8,9},{9,8},{10,11... | collective-permute-start | bytes 4128776 | tf_op jit(solution)/shard_map/ppermute | solution.py:34
  137.8 1.7 %final.2 = (f32[1024,768]{1,0:T(8,128)}, f32[768,768]{1,0:T(8,128)}) custom-call(s32[1]{0:T(128)} %bitcast.core, bf16[896,768]{1,0:T(8,128)(2,1)S(1)} %bitcast.8), custom_call_target="tpu_custom_call" | custom-call | flops 1000000 | bytes 4000000 | tf_op jit(solution)/shard_map/final/pallas_call | solution.py:406
  140.6 1.7 %final.3 = (f32[1024,768]{1,0:T(8,128)}, f32[768,768]{1,0:T(8,128)}) custom-call(s32[1]{0:T(128)} %bitcast.core, bf16[896,768]{1,0:T(8,128)(2,1)S(1)} %collective-permute-done.16.half, f32[1024,768]{1,0:T(8,128)} %get-tuple-element.74.rest_0_, f32[768,768]{1,0:T(8,128)} %get-tuple-element.75.rest_1_), custom_call_target="tpu_custom_call", output_to_operand_aliasing={{0}: (2, {}), {1}: (3, {})} | custom-call | flops 1000000 | bytes 4000000 | tf_op jit(solution)/shard_map/final/pallas_call | solution.py:406
  (65 shorter events, 22.4 us)
Async XLA Ops:
  0.6 10.3 %copy-start.9 = (bf16[768,768]{1,0:T(8,128)(2,1)S(1)}, bf16[768,768]{1,0:T(8,128)(2,1)}, u32[]{:S(2)}) copy-start(bf16[768,768]{1,0:T(8,128)(2,1)} %head.2) | copy-start | bytes 3538948
  3.5 27.2 %collective-permute-start = (bf16[528,1024]{1,0:T(8,128)(2,1)}, bf16[528,1024]{1,0:T(8,128)(2,1)}, u32[]{:S(2)}, u32[]{:S(2)}) collective-permute-start(bf16[528,1024]{1,0:T(8,128)(2,1)} %get-tuple-element.41), channel_id=1, source_target_pairs={{0,16},{16,0},{1,17},{17,1},{2,18},{18,2},{3,19},{19,3},{4,20},{20... | collective-permute-start | bytes 3244040 | tf_op jit(solution)/shard_map/ppermute | solution.py:34
  5.5 22.5 %collective-permute-start.2 = (bf16[272,768]{1,0:T(8,128)(2,1)}, bf16[272,768]{1,0:T(8,128)(2,1)S(1)}, u32[]{:S(2)}, u32[]{:S(2)}) collective-permute-start(bf16[272,768]{1,0:T(8,128)(2,1)} %get-tuple-element.43), channel_id=1, source_target_pairs={{0,96},{32,0},{64,32},{96,64},{1,97},{33,1},{65,33},{97,65},{2,98}... | collective-permute-start | bytes 1253384 | tf_op jit(solution)/shard_map/ppermute | solution.py:34
  8.3 22.4 %collective-permute-start.5 = (bf16[272,768]{1,0:T(8,128)(2,1)}, bf16[272,768]{1,0:T(8,128)(2,1)S(1)}, u32[]{:S(2)}, u32[]{:S(2)}) collective-permute-start(bf16[272,768]{1,0:T(8,128)(2,1)} %get-tuple-element.43), channel_id=1, source_target_pairs={{0,32},{32,64},{64,96},{96,0},{1,33},{33,65},{65,97},{97,1},{2,34}... | collective-permute-start | bytes 1253384 | tf_op jit(solution)/shard_map/ppermute | solution.py:34
  8.3 19.7 %collective-permute-start.1 = (bf16[256,768]{1,0:T(8,128)(2,1)}, bf16[256,768]{1,0:T(8,128)(2,1)S(1)}, u32[]{:S(2)}, u32[]{:S(2)}) collective-permute-start(bf16[256,768]{1,0:T(8,128)(2,1)} %get-tuple-element.42), channel_id=1, source_target_pairs={{0,32},{32,64},{64,96},{96,0},{1,33},{33,65},{65,97},{97,1},{2,34}... | collective-permute-start | bytes 1179656 | tf_op jit(solution)/shard_map/ppermute | solution.py:34
  8.3 22.4 %collective-permute-start.6 = (bf16[256,768]{1,0:T(8,128)(2,1)}, bf16[256,768]{1,0:T(8,128)(2,1)S(1)}, u32[]{:S(2)}, u32[]{:S(2)}) collective-permute-start(bf16[256,768]{1,0:T(8,128)(2,1)} %get-tuple-element.42), channel_id=1, source_target_pairs={{0,96},{32,0},{64,32},{96,64},{1,97},{33,1},{65,33},{97,65},{2,98}... | collective-permute-start | bytes 1179656 | tf_op jit(solution)/shard_map/ppermute | solution.py:34
  13.3 17.4 %copy-start.14 = (bf16[1,512,768]{2,1,0:T(8,128)(2,1)S(1)}, bf16[1,512,768]{2,1,0:T(8,128)(2,1)}, u32[]{:S(2)}) copy-start(bf16[1,512,768]{2,1,0:T(8,128)(2,1)} %param.7) | copy-start | bytes 2359300
  13.3 17.4 %copy-start.15 = (f32[1,512]{1,0:T(1,128)S(1)}, f32[1,512]{1,0:T(1,128)}, u32[]{:S(2)}) copy-start(f32[1,512]{1,0:T(1,128)} %lse_t.3) | copy-start | bytes 6148
  13.3 17.4 %copy-start.16 = (f32[1,512]{1,0:T(1,128)S(1)}, f32[1,512]{1,0:T(1,128)}, u32[]{:S(2)}) copy-start(f32[1,512]{1,0:T(1,128)} %lse_i.5) | copy-start | bytes 6148
  28.0 19.5 %copy-start.12 = (bf16[1,512,1024]{2,1,0:T(8,128)(2,1)S(1)}, bf16[1,512,1024]{2,1,0:T(8,128)(2,1)}, u32[]{:S(2)}) copy-start(bf16[1,512,1024]{2,1,0:T(8,128)(2,1)} %param.6) | copy-start | bytes 3145732
  28.0 19.5 %collective-permute-start.3 = (bf16[256,768]{1,0:T(8,128)(2,1)S(1)}, bf16[256,768]{1,0:T(8,128)(2,1)S(1)}, u32[]{:S(2)}, u32[]{:S(2)}) collective-permute-start(bf16[256,768]{1,0:T(8,128)(2,1)S(1)} %collective-permute-done.1.t1a), channel_id=1, source_target_pairs={{0,32},{32,64},{64,96},{96,0},{1,33},{33,65},{65,97},{97,1},{2,34}... | collective-permute-start | bytes 1179656 | tf_op jit(solution)/shard_map/ppermute | solution.py:34
  28.0 19.5 %collective-permute-start.4 = (bf16[272,768]{1,0:T(8,128)(2,1)S(1)}, bf16[272,768]{1,0:T(8,128)(2,1)S(1)}, u32[]{:S(2)}, u32[]{:S(2)}) collective-permute-start(bf16[272,768]{1,0:T(8,128)(2,1)S(1)} %collective-permute-done.2.t2b), channel_id=1, source_target_pairs={{0,96},{32,0},{64,32},{96,64},{1,97},{33,1},{65,33},{97,65},{2,98}... | collective-permute-start | bytes 1253384 | tf_op jit(solution)/shard_map/ppermute | solution.py:34
  57.9 5.7 %collective-permute-start.7 = (bf16[896,768]{1,0:T(8,128)(2,1)}, bf16[896,768]{1,0:T(8,128)(2,1)S(1)}, u32[]{:S(2)}, u32[]{:S(2)}) collective-permute-start(bf16[896,768]{1,0:T(8,128)(2,1)} %get-tuple-element.61), channel_id=1, source_target_pairs={{0,1},{1,0},{2,3},{3,2},{4,5},{5,4},{6,7},{7,6},{8,9},{9,8},{10,11... | collective-permute-start | bytes 4128776 | tf_op jit(solution)/shard_map/ppermute | solution.py:34
  66.4 27.5 %all-to-all-start = ((bf16[16,56,768]{2,1,0:T(8,128)(2,1)}), bf16[16,56,768]{2,1,0:T(8,128)(2,1)}, u32[]{:S(2)}, u32[]{:S(2)}) async-start(bf16[16,56,768]{2,1,0:T(8,128)(2,1)} %bitcast.3), calls=%async_computation | async-start | bytes 2752512 | tf_op jit(solution)/shard_map/all_to_all | solution.py:457
  73.7 34.6 %collective-permute-start.11 = (bf16[768,768]{1,0:T(8,128)(2,1)}, bf16[768,768]{1,0:T(8,128)(2,1)S(1)}, u32[]{:S(2)}, u32[]{:S(2)}) collective-permute-start(bf16[768,768]{1,0:T(8,128)(2,1)} %get-tuple-element.62), channel_id=1, source_target_pairs={{0,32},{32,64},{64,96},{96,0},{1,33},{33,65},{65,97},{97,1},{2,34}... | collective-permute-start | bytes 3538952 | tf_op jit(solution)/shard_map/ppermute | solution.py:34
  73.8 34.5 %collective-permute-start.12 = (bf16[768,768]{1,0:T(8,128)(2,1)}, bf16[768,768]{1,0:T(8,128)(2,1)S(1)}, u32[]{:S(2)}, u32[]{:S(2)}) collective-permute-start(bf16[768,768]{1,0:T(8,128)(2,1)} %get-tuple-element.63), channel_id=1, source_target_pairs={{0,96},{32,0},{64,32},{96,64},{1,97},{33,1},{65,33},{97,65},{2,98}... | collective-permute-start | bytes 3538952 | tf_op jit(solution)/shard_map/ppermute | solution.py:34
  76.5 31.9 %collective-permute-start.13 = (bf16[512,768]{1,0:T(8,128)(2,1)}, bf16[512,768]{1,0:T(8,128)(2,1)S(1)}, u32[]{:S(2)}, u32[]{:S(2)}) collective-permute-start(bf16[512,768]{1,0:T(8,128)(2,1)} %copy-done.17), channel_id=1, source_target_pairs={{0,16},{16,0},{1,17},{17,1},{2,18},{18,2},{3,19},{19,3},{4,20},{20... | collective-permute-start | bytes 2359304 | tf_op jit(solution)/shard_map/ppermute | solution.py:34
  95.4 7.2 %collective-permute-start.10 = (bf16[56,768]{1,0:T(8,128)(2,1)S(1)}, bf16[56,768]{1,0:T(8,128)(2,1)S(1)}, u32[]{:S(2)}, u32[]{:S(2)}) collective-permute-start(bf16[56,768]{1,0:T(8,128)(2,1)S(1)} %reduce_sum.12.own), channel_id=1, source_target_pairs={{0,64},{32,96},{64,0},{96,32},{1,65},{33,97},{65,1},{97,33},{2,66}... | collective-permute-start | bytes 258056 | tf_op jit(solution)/shard_map/ppermute | solution.py:34
  96.2 8.5 %collective-permute-start.9 = (bf16[56,768]{1,0:T(8,128)(2,1)S(1)}, bf16[56,768]{1,0:T(8,128)(2,1)S(1)}, u32[]{:S(2)}, u32[]{:S(2)}) collective-permute-start(bf16[56,768]{1,0:T(8,128)(2,1)S(1)} %reduce_sum.12.own), channel_id=1, source_target_pairs={{0,96},{32,0},{64,32},{96,64},{1,97},{33,1},{65,33},{97,65},{2,98}... | collective-permute-start | bytes 258056 | tf_op jit(solution)/shard_map/ppermute | solution.py:34
  102.6 4.5 %collective-permute-start.8 = (bf16[56,768]{1,0:T(8,128)(2,1)S(1)}, bf16[56,768]{1,0:T(8,128)(2,1)S(1)}, u32[]{:S(2)}, u32[]{:S(2)}) collective-permute-start(bf16[56,768]{1,0:T(8,128)(2,1)S(1)} %reduce_sum.12.own), channel_id=1, source_target_pairs={{0,32},{32,64},{64,96},{96,0},{1,33},{33,65},{65,97},{97,1},{2,34}... | collective-permute-start | bytes 258056 | tf_op jit(solution)/shard_map/ppermute | solution.py:34
  109.4 24.6 %all-to-all-start.1 = ((bf16[16,56,768]{2,1,0:T(8,128)(2,1)}), bf16[16,56,768]{2,1,0:T(8,128)(2,1)S(1)}, u32[]{:S(2)}, u32[]{:S(2)}) async-start(bf16[16,56,768]{2,1,0:T(8,128)(2,1)} %total.1), calls=%async_computation.1 | async-start | bytes 2752512 | tf_op jit(solution)/shard_map/all_to_all | solution.py:464
  118.0 7.9 %collective-permute-start.15 = (bf16[256,768]{1,0:T(8,128)(2,1)S(1)}, bf16[256,768]{1,0:T(8,128)(2,1)S(1)}, u32[]{:S(2)}, u32[]{:S(2)}) collective-permute-start(bf16[256,768]{1,0:T(8,128)(2,1)S(1)} %slice.7), channel_id=1, source_target_pairs={{0,96},{32,0},{64,32},{96,64},{1,97},{33,1},{65,33},{97,65},{2,98}... | collective-permute-start | bytes 1179656 | tf_op jit(solution)/shard_map/ppermute | solution.py:34
  118.5 8.1 %collective-permute-start.14 = (bf16[256,768]{1,0:T(8,128)(2,1)S(1)}, bf16[256,768]{1,0:T(8,128)(2,1)S(1)}, u32[]{:S(2)}, u32[]{:S(2)}) collective-permute-start(bf16[256,768]{1,0:T(8,128)(2,1)S(1)} %slice.6), channel_id=1, source_target_pairs={{0,32},{32,64},{64,96},{96,0},{1,33},{33,65},{65,97},{97,1},{2,34}... | collective-permute-start | bytes 1179656 | tf_op jit(solution)/shard_map/ppermute | solution.py:34
  133.9 6.6 %collective-permute-start.16 = (bf16[896,768]{1,0:T(8,128)(2,1)S(1)}, bf16[896,768]{1,0:T(8,128)(2,1)S(1)}, u32[]{:S(2)}, u32[]{:S(2)}) collective-permute-start(bf16[896,768]{1,0:T(8,128)(2,1)S(1)} %bitcast.7), channel_id=1, source_target_pairs={{0,1},{1,0},{2,3},{3,2},{4,5},{5,4},{6,7},{7,6},{8,9},{9,8},{10,11... | collective-permute-start | bytes 4128776 | tf_op jit(solution)/shard_map/ppermute | solution.py:34
  (14 other events, 38.1 us)

commit v5 on v4

--- a/solution.py
+++ b/solution.py
@@ -433,9 +433,8 @@
     )(a, b)
 
 
-def total_kernel(own, plus, minus, across, out):
-    total = (own[...].astype(f32) + across[...].astype(f32)) + (plus[...].astype(f32) + minus[...].astype(f32))
-    total = total.astype(bf16)
+def total_kernel(own, other, out):
+    total = (own[...].astype(f32) + other[...].astype(f32)).astype(bf16)
     for k in range(16):
         out[k] = total
 
@@ -444,7 +443,7 @@
     return pl.pallas_call(
         total_kernel,
         out_shape=jax.ShapeDtypeStruct((16, HALF // 16, EMB), bf16),
-        in_specs=[VMEM] * 4,
+        in_specs=[VMEM] * 2,
         out_specs=VMEM,
         compiler_params=pltpu.CompilerParams(vmem_limit_bytes=16 * 1024 * 1024),
         cost_estimate=pl.CostEstimate(flops=10**6, bytes_accessed=2 * 10**6, transcendentals=0),
@@ -459,7 +458,9 @@
 
 
 def spread_heads(part, *beside):
-    whole = total_call(part, *[permute(part, "y", 4, d) for d in (1, 3, 2)])
+    near = lax.ppermute(part, "y", [(0, 1), (1, 0), (2, 3), (3, 2)])
+    part = (part.astype(f32) + near.astype(f32)).astype(bf16)
+    whole = total_call(part, lax.ppermute(part, "y", [(0, 3), (3, 0), (1, 2), (2, 1)]))
     whole, *beside = lax.optimization_barrier((whole, *beside))
     return lax.all_to_all(whole, PLANE, 0, 0, tiled=True).reshape(HALF, EMB), *beside
 

time: 143 us -> 143 us (level)
  starting transfers between devices: 40.2 us -> 37.4 us
  waiting for transfers between devices: 43.7 us -> 46.5 us
    ppermute x0 -> x2, waiting for transfers between devices: none -> 11.4 us  [the longest x1 7.27 us: spread_heads(): near = lax.ppermute(part, 'y', [(0, 1), (1, 0), (2, 3), (3, 2)])]
    ppermute x17 -> x14, waiting for transfers between devices: 22.8 us -> 15.2 us  [permute(): lax.ppermute(value, axis, [(i, (i + shift) % size) for i in range(size)])]
    ppermute x17 -> x14, starting transfers between devices: 25.4 us -> 22.4 us  [permute(): lax.ppermute(value, axis, [(i, (i + shift) % size) for i in range(size)])]
  transfers between devices with their start and end apart: 19 -> 18, of which waited for: 10 -> 9; matrix products, arithmetic and copies ran while one was open for 2% -> 2% of each run, Pallas kernels for 20% -> 20%
where the time goes in v5:
time: 143 us; the launch traced here: 142 us
  waiting for transfers between devices  46.5 us (33%)
  Pallas kernels  45.3 us (32%)
  starting transfers between devices  37.4 us (26%)
  local copies, waits for them, and re-layouts  10.7 us (7%)
  other arithmetic  1.55 us (1%)
    ppermute x14, starting transfers between devices, permute(): lax.ppermute(value, axis, [(i, (i + shift) % size) for i in range(size)])  22.4 us
    pallas_call x1, Pallas kernels, first_call(): pl.pallas_call(first_kernel, out_shape=(wide(n), narrow(n), narrow(n), na...  16.8 us
    all_to_all x1, waiting for transfers between devices, reduce_heads(): part = lax.all_to_all(part, PLANE, 0, 0, tiled=True)  16.2 us
    ppermute x14, waiting for transfers between devices, permute(): lax.ppermute(value, axis, [(i, (i + shift) % size) for i in range(size)])  15.2 us
    pallas_call x1, Pallas kernels, second_call(): pl.pallas_call(second_kernel, out_shape=(narrow(n + MID), narrow(n + MID)...  10.3 us
    unnamed x38, local copies, waits for them, and re-layouts  9.58 us
    all_to_all x1, starting transfers between devices, reduce_heads(): part = lax.all_to_all(part, PLANE, 0, 0, tiled=True)  7.35 us
    ppermute x1, waiting for transfers between devices, spread_heads(): near = lax.ppermute(part, 'y', [(0, 1), (1, 0), (2, 3), (3, 2)])  7.27 us
  transfers between devices with their start and end apart: 18, of which 9 were waited for; matrix products, arithmetic and copies ran while one was open for 2% of the time, Pallas kernels for 20%

profile of v5, /device:TPU:1, one launch (start us, length us, event | category | flops | bytes accessed | tf_op | source)
XLA Modules:
  0.0 142.4 jit_solution(912726867309112421)
XLA Ops:
  0.6 2.8 %pack.1 = (bf16[256,768]{1,0:T(8,128)(2,1)}, bf16[272,768]{1,0:T(8,128)(2,1)}, bf16[528,1024]{1,0:T(8,128)(2,1)}) custom-call(bf16[512,768]{1,0:T(8,128)(2,1)} %bitcast.12, bf16[512,1024]{1,0:T(8,128)(2,1)} %bitcast.9, f32[1,512]{1,0:T(1,128)} %lse_t.3, f32[1,512]{1,0:T(1,128)} %lse_i.5), custom_call_target="tpu_custom_call" | custom-call | flops 100000 | bytes 4000000 | tf_op jit(solution)/shard_map/pack/pallas_call | solution.py:105
  3.5 2.0 %collective-permute-start = (bf16[528,1024]{1,0:T(8,128)(2,1)}, bf16[528,1024]{1,0:T(8,128)(2,1)}, u32[]{:S(2)}, u32[]{:S(2)}) collective-permute-start(bf16[528,1024]{1,0:T(8,128)(2,1)} %get-tuple-element.41), channel_id=1, source_target_pairs={{0,16},{16,0},{1,17},{17,1},{2,18},{18,2},{3,19},{19,3},{4,20},{20... | collective-permute-start | bytes 3244040 | tf_op jit(solution)/shard_map/ppermute | solution.py:34
  5.5 2.7 %collective-permute-start.2 = (bf16[272,768]{1,0:T(8,128)(2,1)}, bf16[272,768]{1,0:T(8,128)(2,1)S(1)}, u32[]{:S(2)}, u32[]{:S(2)}) collective-permute-start(bf16[272,768]{1,0:T(8,128)(2,1)} %get-tuple-element.43), channel_id=1, source_target_pairs={{0,96},{32,0},{64,32},{96,64},{1,97},{33,1},{65,33},{97,65},{2,98}... | collective-permute-start | bytes 1253384 | tf_op jit(solution)/shard_map/ppermute | solution.py:34
  8.3 2.7 %collective-permute-start.6 = (bf16[256,768]{1,0:T(8,128)(2,1)}, bf16[256,768]{1,0:T(8,128)(2,1)S(1)}, u32[]{:S(2)}, u32[]{:S(2)}) collective-permute-start(bf16[256,768]{1,0:T(8,128)(2,1)} %get-tuple-element.42), channel_id=1, source_target_pairs={{0,96},{32,0},{64,32},{96,64},{1,97},{33,1},{65,33},{97,65},{2,98}... | collective-permute-start | bytes 1179656 | tf_op jit(solution)/shard_map/ppermute | solution.py:34
  13.3 4.2 %own.1 = (f32[512,768]{1,0:T(8,128)S(1)}, bf16[512,768]{1,0:T(8,128)(2,1)S(1)}, f32[512,768]{1,0:T(8,128)}, bf16[512,768]{1,0:T(8,128)(2,1)S(1)}) custom-call(bf16[512,1024]{1,0:T(8,128)(2,1)S(1)} %bitcast.10, bf16[512,768]{1,0:T(8,128)(2,1)S(1)} %bitcast.13, bf16[1024,768]{1,0:T(8,128)(2,1)} %head.3, bf16[768,768]{1,0:T(8,128)(2,1)S(1)} %copy-done.9), custom_call_target="tpu_custom_call" | custom-call | flops 1400000000 | bytes 10000000 | tf_op jit(solution)/shard_map/own/pallas_call | solution.py:125
  19.6 8.4 %collective-permute-done.1.t1a = bf16[256,768]{1,0:T(8,128)(2,1)S(1)} collective-permute-done((bf16[256,768]{1,0:T(8,128)(2,1)}, bf16[256,768]{1,0:T(8,128)(2,1)S(1)}, u32[]{:S(2)}, u32[]{:S(2)}) %collective-permute-start.1) | collective-permute-done | bytes 393248 | tf_op jit(solution)/shard_map/ppermute | solution.py:34
  28.0 2.7 %collective-permute-start.4 = (bf16[272,768]{1,0:T(8,128)(2,1)S(1)}, bf16[272,768]{1,0:T(8,128)(2,1)S(1)}, u32[]{:S(2)}, u32[]{:S(2)}) collective-permute-start(bf16[272,768]{1,0:T(8,128)(2,1)S(1)} %collective-permute-done.2.t2b), channel_id=1, source_target_pairs={{0,96},{32,0},{64,32},{96,64},{1,97},{33,1},{65,33},{97,65},{2,98}... | collective-permute-start | bytes 1253384 | tf_op jit(solution)/shard_map/ppermute | solution.py:34
  30.7 16.8 %first.1 = (f32[512,768]{1,0:T(8,128)}, bf16[512,768]{1,0:T(8,128)(2,1)S(1)}, bf16[512,768]{1,0:T(8,128)(2,1)S(1)}, bf16[512,768]{1,0:T(8,128)(2,1)S(1)}, f32[51...) custom-call(bf16[528,1024]{1,0:T(8,128)(2,1)} %collective-permute-done.i1, bf16[512,768]{1,0:T(8,128)(2,1)S(1)} %bitcast.14, ...), custom_call_target="tpu_custom_call" | custom-call | flops 12000000000 | bytes 20000000 | tf_op jit(solution)/shard_map/first/pallas_call | solution.py:232
  47.5 10.3 %second.1 = (bf16[768,768]{1,0:T(8,128)(2,1)}, bf16[768,768]{1,0:T(8,128)(2,1)}, bf16[512,768]{1,0:T(8,128)(2,1)S(1)}, f32[512,768]{1,0:T(8,128)}, bf16[896,768]{1,0:T(8,128)(2,1)}, /*index=5*/bf16[896,768]{1,0:T(8,128)(2,1)}) custom-call(s32[1]{0:T(128)} %bitcast.core, bf16[512,1024]{1,0:T(8,128)(2,1)S(1)} %bitcast.11, ...), custom_call_target="tpu_custom_call" | custom-call | flops 8000000000 | bytes 20000000 | tf_op jit(solution)/shard_map/second/pallas_call | solution.py:333
  57.8 2.8 %collective-permute-start.7 = (bf16[896,768]{1,0:T(8,128)(2,1)}, bf16[896,768]{1,0:T(8,128)(2,1)S(1)}, u32[]{:S(2)}, u32[]{:S(2)}) collective-permute-start(bf16[896,768]{1,0:T(8,128)(2,1)} %get-tuple-element.61), channel_id=1, source_target_pairs={{0,1},{1,0},{2,3},{3,2},{4,5},{5,4},{6,7},{7,6},{8,9},{9,8},{10,11... | collective-permute-start | bytes 4128776 | tf_op jit(solution)/shard_map/ppermute | solution.py:34
  60.6 3.0 %collective-permute-done.7.b = bf16[896,768]{1,0:T(8,128)(2,1)S(1)} collective-permute-done((bf16[896,768]{1,0:T(8,128)(2,1)}, bf16[896,768]{1,0:T(8,128)(2,1)S(1)}, u32[]{:S(2)}, u32[]{:S(2)}) %collective-permute-start.7) | collective-permute-done | bytes 1376288 | tf_op jit(solution)/shard_map/ppermute | solution.py:34
  66.3 7.3 %all-to-all-start = ((bf16[16,56,768]{2,1,0:T(8,128)(2,1)}), bf16[16,56,768]{2,1,0:T(8,128)(2,1)}, u32[]{:S(2)}, u32[]{:S(2)}) async-start(bf16[16,56,768]{2,1,0:T(8,128)(2,1)} %bitcast.3), calls=%async_computation | async-start | bytes 2752512 | tf_op jit(solution)/shard_map/all_to_all | solution.py:456
  73.8 2.7 %collective-permute-start.11 = (bf16[768,768]{1,0:T(8,128)(2,1)}, bf16[768,768]{1,0:T(8,128)(2,1)S(1)}, u32[]{:S(2)}, u32[]{:S(2)}) collective-permute-start(bf16[768,768]{1,0:T(8,128)(2,1)} %get-tuple-element.63), channel_id=1, source_target_pairs={{0,96},{32,0},{64,32},{96,64},{1,97},{33,1},{65,33},{97,65},{2,98}... | collective-permute-start | bytes 3538952 | tf_op jit(solution)/shard_map/ppermute | solution.py:34
  77.7 16.2 %all-to-all-done = bf16[16,56,768]{2,1,0:T(8,128)(2,1)} async-done(((bf16[16,56,768]{2,1,0:T(8,128)(2,1)}), bf16[16,56,768]{2,1,0:T(8,128)(2,1)}, u32[]{:S(2)}, u32[]{:S(2)}) %all-to-all-start) | async-done | bytes 1376288 | tf_op jit(solution)/shard_map/all_to_all | solution.py:456
  93.8 1.5 %reduce_sum.12 = bf16[56,768]{1,0:T(8,128)(2,1)S(1)} reduce(bf16[16,56,768]{2,1,0:T(8,128)(2,1)} %all-to-all-done, bf16[]{:T(256)} %constant.6.clone.1), dimensions={0}, to_apply=%region_0.0 | reduce | flops 645120 | bytes 1462274 | tf_op jit(solution)/shard_map/reduce_sum | solution.py:457
  95.5 7.3 %collective-permute-done.8 = bf16[56,768]{1,0:T(8,128)(2,1)S(1)} collective-permute-done((bf16[56,768]{1,0:T(8,128)(2,1)S(1)}, bf16[56,768]{1,0:T(8,128)(2,1)S(1)}, u32[]{:S(2)}, u32[]{:S(2)}) %collective-permute-start.8) | collective-permute-done | bytes 86048 | tf_op jit(solution)/shard_map/ppermute | solution.py:461
  103.3 4.1 %collective-permute-done.9.other = bf16[56,768]{1,0:T(8,128)(2,1)S(1)} collective-permute-done((bf16[56,768]{1,0:T(8,128)(2,1)S(1)}, bf16[56,768]{1,0:T(8,128)(2,1)S(1)}, u32[]{:S(2)}, u32[]{:S(2)}) %collective-permute-start.9) | collective-permute-done | bytes 86048 | tf_op jit(solution)/shard_map/ppermute | solution.py:463
  109.6 7.1 %all-to-all-start.1 = ((bf16[16,56,768]{2,1,0:T(8,128)(2,1)}), bf16[16,56,768]{2,1,0:T(8,128)(2,1)S(1)}, u32[]{:S(2)}, u32[]{:S(2)}) async-start(bf16[16,56,768]{2,1,0:T(8,128)(2,1)} %total.1), calls=%async_computation.1 | async-start | bytes 2752512 | tf_op jit(solution)/shard_map/all_to_all | solution.py:465
  122.3 2.6 %back.3 = f32[512,1024]{1,0:T(8,128)} custom-call(f32[512,768]{1,0:T(8,128)S(1)} %copy-done.5, bf16[1024,768]{1,0:T(8,128)(2,1)S(1)} %copy-done.2, f32[512,768]{1,0:T(8,128)S(1)} %copy-done.7, bf16[512,768]{1,0:T(8,128)(2,1)S(1)} %collective-permute-done.12.rest_0_), custom_call_target="tpu_custom_call" | custom-call | flops 805306368 | bytes 10000000 | tf_op jit(solution)/shard_map/back/pallas_call | solution.py:381
  127.7 2.5 %back.2 = f32[512,768]{1,0:T(8,128)} custom-call(f32[512,768]{1,0:T(8,128)S(1)} %copy-done.3, bf16[768,768]{1,0:T(8,128)(2,1)S(1)} %copy-done.10, f32[512,768]{1,0:T(8,128)S(1)} %copy-done.6, bf16[768,768]{1,0:T(8,128)(2,1)S(1)} %collective-permute-done.10.rest_0_, bf16[768,768]{1,0:T(8,128)(2,1)S(1)} %copy-done.1, ...), custom_call_target="tpu_custom_call" | custom-call | flops 603979776 | bytes 10000000 | tf_op jit(solution)/shard_map/back/pallas_call | solution.py:381
  130.2 3.7 %all-to-all-done.1 = bf16[16,56,768]{2,1,0:T(8,128)(2,1)S(1)} async-done(((bf16[16,56,768]{2,1,0:T(8,128)(2,1)}), bf16[16,56,768]{2,1,0:T(8,128)(2,1)S(1)}, u32[]{:S(2)}, u32[]{:S(2)}) %all-to-all-start.1) | async-done | bytes 1376288 | tf_op jit(solution)/shard_map/all_to_all | solution.py:465
  133.9 3.9 %collective-permute-start.15 = (bf16[896,768]{1,0:T(8,128)(2,1)S(1)}, bf16[896,768]{1,0:T(8,128)(2,1)S(1)}, u32[]{:S(2)}, u32[]{:S(2)}) collective-permute-start(bf16[896,768]{1,0:T(8,128)(2,1)S(1)} %bitcast.7), channel_id=1, source_target_pairs={{0,1},{1,0},{2,3},{3,2},{4,5},{5,4},{6,7},{7,6},{8,9},{9,8},{10,11... | collective-permute-start | bytes 4128776 | tf_op jit(solution)/shard_map/ppermute | solution.py:34
  137.8 1.7 %final.2 = (f32[1024,768]{1,0:T(8,128)}, f32[768,768]{1,0:T(8,128)}) custom-call(s32[1]{0:T(128)} %bitcast.core, bf16[896,768]{1,0:T(8,128)(2,1)S(1)} %bitcast.8), custom_call_target="tpu_custom_call" | custom-call | flops 1000000 | bytes 4000000 | tf_op jit(solution)/shard_map/final/pallas_call | solution.py:406
  140.5 1.7 %final.3 = (f32[1024,768]{1,0:T(8,128)}, f32[768,768]{1,0:T(8,128)}) custom-call(s32[1]{0:T(128)} %bitcast.core, bf16[896,768]{1,0:T(8,128)(2,1)S(1)} %collective-permute-done.15.half, f32[1024,768]{1,0:T(8,128)} %get-tuple-element.74.rest_0_, f32[768,768]{1,0:T(8,128)} %get-tuple-element.75.rest_1_), custom_call_target="tpu_custom_call", output_to_operand_aliasing={{0}: (2, {}), {1}: (3, {})} | custom-call | flops 1000000 | bytes 4000000 | tf_op jit(solution)/shard_map/final/pallas_call | solution.py:406
  (64 shorter events, 20.6 us)
Async XLA Ops:
  0.6 10.3 %copy-start.9 = (bf16[768,768]{1,0:T(8,128)(2,1)S(1)}, bf16[768,768]{1,0:T(8,128)(2,1)}, u32[]{:S(2)}) copy-start(bf16[768,768]{1,0:T(8,128)(2,1)} %head.2) | copy-start | bytes 3538948
  3.5 27.2 %collective-permute-start = (bf16[528,1024]{1,0:T(8,128)(2,1)}, bf16[528,1024]{1,0:T(8,128)(2,1)}, u32[]{:S(2)}, u32[]{:S(2)}) collective-permute-start(bf16[528,1024]{1,0:T(8,128)(2,1)} %get-tuple-element.41), channel_id=1, source_target_pairs={{0,16},{16,0},{1,17},{17,1},{2,18},{18,2},{3,19},{19,3},{4,20},{20... | collective-permute-start | bytes 3244040 | tf_op jit(solution)/shard_map/ppermute | solution.py:34
  5.5 22.5 %collective-permute-start.2 = (bf16[272,768]{1,0:T(8,128)(2,1)}, bf16[272,768]{1,0:T(8,128)(2,1)S(1)}, u32[]{:S(2)}, u32[]{:S(2)}) collective-permute-start(bf16[272,768]{1,0:T(8,128)(2,1)} %get-tuple-element.43), channel_id=1, source_target_pairs={{0,96},{32,0},{64,32},{96,64},{1,97},{33,1},{65,33},{97,65},{2,98}... | collective-permute-start | bytes 1253384 | tf_op jit(solution)/shard_map/ppermute | solution.py:34
  8.3 22.4 %collective-permute-start.5 = (bf16[272,768]{1,0:T(8,128)(2,1)}, bf16[272,768]{1,0:T(8,128)(2,1)S(1)}, u32[]{:S(2)}, u32[]{:S(2)}) collective-permute-start(bf16[272,768]{1,0:T(8,128)(2,1)} %get-tuple-element.43), channel_id=1, source_target_pairs={{0,32},{32,64},{64,96},{96,0},{1,33},{33,65},{65,97},{97,1},{2,34}... | collective-permute-start | bytes 1253384 | tf_op jit(solution)/shard_map/ppermute | solution.py:34
  8.3 19.7 %collective-permute-start.1 = (bf16[256,768]{1,0:T(8,128)(2,1)}, bf16[256,768]{1,0:T(8,128)(2,1)S(1)}, u32[]{:S(2)}, u32[]{:S(2)}) collective-permute-start(bf16[256,768]{1,0:T(8,128)(2,1)} %get-tuple-element.42), channel_id=1, source_target_pairs={{0,32},{32,64},{64,96},{96,0},{1,33},{33,65},{65,97},{97,1},{2,34}... | collective-permute-start | bytes 1179656 | tf_op jit(solution)/shard_map/ppermute | solution.py:34
  8.3 22.4 %collective-permute-start.6 = (bf16[256,768]{1,0:T(8,128)(2,1)}, bf16[256,768]{1,0:T(8,128)(2,1)S(1)}, u32[]{:S(2)}, u32[]{:S(2)}) collective-permute-start(bf16[256,768]{1,0:T(8,128)(2,1)} %get-tuple-element.42), channel_id=1, source_target_pairs={{0,96},{32,0},{64,32},{96,64},{1,97},{33,1},{65,33},{97,65},{2,98}... | collective-permute-start | bytes 1179656 | tf_op jit(solution)/shard_map/ppermute | solution.py:34
  13.3 17.4 %copy-start.14 = (bf16[1,512,768]{2,1,0:T(8,128)(2,1)S(1)}, bf16[1,512,768]{2,1,0:T(8,128)(2,1)}, u32[]{:S(2)}) copy-start(bf16[1,512,768]{2,1,0:T(8,128)(2,1)} %param.7) | copy-start | bytes 2359300
  13.3 17.4 %copy-start.15 = (f32[1,512]{1,0:T(1,128)S(1)}, f32[1,512]{1,0:T(1,128)}, u32[]{:S(2)}) copy-start(f32[1,512]{1,0:T(1,128)} %lse_t.3) | copy-start | bytes 6148
  13.3 17.4 %copy-start.16 = (f32[1,512]{1,0:T(1,128)S(1)}, f32[1,512]{1,0:T(1,128)}, u32[]{:S(2)}) copy-start(f32[1,512]{1,0:T(1,128)} %lse_i.5) | copy-start | bytes 6148
  28.0 19.5 %copy-start.12 = (bf16[1,512,1024]{2,1,0:T(8,128)(2,1)S(1)}, bf16[1,512,1024]{2,1,0:T(8,128)(2,1)}, u32[]{:S(2)}) copy-start(bf16[1,512,1024]{2,1,0:T(8,128)(2,1)} %param.6) | copy-start | bytes 3145732
  28.0 19.5 %collective-permute-start.3 = (bf16[256,768]{1,0:T(8,128)(2,1)S(1)}, bf16[256,768]{1,0:T(8,128)(2,1)S(1)}, u32[]{:S(2)}, u32[]{:S(2)}) collective-permute-start(bf16[256,768]{1,0:T(8,128)(2,1)S(1)} %collective-permute-done.1.t1a), channel_id=1, source_target_pairs={{0,32},{32,64},{64,96},{96,0},{1,33},{33,65},{65,97},{97,1},{2,34}... | collective-permute-start | bytes 1179656 | tf_op jit(solution)/shard_map/ppermute | solution.py:34
  28.0 19.5 %collective-permute-start.4 = (bf16[272,768]{1,0:T(8,128)(2,1)S(1)}, bf16[272,768]{1,0:T(8,128)(2,1)S(1)}, u32[]{:S(2)}, u32[]{:S(2)}) collective-permute-start(bf16[272,768]{1,0:T(8,128)(2,1)S(1)} %collective-permute-done.2.t2b), channel_id=1, source_target_pairs={{0,96},{32,0},{64,32},{96,64},{1,97},{33,1},{65,33},{97,65},{2,98}... | collective-permute-start | bytes 1253384 | tf_op jit(solution)/shard_map/ppermute | solution.py:34
  57.8 8.5 %copy-start.17 = (bf16[512,768]{1,0:T(8,128)(2,1)}, bf16[512,768]{1,0:T(8,128)(2,1)S(1)}, u32[]{:S(2)}) copy-start(bf16[512,768]{1,0:T(8,128)(2,1)S(1)} %get-tuple-element.64) | copy-start | bytes 2359300
  57.8 5.8 %collective-permute-start.7 = (bf16[896,768]{1,0:T(8,128)(2,1)}, bf16[896,768]{1,0:T(8,128)(2,1)S(1)}, u32[]{:S(2)}, u32[]{:S(2)}) collective-permute-start(bf16[896,768]{1,0:T(8,128)(2,1)} %get-tuple-element.61), channel_id=1, source_target_pairs={{0,1},{1,0},{2,3},{3,2},{4,5},{5,4},{6,7},{7,6},{8,9},{9,8},{10,11... | collective-permute-start | bytes 4128776 | tf_op jit(solution)/shard_map/ppermute | solution.py:34
  66.3 27.5 %all-to-all-start = ((bf16[16,56,768]{2,1,0:T(8,128)(2,1)}), bf16[16,56,768]{2,1,0:T(8,128)(2,1)}, u32[]{:S(2)}, u32[]{:S(2)}) async-start(bf16[16,56,768]{2,1,0:T(8,128)(2,1)} %bitcast.3), calls=%async_computation | async-start | bytes 2752512 | tf_op jit(solution)/shard_map/all_to_all | solution.py:456
  73.7 34.9 %collective-permute-start.10 = (bf16[768,768]{1,0:T(8,128)(2,1)}, bf16[768,768]{1,0:T(8,128)(2,1)S(1)}, u32[]{:S(2)}, u32[]{:S(2)}) collective-permute-start(bf16[768,768]{1,0:T(8,128)(2,1)} %get-tuple-element.62), channel_id=1, source_target_pairs={{0,32},{32,64},{64,96},{96,0},{1,33},{33,65},{65,97},{97,1},{2,34}... | collective-permute-start | bytes 3538952 | tf_op jit(solution)/shard_map/ppermute | solution.py:34
  73.8 34.8 %collective-permute-start.11 = (bf16[768,768]{1,0:T(8,128)(2,1)}, bf16[768,768]{1,0:T(8,128)(2,1)S(1)}, u32[]{:S(2)}, u32[]{:S(2)}) collective-permute-start(bf16[768,768]{1,0:T(8,128)(2,1)} %get-tuple-element.63), channel_id=1, source_target_pairs={{0,96},{32,0},{64,32},{96,64},{1,97},{33,1},{65,33},{97,65},{2,98}... | collective-permute-start | bytes 3538952 | tf_op jit(solution)/shard_map/ppermute | solution.py:34
  76.4 32.1 %collective-permute-start.12 = (bf16[512,768]{1,0:T(8,128)(2,1)}, bf16[512,768]{1,0:T(8,128)(2,1)S(1)}, u32[]{:S(2)}, u32[]{:S(2)}) collective-permute-start(bf16[512,768]{1,0:T(8,128)(2,1)} %copy-done.17), channel_id=1, source_target_pairs={{0,16},{16,0},{1,17},{17,1},{2,18},{18,2},{3,19},{19,3},{4,20},{20... | collective-permute-start | bytes 2359304 | tf_op jit(solution)/shard_map/ppermute | solution.py:34
  95.4 7.4 %collective-permute-start.8 = (bf16[56,768]{1,0:T(8,128)(2,1)S(1)}, bf16[56,768]{1,0:T(8,128)(2,1)S(1)}, u32[]{:S(2)}, u32[]{:S(2)}) collective-permute-start(bf16[56,768]{1,0:T(8,128)(2,1)S(1)} %reduce_sum.12), channel_id=1, source_target_pairs={{0,32},{32,0},{64,96},{96,64},{1,33},{33,1},{65,97},{97,65},{2,34}... | collective-permute-start | bytes 258056 | tf_op jit(solution)/shard_map/ppermute | solution.py:461
  102.8 4.6 %collective-permute-start.9 = (bf16[56,768]{1,0:T(8,128)(2,1)S(1)}, bf16[56,768]{1,0:T(8,128)(2,1)S(1)}, u32[]{:S(2)}, u32[]{:S(2)}) collective-permute-start(bf16[56,768]{1,0:T(8,128)(2,1)S(1)} %add_convert_fusion.own), channel_id=1, source_target_pairs={{0,96},{96,0},{32,64},{64,32},{1,97},{97,1},{33,65},{65,33},{2,98}... | collective-permute-start | bytes 258056 | tf_op jit(solution)/shard_map/ppermute | solution.py:463
  109.6 24.3 %all-to-all-start.1 = ((bf16[16,56,768]{2,1,0:T(8,128)(2,1)}), bf16[16,56,768]{2,1,0:T(8,128)(2,1)S(1)}, u32[]{:S(2)}, u32[]{:S(2)}) async-start(bf16[16,56,768]{2,1,0:T(8,128)(2,1)} %total.1), calls=%async_computation.1 | async-start | bytes 2752512 | tf_op jit(solution)/shard_map/all_to_all | solution.py:465
  117.9 8.3 %collective-permute-start.14 = (bf16[256,768]{1,0:T(8,128)(2,1)S(1)}, bf16[256,768]{1,0:T(8,128)(2,1)S(1)}, u32[]{:S(2)}, u32[]{:S(2)}) collective-permute-start(bf16[256,768]{1,0:T(8,128)(2,1)S(1)} %slice.7), channel_id=1, source_target_pairs={{0,96},{32,0},{64,32},{96,64},{1,97},{33,1},{65,33},{97,65},{2,98}... | collective-permute-start | bytes 1179656 | tf_op jit(solution)/shard_map/ppermute | solution.py:34
  118.5 9.2 %collective-permute-start.13 = (bf16[256,768]{1,0:T(8,128)(2,1)S(1)}, bf16[256,768]{1,0:T(8,128)(2,1)S(1)}, u32[]{:S(2)}, u32[]{:S(2)}) collective-permute-start(bf16[256,768]{1,0:T(8,128)(2,1)S(1)} %slice.6), channel_id=1, source_target_pairs={{0,32},{32,64},{64,96},{96,0},{1,33},{33,65},{65,97},{97,1},{2,34}... | collective-permute-start | bytes 1179656 | tf_op jit(solution)/shard_map/ppermute | solution.py:34
  133.9 6.6 %collective-permute-start.15 = (bf16[896,768]{1,0:T(8,128)(2,1)S(1)}, bf16[896,768]{1,0:T(8,128)(2,1)S(1)}, u32[]{:S(2)}, u32[]{:S(2)}) collective-permute-start(bf16[896,768]{1,0:T(8,128)(2,1)S(1)} %bitcast.7), channel_id=1, source_target_pairs={{0,1},{1,0},{2,3},{3,2},{4,5},{5,4},{6,7},{7,6},{8,9},{9,8},{10,11... | collective-permute-start | bytes 4128776 | tf_op jit(solution)/shard_map/ppermute | solution.py:34
  (13 other events, 34.0 us)
